TPU v7x, 256 devices: a whole 4x4x8 slice. The times are simulated.
256 devices in a mesh: grp: 4 (over y_hi, core), blk: 64 (over x, y_lo, z).
Axes of the slice: x: 4, y: 4 (y_hi: 2, y_lo: 2; y = y_hi * 2 + y_lo), z: 8, core: 2. Of those that a mesh axis runs over, the one named last changes fastest.
Arguments:
- main_hidden: bfloat16 [8192, 3072], P('blk', 'grp'), may hold values from -6 to 6
- ctrl_query: bfloat16 [8192, 1536], P('blk', 'grp'), may hold values from -150 to 150
- ctrl_key: bfloat16 [8192, 1536], P('blk', 'grp'), may hold values from -6 to 6
- ctrl_value: bfloat16 [8192, 1536], P('blk', 'grp'), may hold values from -6 to 6
- w_out: bfloat16 [1536, 3072], P('grp'), may hold values from -1 to 1
- d_mixed: bfloat16 [8192, 3072], P('blk', 'grp'), may hold values from -3 to 3
- control_slot: int32 [8192], P('blk'), may hold values from 0 to 8191, as said below
Outputs:
- main_mixed: bfloat16 [8192, 3072], P('blk', 'grp')
- d_query: bfloat16 [8192, 1536], P('blk', 'grp')
- d_key: bfloat16 [8192, 1536], P('blk', 'grp')
- d_value: bfloat16 [8192, 1536], P('blk', 'grp')
- d_w_out: float32 [1536, 3072], P('grp', 'blk')
Inputs may be any that keep to these rules, and one draw needn't show every extreme that they name: `control_slot`: A permutation of the token positions. Every aligned block of 128 entries sends exactly 2 of its tokens into each aligned block of 128 control positions.
All inputs are finite; a program needn't handle non-finite values.
Results may differ from a plain program's by a relative error of at most 0.038.
Values may be sent and summed in bfloat16 or wider, within the bound.
No kernel may reach another device: no remote copies, remote signals or barrier semaphores. Data moves between devices by JAX's collectives and lax.ppermute only.
A program may use at most 128 MiB of HBM per device.

v0:
```python
import math

import jax
import jax.numpy as jnp
from jax import lax
from jax.sharding import PartitionSpec as P

HD = 128
HEAD_GRP = 3


def on_device(main_hidden, ctrl_query, ctrl_key, ctrl_value, w_out, d_mixed, control_slot):
    rows_dev = ctrl_query.shape[0]
    feature_cols = d_mixed.shape[1]
    blocks = lax.axis_size("blk")
    per_peer = rows_dev // blocks
    score_scale = 1.0 / math.sqrt(HD)
    whole_key, whole_value = (
        lax.all_gather(ctrl_key, "blk", axis=0, tiled=True),
        lax.all_gather(ctrl_value, "blk", axis=0, tiled=True),
    )
    outputs = []
    norm_list = []
    for head_idx in range(HEAD_GRP):
        columns = slice(head_idx * HD, (head_idx + 1) * HD)
        scores = (
            jnp.dot(
                ctrl_query[:, columns], whole_key[:, columns].T, preferred_element_type=jnp.float32
            )
            * score_scale
        )
        row_peak = jnp.max(scores, axis=1, keepdims=True)
        log_norm = row_peak + jnp.log(jnp.sum(jnp.exp(scores - row_peak), axis=1, keepdims=True))
        soft_weights = jnp.exp(scores - log_norm).astype(jnp.bfloat16)
        outputs.append(
            jnp.dot(soft_weights, whole_value[:, columns], preferred_element_type=jnp.float32)
        )
        norm_list.append(log_norm[:, 0])
    attended = jnp.concatenate(outputs, axis=1).astype(jnp.bfloat16)
    log_norms = jnp.stack(norm_list, axis=1)
    target = control_slot // rows_dev
    within = control_slot % rows_dev
    sort_order = jnp.argsort(target)
    inverse = jnp.argsort(sort_order)
    send_within = within[sort_order].reshape(blocks, per_peer)
    arrived, arrived_grad = (
        lax.all_to_all(send_within, "blk", split_axis=0, concat_axis=0, tiled=True),
        lax.all_to_all(
            d_mixed[sort_order].reshape(blocks, per_peer, feature_cols),
            "blk",
            split_axis=0,
            concat_axis=0,
            tiled=True,
        ),
    )
    placed = arrived.reshape(rows_dev)
    grad_rows = jnp.zeros_like(d_mixed).at[placed].set(arrived_grad.reshape(rows_dev, feature_cols))
    residual = lax.psum_scatter(
        jnp.dot(attended, w_out, preferred_element_type=jnp.float32).astype(jnp.bfloat16),
        "grp",
        scatter_dimension=1,
        tiled=True,
    ).astype(jnp.float32)
    returned = lax.all_to_all(
        residual[placed].reshape(blocks, per_peer, feature_cols),
        "blk",
        split_axis=0,
        concat_axis=0,
        tiled=True,
    )
    residual = returned.reshape(rows_dev, feature_cols)[inverse]
    main_mixed = (main_hidden.astype(jnp.float32) + residual).astype(jnp.bfloat16)
    grad_full = lax.all_gather(grad_rows, "grp", axis=1, tiled=True)
    d_proj = jnp.dot(grad_full, w_out.T, preferred_element_type=jnp.float32).astype(jnp.bfloat16)
    d_w_out = lax.psum_scatter(
        jnp.dot(attended.T, grad_full, preferred_element_type=jnp.float32),
        "blk",
        scatter_dimension=1,
        tiled=True,
    )
    row_delta = jnp.sum(
        (d_proj.astype(jnp.float32) * attended.astype(jnp.float32)).reshape(rows_dev, HEAD_GRP, HD),
        axis=2,
    )
    all_norms, all_delta = (
        lax.all_gather(log_norms, "blk", axis=0, tiled=True),
        lax.all_gather(row_delta, "blk", axis=0, tiled=True),
    )
    query_grads = []
    for head_idx in range(HEAD_GRP):
        columns = slice(head_idx * HD, (head_idx + 1) * HD)
        scores = (
            jnp.dot(
                ctrl_query[:, columns], whole_key[:, columns].T, preferred_element_type=jnp.float32
            )
            * score_scale
        )
        soft_weights = jnp.exp(scores - log_norms[:, head_idx : head_idx + 1])
        d_probs = jnp.dot(
            d_proj[:, columns], whole_value[:, columns].T, preferred_element_type=jnp.float32
        )
        d_scores = (soft_weights * (d_probs - row_delta[:, head_idx : head_idx + 1])).astype(
            jnp.bfloat16
        )
        query_grads.append(
            jnp.dot(d_scores, whole_key[:, columns], preferred_element_type=jnp.float32)
            * score_scale
        )
    d_query = jnp.concatenate(query_grads, axis=1).astype(jnp.bfloat16)
    query_piece = lax.all_gather(ctrl_query, "blk", axis=0, tiled=True)
    grad_piece = lax.all_gather(d_proj, "blk", axis=0, tiled=True)
    key_terms = []
    value_terms = []
    for head_idx in range(HEAD_GRP):
        columns = slice(head_idx * HD, (head_idx + 1) * HD)
        scores = (
            jnp.dot(
                query_piece[:, columns], ctrl_key[:, columns].T, preferred_element_type=jnp.float32
            )
            * score_scale
        )
        soft_weights = jnp.exp(scores - all_norms[:, head_idx : head_idx + 1])
        d_probs = jnp.dot(
            grad_piece[:, columns], ctrl_value[:, columns].T, preferred_element_type=jnp.float32
        )
        d_scores = (soft_weights * (d_probs - all_delta[:, head_idx : head_idx + 1])).astype(
            jnp.bfloat16
        )
        key_terms.append(
            jnp.dot(d_scores.T, query_piece[:, columns], preferred_element_type=jnp.float32)
            * score_scale
        )
        value_terms.append(
            jnp.dot(
                soft_weights.astype(jnp.bfloat16).T,
                grad_piece[:, columns],
                preferred_element_type=jnp.float32,
            )
        )
    key_grad = jnp.concatenate(key_terms, axis=1)
    value_grad = jnp.concatenate(value_terms, axis=1)
    return (
        main_mixed,
        d_query,
        key_grad.astype(jnp.bfloat16),
        value_grad.astype(jnp.bfloat16),
        d_w_out,
    )


def solution(mesh):
    in_specs = (
        P("blk", "grp"),
        P("blk", "grp"),
        P("blk", "grp"),
        P("blk", "grp"),
        P("grp", None),
        P("blk", "grp"),
        P("blk"),
    )
    out_specs = (
        P("blk", "grp"),
        P("blk", "grp"),
        P("blk", "grp"),
        P("blk", "grp"),
        P("grp", "blk"),
    )
    return jax.shard_map(
        on_device, mesh=mesh, in_specs=in_specs, out_specs=out_specs, check_vma=False
    )
```

profile of v0, /device:TPU:32, one launch (start us, length us, event | category | flops | bytes accessed | tf_op | source)
XLA Modules:
  0.0 1554.5 jit_solution(1669932471900836220)
XLA Ops:
  7.2 0.7 all-gather.5.cloned.1.call-update
  8.0 0.7 all-gather.7.cloned.1.call-update
  8.7 0.7 all-gather.9.cloned.1.call-update
  9.5 309.9 %all-gather.5.cloned.1.call-done = bf16[8192,384]{1,0:T(8,128)(2,1)} async-done(((bf16[128,384]{1,0:T(8,128)(2,1)}), bf16[8192,384]{1,0:T(8,128)(2,1)}) %all-gather.5.cloned.1.call-update) | async-done | bytes 6291472 | tf_op jit(solution)/shard_map/all_gather | solution.py:19
  319.3 2.5 fusion.180
  321.9 0.8 exponential_reduce_fusion
  322.7 0.8 fusion.181
  323.5 0.3 copy-done.1
  323.9 0.8 exponential_reduce_fusion.1
  324.6 0.8 fusion.182
  325.4 0.4 copy-done.2
  325.8 2.1 copy-done.4
  327.9 0.8 exponential_reduce_fusion.2
  328.7 297.4 %all-gather.7.cloned.1.call-done = bf16[8192,384]{1,0:T(8,128)(2,1)} async-done(((bf16[128,384]{1,0:T(8,128)(2,1)}), bf16[8192,384]{1,0:T(8,128)(2,1)}) %all-gather.7.cloned.1.call-update) | async-done | bytes 6291472 | tf_op jit(solution)/shard_map/all_gather | solution.py:20
  626.0 4.1 fusion.130
  630.2 2.9 fusion.125
  633.2 2.8 fusion.120
  636.0 1.5 convolution_convert_fusion
  637.6 2.5 sort.31
  640.2 1.2 gather_fusion
  641.4 0.8 all_to_all.12
  642.1 8.1 all-to-all-start
  650.2 0.9 gather_fusion.3
  651.1 0.8 reshape.121
  651.9 7.7 all-to-all-done
  659.6 5.5 all-to-all-start.2
  665.3 0.5 broadcast.86
  665.8 0.7 reduce.3
  666.7 10.3 all-to-all-done.2
  677.1 1.2 scatter_custom_fusion
  678.2 10.5 all_gather.23
  688.7 1.4 convert_multiply_fusion
  690.3 2.5 sort.32
  692.9 161.6 %all_gather.25 = f32[8192,3]{0,1:T(4,128)} all-gather(f32[128,3]{0,1:T(4,128)S(1)} %pad_maximum_fusion.4), channel_id=1, replica_groups=mesh['grp'=4,'blk'=64] {'blk'}, dimensions={0}, use_global_device_ids=true | all-gather | bytes 99840 | tf_op jit(solution)/shard_map/all_gather | solution.py:86
  854.5 150.8 %all_gather.27 = f32[8192,3]{0,1:T(4,128)S(1)} all-gather(f32[128,3]{0,1:T(4,128)S(1)} %reduce_sum.39), channel_id=1, replica_groups=mesh['grp'=4,'blk'=64] {'blk'}, dimensions={0}, use_global_device_ids=true | all-gather | bytes 99840 | tf_op jit(solution)/shard_map/all_gather | solution.py:87
  1005.3 0.5 slice_bitcast_fusion.2
  1005.8 3.0 fusion.177
  1008.9 0.9 copy-done.10
  1009.9 3.9 fusion.2
  1013.8 5.6 fusion.111
  1019.4 5.6 fusion.114
  1025.1 5.6 fusion.117
  1030.7 0.7 fusion.178
  1031.4 1.0 convert_element_type.66
  1032.4 0.8 gather_fusion.1
  1033.2 1.0 reshape.119
  1034.2 5.8 all-to-all-start.1
  1040.1 0.8 copy.22
  1040.8 3.8 fusion.5
  1044.6 3.9 fusion.8
  1048.5 6.3 all-to-all-done.1
  1055.1 0.8 gather_fusion.2
  1056.0 0.7 add_convert_fusion
  1056.7 170.4 %all-gather.11.cloned.1.call-done = bf16[8192,384]{0,1:T(8,128)(2,1)} async-done(((bf16[128,384]{0,1:T(8,128)(2,1)}), bf16[8192,384]{0,1:T(8,128)(2,1)}) %all-gather.11.cloned.1.call-update) | async-done | bytes 6291472 | tf_op jit(solution)/shard_map/all_gather | solution.py:111
  1227.0 5.9 fusion.96
  1233.0 5.9 fusion.101
  1238.9 6.0 fusion.106
  1244.9 0.8 copy.23
  1245.7 3.7 fusion.145
  1249.3 0.4 copy-done.6
  1249.7 2.5 fusion.140
  1252.5 2.4 fusion.135
  1254.9 0.8 copy.24
  1255.7 291.9 %reduce-scatter.5.cloned.1.call-done = f32[384,48]{0,1:T(8,128)} async-done(((f32[384,3072]{0,1:T(8,128)}), f32[384,48]{0,1:T(8,128)}) %reduce-scatter.5.cloned.1.call-update) | async-done | bytes 73744 | tf_op jit(solution)/shard_map/reduce_scatter | solution.py:75
  (83 shorter events, 1.7 us)
Async XLA Ops:
  7.2 628.9 %copy-start = (bf16[384,3072]{1,0:T(8,128)(2,1)S(1)}, bf16[384,3072]{1,0:T(8,128)(2,1)}, u32[]{:S(2)}) copy-start(bf16[384,3072]{1,0:T(8,128)(2,1)} %param.11) | copy-start | bytes 7077892
  7.2 312.1 %all-gather.5.cloned.1.call-start = ((), (), s32[]{:S(2)}) async-start(), calls=%async_computation.5 | async-start | bytes 6389760 | tf_op jit(solution)/shard_map/all_gather | solution.py:19
  7.9 618.1 %all-gather.7.cloned.1.call-start = ((), (), s32[]{:S(2)}) async-start(), calls=%async_computation.6 | async-start | bytes 6389760 | tf_op jit(solution)/shard_map/all_gather | solution.py:20
  8.7 1001.2 %all-gather.9.cloned.1.call-start = ((), (), s32[]{:S(2)}) async-start(), calls=%async_computation.8 | async-start | bytes 6389760 | tf_op jit(solution)/shard_map/all_gather | solution.py:110
  9.4 313.2 %copy-start.11 = (bf16[128,384]{1,0:T(8,128)(2,1)S(1)}, bf16[128,384]{1,0:T(8,128)(2,1)}, u32[]{:S(2)}) copy-start(bf16[128,384]{1,0:T(8,128)(2,1)} %param.8) | copy-start | bytes 294916
  9.4 1022.0 %reduce-scatter.3.cloned.1.call-start = ((), (), s32[]{:S(2)}) async-start(), calls=%async_computation.7 | async-start | bytes 983040 | tf_op jit(solution)/shard_map/reduce_scatter | solution.py:58
  319.3 3.4 copy-start.9
  321.9 2.0 copy-start.1
  323.9 2.0 copy-start.2
  325.8 2.1 copy-start.4
  328.7 364.2 %copy-start.22 = (f32[128]{0:T(128)}, f32[128]{0:T(128)S(1)}, u32[]{:S(2)}) copy-start(f32[128]{0:T(128)S(1)} %log_add_fusion.2) | copy-start | bytes 1540
  626.0 4.1 copy-start.3
  630.2 3.0 copy-start.5
  633.2 4.4 copy-start.27
  633.2 17.1 %copy-start.8 = (bf16[128,768]{1,0:T(8,128)(2,1)S(1)}, bf16[128,768]{1,0:T(8,128)(2,1)}, u32[]{:S(2)}) copy-start(bf16[128,768]{1,0:T(8,128)(2,1)} %param.12) | copy-start | bytes 589828
  642.1 17.4 %all-to-all-start = ((s32[64,1,2]{2,1,0:T(1,128)}), s32[64,1,2]{2,1,0:T(1,128)S(1)}, u32[]{:S(2)}, u32[]{:S(2)}) async-start(s32[64,1,2]{2,1,0:T(1,128)} %bitcast), calls=%async_computation.1 | async-start | bytes 65536 | tf_op jit(solution)/shard_map/all_to_all | solution.py:47
  659.6 17.4 %all-to-all-start.2 = ((bf16[64,2,768]{2,1,0:T(2,128)(2,1)}), bf16[64,2,768]{2,1,0:T(2,128)(2,1)S(1)}, u32[]{:S(2)}, u32[]{:S(2)}) async-start(bf16[64,2,768]{2,1,0:T(2,128)(2,1)} %reshape.121), calls=%async_computation.3 | async-start | bytes 393216 | tf_op jit(solution)/shard_map/all_to_all | solution.py:48
  665.1 562.0 %all-gather.11.cloned.1.call-start = ((), (), s32[]{:S(2)}) async-start(), calls=%async_computation.9 | async-start | bytes 6389760 | tf_op jit(solution)/shard_map/all_gather | solution.py:111
  690.2 857.4 %reduce-scatter.5.cloned.1.call-start = ((), (), s32[]{:S(2)}) async-start(), calls=%async_computation.10 | async-start | bytes 4792320 | tf_op jit(solution)/shard_map/reduce_scatter | solution.py:75
  1005.8 4.0 copy-start.12
  1008.8 0.9 copy-start.10
  1009.9 3.9 copy-start.13
  1009.9 3.9 copy-start.26
  1013.8 5.6 copy-start.25
  1019.4 5.7 copy-start.23
  1019.4 5.7 copy-start.24
  1030.7 9.3 copy-start.19
  1030.7 9.3 copy-start.20
  1030.7 9.3 copy-start.21
  1034.2 20.7 %all-to-all-start.1 = ((f32[64,2,768]{2,1,0:T(2,128)}), f32[64,2,768]{2,1,0:T(2,128)S(1)}, u32[]{:S(2)}, u32[]{:S(2)}) async-start(f32[64,2,768]{2,1,0:T(2,128)} %reshape.119), calls=%async_computation.2 | async-start | bytes 786432 | tf_op jit(solution)/shard_map/all_to_all | solution.py:64
  1048.5 7.5 copy-start.14
  1048.5 178.5 %copy-start.15 = (bf16[128,384]{1,0:T(8,128)(2,1)S(1)}, bf16[128,384]{1,0:T(8,128)(2,1)}, u32[]{:S(2)}) copy-start(bf16[128,384]{1,0:T(8,128)(2,1)} %param.10) | copy-start | bytes 294916
  1048.5 178.5 %copy-start.18 = (f32[8192,1]{0,1:T(1,128)S(1)}, f32[8192,1]{0,1:T(1,128)}, u32[]{:S(2)}) copy-start(f32[8192,1]{0,1:T(1,128)} %get-tuple-element.25) | copy-start | bytes 98308
  1227.0 5.9 copy-start.17
  1233.0 5.9 copy-start.16
  1245.7 4.0 copy-start.6
  1249.7 2.9 copy-start.7
Sparse Core Ops, SparseCore 0:
  9.8 309.4 all-gather.4
  321.1 304.9 all-gather.6
  627.8 306.0 all-gather.8
  936.6 32.8 reduce-scatter.2
  971.7 255.3 all-gather.10
  1230.2 317.4 reduce-scatter.4
where the time goes:
time: 1560 us; the launch traced here: 1550 us
  waiting for transfers between devices  1100 us (71%)
  blocking collectives  323 us (21%)
  matrix products  74.8 us (5%)
  starting transfers between devices  19.8 us (1%)
  local copies, waits for them, and re-layouts  16.5 us (1%)
    all_gather x1, waiting for transfers between devices, on_device(): lax.all_gather(ctrl_key, 'blk', axis=0, tiled=True)  310 us
    all_gather x1, waiting for transfers between devices, on_device(): lax.all_gather(ctrl_value, 'blk', axis=0, tiled=True)  297 us
    reduce_scatter x1, waiting for transfers between devices, on_device(): lax.psum_scatter(jnp.dot(attended.T, grad_full, preferred_element_type=jn...  292 us
    all_gather x1, waiting for transfers between devices, on_device(): grad_piece = lax.all_gather(d_proj, 'blk', axis=0, tiled=True)  170 us
    all_gather x1, blocking collectives, on_device(): lax.all_gather(log_norms, 'blk', axis=0, tiled=True)  162 us
    all_gather x1, blocking collectives, on_device(): lax.all_gather(row_delta, 'blk', axis=0, tiled=True)  151 us
  transfers between devices with their start and end apart: 9, of which 7 were waited for; matrix products, arithmetic and copies ran while one was open for 6% of the time, Pallas kernels for 0%

commit v1 on v0

v1 whole, which is shorter than its diff:
```python
import math

import jax
import jax.numpy as jnp
from jax import lax
from jax.experimental import pallas as pl
from jax.experimental.pallas import tpu as pltpu
from jax.sharding import Mesh
from jax.sharding import PartitionSpec as P

HD = 128
HEADS = 3
COLS = HEADS * HD
TOK = 128
SIDE = 8
TILE = TOK * SIDE
QB = 256
SCALE = 1.0 / math.sqrt(HD)
LOG2E = math.log2(math.e)
PEER = TOK // SIDE
SPAN = 768
QUAD = ("x", "yl")
F32 = jnp.float32
BF16 = jnp.bfloat16
NT = (((1,), (1,)), ((), ()))
TN = (((0,), (0,)), ((), ()))
VMEM = pl.BlockSpec(memory_space=pltpu.VMEM)
SMEM = pl.BlockSpec(memory_space=pltpu.SMEM)
PARAMS = pltpu.CompilerParams(vmem_limit_bytes=48 * 1024 * 1024)
RING = (0, -1, 1, -2, 2, -3, 3, 4)


def dot(left, right, dims=(((1,), (0,)), ((), ()))):
    return lax.dot_general(left, right, dims, preferred_element_type=F32)


def call(body, out, *args, specs=None):
    return pl.pallas_call(
        body,
        out_shape=[jax.ShapeDtypeStruct(shape, dtype) for shape, dtype in out],
        in_specs=specs or [VMEM] * len(args),
        out_specs=[VMEM] * len(out),
        compiler_params=PARAMS,
    )(*args)


def head(idx):
    return slice(idx * HD, (idx + 1) * HD)


def block_of(slot):
    return (slot >> 7) & (SIDE - 1)


def project_body(d_ref, w_ref, row_ref, col_ref, pay_ref, cut_ref):
    total = jnp.zeros((TOK, COLS), F32)
    for part in range(4):
        total += dot(d_ref[part], w_ref[:, part * SPAN : (part + 1) * SPAN], NT)
        for half in range(2):
            cut_ref[2 * part + half] = d_ref[part][:, half * COLS : (half + 1) * COLS]
    slot_row, slot_col = row_ref[...], col_ref[...]
    first = lax.broadcasted_iota(jnp.int32, (TOK, TOK), 0)
    second = lax.broadcasted_iota(jnp.int32, (TOK, TOK), 1)
    same = (block_of(slot_row) == block_of(slot_col)) & (first < second)
    ahead = jnp.sum(jnp.where(same, 1.0, 0.0), axis=0, keepdims=True).astype(jnp.int32)
    rank = block_of(slot_row) * PEER + ahead
    order = jnp.where(first == rank, 1.0, 0.0).astype(BF16)
    place = jnp.where(
        second == 0,
        (slot_col >> 10).astype(F32),
        jnp.where(second == 1, (slot_col & (TOK - 1)).astype(F32), 0.0),
    )
    pay_ref[:, :COLS] = dot(order, total.astype(BF16)).astype(BF16)
    pay_ref[:, COLS:] = dot(order, place.astype(BF16)).astype(BF16)


def forward_body(q_ref, kv_ref, out_ref, lse_ref):
    lse_ref[...] = jnp.zeros_like(lse_ref)
    for idx in range(HEADS):
        keys = kv_ref[:, head(idx)]
        values_t = kv_ref[:, head(HEADS + idx)].T
        for start in range(0, TILE, QB):
            cols = slice(start, start + QB)
            scores = dot(keys, q_ref[cols, head(idx)], NT)
            peak = jnp.max(scores, axis=0, keepdims=True)
            weights = jnp.exp2((scores - peak) * (SCALE * LOG2E))
            total = jnp.sum(weights, axis=0, keepdims=True)
            out_ref[head(idx), cols] = dot(values_t, weights.astype(BF16)) / total
            lse_ref[idx : idx + 1, cols] = peak * SCALE + jnp.log(total)


def places(arrived_ref):
    place = arrived_ref[:, COLS : COLS + HD].astype(F32)
    target = place[:, 0:1] * float(TOK) + place[:, 1:2]
    lanes = lax.broadcasted_iota(jnp.int32, (TILE, TILE), 1)
    return jnp.where(lanes == target.astype(jnp.int32), 1.0, 0.0).astype(BF16)


def delta_body(arrived_ref, out_ref, lse_ref, grad_ref, stat_ref):
    order = places(arrived_ref)
    stat_ref[...] = lse_ref[...]
    for idx in range(HEADS):
        grad_t = dot(arrived_ref[:, head(idx)].T, order)
        grad_ref[:, head(idx)] = grad_t.T.astype(BF16)
        stat_ref[HEADS + idx : HEADS + idx + 1, :] = jnp.sum(
            grad_t * out_ref[head(idx), :], axis=0, keepdims=True
        )


def merge_body(all_ref, stat_ref, out_ref, arrived_ref, norm_ref, part_ref):
    order = places(arrived_ref)
    norm_ref[...] = jnp.zeros_like(norm_ref)
    for idx in range(HEADS):
        lses = [all_ref[SIDE * s + idx : SIDE * s + idx + 1, :] for s in range(SIDE)]
        peak = lses[0]
        for one in lses[1:]:
            peak = jnp.maximum(peak, one)
        total = jnp.zeros_like(peak)
        delta = jnp.zeros_like(peak)
        for s, one in enumerate(lses):
            weight = jnp.exp(one - peak)
            total += weight
            row = SIDE * s + HEADS + idx
            delta += weight * all_ref[row : row + 1, :]
        norm = peak + jnp.log(total)
        norm_ref[idx : idx + 1, :] = norm
        norm_ref[HEADS + idx : HEADS + idx + 1, :] = delta / total
        share = jnp.exp(stat_ref[idx : idx + 1, :] - norm)
        scaled = (out_ref[head(idx), :] * share).astype(BF16)
        part_ref[:, head(idx)] = dot(scaled, order, NT).T.astype(BF16)


def backward_body(z_ref, q_ref, kv_ref, grad_ref, norm_ref, dq_ref, dkv_ref):
    z_pos = z_ref[0]
    for idx in range(HEADS):
        keys = kv_ref[:, head(idx)]
        keys_t = keys.T
        values = kv_ref[:, head(HEADS + idx)]
        d_keys = jnp.zeros((TILE, HD), F32)
        d_values = jnp.zeros((TILE, HD), F32)
        for start in range(0, TILE, QB):
            cols = slice(start, start + QB)
            query = q_ref[cols, head(idx)]
            grad = grad_ref[cols, head(idx)]
            scores = dot(keys, query, NT) * SCALE
            weights = jnp.exp2((scores - norm_ref[idx : idx + 1, cols]) * LOG2E)
            d_probs = dot(values, grad, NT)
            d_scores = (weights * (d_probs - norm_ref[HEADS + idx : HEADS + idx + 1, cols])).astype(BF16)
            d_values += dot(weights.astype(BF16), grad)
            d_keys += dot(d_scores, query)
            dq_ref[cols, head(idx)] = (dot(keys_t, d_scores) * SCALE).T.astype(BF16)
        d_keys = (d_keys * SCALE).astype(BF16)
        d_values = d_values.astype(BF16)
        for spot, offset in enumerate(RING):
            rows = slice(spot * TOK, (spot + 1) * TOK)
            owner = lax.rem(z_pos + (offset + SIDE), SIDE)
            here = pl.ds(pl.multiple_of(owner * TOK, TOK), TOK)
            dkv_ref[here, head(idx)] = d_keys[rows]
            dkv_ref[here, head(HEADS + idx)] = d_values[rows]


def output_body(sorted_ref, w_ref, row_ref, col_ref, att_ref, part_ref):
    slot_row, slot_col = row_ref[...], col_ref[...]
    first = lax.broadcasted_iota(jnp.int32, (TOK, TOK), 0)
    second = lax.broadcasted_iota(jnp.int32, (TOK, TOK), 1)
    same = (block_of(slot_row) == block_of(slot_col)) & (second < first)
    ahead = jnp.sum(jnp.where(same, 1.0, 0.0), axis=1, keepdims=True).astype(jnp.int32)
    rank = block_of(slot_col) * PEER + ahead
    order = jnp.where(second == rank, 1.0, 0.0).astype(BF16)
    attended = dot(order, sorted_ref[...]).astype(BF16)
    att_ref[...] = attended
    for part in range(4):
        part_ref[part] = dot(attended, w_ref[:, part * SPAN : (part + 1) * SPAN]).astype(BF16)


def shift(value, axis, step, size):
    return lax.ppermute(value, axis, [(i, (i + step) % size) for i in range(size)])


def exchange(value, axis):
    return lax.all_to_all(value, axis, split_axis=0, concat_axis=0, tiled=True)


def gather_quad(value):
    return exchange(jnp.tile(value, (SIDE, 1)), QUAD)


def ring_gather(value):
    ahead = back = value
    blocks = [value]
    for _ in range(3):
        ahead, back = shift(ahead, "z", 1, SIDE), shift(back, "z", SIDE - 1, SIDE)
        blocks += [ahead, back]
    half = TOK // 2
    blocks += [shift(ahead[:half], "z", 1, SIDE), shift(back[half:], "z", SIDE - 1, SIDE)]
    return jnp.concatenate(blocks, axis=0)


def pick(value, idx, axis):
    return lax.dynamic_index_in_dim(value, idx, axis, keepdims=False)


def on_device(main_hidden, ctrl_query, ctrl_key, ctrl_value, w_out, d_mixed, control_slot):
    y_pos, core, z_pos = lax.axis_index("yh"), lax.axis_index("co"), lax.axis_index("z")
    slot_row, slot_col = control_slot.reshape(1, TOK), control_slot.reshape(TOK, 1)

    other = shift(d_mixed, "yh", 1, 2)
    pair = jnp.where(y_pos == 0, jnp.stack([d_mixed, other]), jnp.stack([other, d_mixed]))
    other = shift(pair, "co", 1, 2)
    d_full = jnp.where(core == 0, jnp.stack([pair, other], 1), jnp.stack([other, pair], 1))
    d_full = d_full.reshape(4, TOK, SPAN)

    key_value = ring_gather(jnp.concatenate([ctrl_key, ctrl_value], axis=1))
    query = gather_quad(ctrl_query)

    payload, d_cut = call(
        project_body,
        [((TOK, COLS + HD), BF16), ((SIDE, TOK, COLS), BF16)],
        d_full,
        w_out,
        slot_row,
        slot_col,
    )
    arrived = gather_quad(exchange(payload, "z"))

    out_t, lse = call(forward_body, [((COLS, TILE), F32), ((SIDE, TILE), F32)], query, key_value)
    grad, stats = call(
        delta_body, [((TILE, COLS), BF16), ((SIDE, TILE), F32)], arrived, out_t, lse
    )
    all_stats = gather_quad(stats)
    norms, part = call(
        merge_body, [((SIDE, TILE), F32), ((TILE, COLS), BF16)], all_stats, stats, out_t, arrived
    )
    d_query, d_key_value = call(
        backward_body,
        [((TILE, COLS), BF16), ((TILE, 2 * COLS), BF16)],
        z_pos.reshape(1).astype(jnp.int32),
        query,
        key_value,
        grad,
        norms,
        specs=[SMEM, VMEM, VMEM, VMEM, VMEM],
    )
    d_key_value = lax.psum_scatter(d_key_value, "z", scatter_dimension=0, tiled=True)

    attended = jnp.sum(exchange(part, QUAD).reshape(SIDE, TOK, COLS).astype(F32), axis=0)
    attended = exchange(attended.astype(BF16), "z")
    attended, partial_out = call(
        output_body,
        [((TOK, COLS), BF16), ((4, TOK, SPAN), BF16)],
        attended,
        w_out,
        slot_row,
        slot_col,
    )

    by_core = partial_out.reshape(2, 2, TOK, SPAN)
    summed = pick(by_core, core, 1).astype(F32) + shift(
        pick(by_core, 1 - core, 1), "co", 1, 2
    ).astype(F32)
    residual = pick(summed, y_pos, 0) + shift(
        pick(summed, 1 - y_pos, 0).astype(BF16), "yh", 1, 2
    ).astype(F32)
    main_mixed = (main_hidden.astype(F32) + residual).astype(BF16)

    d_query = jnp.sum(exchange(d_query, QUAD).reshape(SIDE, TOK, COLS).astype(F32), axis=0)

    d_cut = exchange(d_cut, QUAD).reshape(TILE, COLS)
    d_w_out = dot(d_cut, gather_quad(attended), TN).astype(BF16)
    d_w_out = exchange(d_w_out, "z").reshape(SIDE, COLS // SIDE, COLS)
    d_w_out = jnp.sum(d_w_out.astype(F32), axis=0).T
    return (
        main_mixed,
        d_query.astype(BF16),
        d_key_value[:, :COLS],
        d_key_value[:, COLS:],
        d_w_out,
    )


def solution(mesh):
    fine = Mesh(mesh.devices.reshape(2, 2, 4, 2, 8), ("yh", "co", "x", "yl", "z"))
    grp, blk = ("yh", "co"), ("x", "yl", "z")
    in_specs = (
        P(blk, grp),
        P(blk, grp),
        P(blk, grp),
        P(blk, grp),
        P(grp, None),
        P(blk, grp),
        P(blk),
    )
    out_specs = (
        P(blk, grp),
        P(blk, grp),
        P(blk, grp),
        P(blk, grp),
        P(grp, blk),
    )
    return jax.shard_map(
        on_device, mesh=fine, in_specs=in_specs, out_specs=out_specs, check_vma=False
    )
```

time: 1560 us -> 205 us (0.13)
  waiting for transfers between devices: 1100 us -> 42 us
  blocking collectives: 323 us -> 27.9 us
  matrix products: 74.8 us -> 2.5 us
  starting transfers between devices: 19.8 us -> 57.1 us
  Pallas kernels: 0 us -> 23.7 us
    all_gather x4 -> x0, waiting for transfers between devices: 778 us -> none  [the longest x1 310 us: on_device(): lax.all_gather(ctrl_key, 'blk', axis=0, tiled=True)]
    all_gather x3 -> x0, blocking collectives: 323 us -> none  [the longest x1 162 us: on_device(): lax.all_gather(log_norms, 'blk', axis=0, tiled=True)]
    reduce_scatter x2 -> x1, waiting for transfers between devices: 292 us -> 0.01 us  [on_device(): lax.psum_scatter(d_key_value, 'z', scatter_dimension=0, tiled=True)]
    dot_general x21 -> x1, matrix products: 74.8 us -> 2.5 us  [dot(): return lax.dot_general(left, right, dims, preferred_element_type=F32)]
    all_to_all x0 -> x2, blocking collectives: none -> 27.9 us  [exchange(): return lax.all_to_all(value, axis, split_axis=0, concat_axis=0, tiled=True)]
    pallas_call x0 -> x6, Pallas kernels: none -> 23.7 us  [call(): pl.pallas_call(body, out_shape=[jax.ShapeDtypeStruct(shape, dtype) for sh...]
    all_to_all x3 -> x8, starting transfers between devices: 19.4 us -> 40.8 us  [exchange(): return lax.all_to_all(value, axis, split_axis=0, concat_axis=0, tiled=True)]
    ppermute x0 -> x12, starting transfers between devices: none -> 16.1 us  [shift(): lax.ppermute(value, axis, [(i, (i + step) % size) for i in range(size)])]
  transfers between devices with their start and end apart: 9 -> 21, of which waited for: 7 -> 11; matrix products, arithmetic and copies ran while one was open for 6% -> 13% of each run, Pallas kernels for 0% -> 10%
where the time goes in v1:
time: 205 us; the launch traced here: 203 us
  starting transfers between devices  57.1 us (28%)
  waiting for transfers between devices  42 us (20%)
  blocking collectives  27.9 us (14%)
  local copies, waits for them, and re-layouts  26.5 us (13%)
  Pallas kernels  23.7 us (12%)
  between operations  14.3 us (7%)
  other arithmetic  8.79 us (4%)
  matrix products  2.5 us (1%)
    all_to_all x8, starting transfers between devices, exchange(): return lax.all_to_all(value, axis, split_axis=0, concat_axis=0, tiled=True)  40.8 us
    all_to_all x8, waiting for transfers between devices, exchange(): return lax.all_to_all(value, axis, split_axis=0, concat_axis=0, tiled=True)  30.5 us
    all_to_all x2, blocking collectives, exchange(): return lax.all_to_all(value, axis, split_axis=0, concat_axis=0, tiled=True)  27.9 us
    pallas_call x6, Pallas kernels, call(): pl.pallas_call(body, out_shape=[jax.ShapeDtypeStruct(shape, dtype) for sh...  23.7 us
    unnamed x44, local copies, waits for them, and re-layouts  19.5 us
    ppermute x12, starting transfers between devices, shift(): lax.ppermute(value, axis, [(i, (i + step) % size) for i in range(size)])  16.1 us
    ppermute x12, waiting for transfers between devices, shift(): lax.ppermute(value, axis, [(i, (i + step) % size) for i in range(size)])  11.5 us
  transfers between devices with their start and end apart: 21, of which 11 were waited for; matrix products, arithmetic and copies ran while one was open for 13% of the time, Pallas kernels for 10%

profile of v1, /device:TPU:32, one launch (start us, length us, event | category | flops | bytes accessed | tf_op | source)
XLA Modules:
  0.0 202.9 jit_solution(6986715990010871499)
XLA Ops:
  7.2 3.3 %collective-permute-start = (bf16[128,768]{1,0:T(8,128)(2,1)}, bf16[128,768]{1,0:T(8,128)(2,1)S(1)}, u32[]{:S(2)}, u32[]{:S(2)}) collective-permute-start(bf16[128,768]{1,0:T(8,128)(2,1)} %param.12), channel_id=1, source_target_pairs={{0,128},{128,0},{1,129},{129,1},{2,130},{130,2},{3,131},{131,3},{4... | collective-permute-start | bytes 589832 | tf_op jit(solution)/shard_map/ppermute | solution.py:177
  10.5 1.9 tile.12
  12.3 4.4 %all-to-all-start.2 = ((bf16[8,128,384]{2,1,0:T(8,128)(2,1)}), bf16[8,128,384]{2,1,0:T(8,128)(2,1)S(1)}, u32[]{:S(2)}, u32[]{:S(2)}) async-start(bf16[8,128,384]{2,1,0:T(8,128)(2,1)} %tile.12), calls=%async_computation.2 | async-start | bytes 1572864 | tf_op jit(solution)/shard_map/all_to_all | solution.py:181
  16.8 0.7 copy-done.14
  17.4 2.0 maximum_select_fusion.2
  19.5 0.7 constant_dynamic-update-slice_fusion.1
  20.3 1.1 maximum_select_fusion.1
  21.5 1.2 maximum_select_fusion
  22.7 2.0 shard_map.110
  24.7 4.2 %all-to-all-done.2 = bf16[8,128,384]{2,1,0:T(8,128)(2,1)S(1)} async-done(((bf16[8,128,384]{2,1,0:T(8,128)(2,1)}), bf16[8,128,384]{2,1,0:T(8,128)(2,1)S(1)}, u32[]{:S(2)}, u32[]{:S(2)}) %all-to-all-start.2) | async-done | bytes 786464 | tf_op jit(solution)/shard_map/all_to_all | solution.py:181
  28.9 8.6 %all-to-all-start = ((bf16[8,16,512]{2,1,0:T(8,128)(2,1)}), bf16[8,16,512]{2,1,0:T(8,128)(2,1)S(1)}, u32[]{:S(2)}, u32[]{:S(2)}) async-start(bf16[8,16,512]{2,1,0:T(8,128)(2,1)} %bitcast.8), calls=%async_computation | async-start | bytes 262144 | tf_op jit(solution)/shard_map/all_to_all | solution.py:181
  37.4 0.7 constant_dynamic-update-slice_fusion
  38.1 1.5 collective-permute-start.2
  40.2 5.1 %collective-permute-done.2 = bf16[128,768]{1,0:T(8,128)(2,1)} collective-permute-done((bf16[128,768]{1,0:T(8,128)(2,1)}, bf16[128,768]{1,0:T(8,128)(2,1)}, u32[]{:S(2)}, u32[]{:S(2)}) %collective-permute-start.2) | collective-permute-done | bytes 196640 | tf_op jit(solution)/shard_map/ppermute | solution.py:177
  45.3 1.1 collective-permute-start.4
  46.4 0.9 collective-permute-start.5
  47.3 1.1 tile.11
  48.4 3.8 %all-to-all-start.1 = ((bf16[8,128,512]{2,1,0:T(8,128)(2,1)}), bf16[8,128,512]{2,1,0:T(8,128)(2,1)S(1)}, u32[]{:S(2)}, u32[]{:S(2)}) async-start(bf16[8,128,512]{2,1,0:T(8,128)(2,1)} %tile.11), calls=%async_computation.1 | async-start | bytes 2097152 | tf_op jit(solution)/shard_map/all_to_all | solution.py:181
  52.2 1.7 constant_dynamic-update-slice_fusion.9
  53.9 1.6 constant_dynamic-update-slice_fusion.8
  55.6 0.9 collective-permute-start.6
  56.4 2.5 %collective-permute-start.7 = (bf16[128,768]{1,0:T(8,128)(2,1)}, bf16[128,768]{1,0:T(8,128)(2,1)S(1)}, u32[]{:S(2)}, u32[]{:S(2)}) collective-permute-start(bf16[128,768]{1,0:T(8,128)(2,1)} %collective-permute-done.5), channel_id=1, source_target_pairs={{0,7},{1,0},{2,1},{3,2},{4,3},{5,4},{6,5},{7,6},{8,15},{9,8},{10,9... | collective-permute-start | bytes 589832 | tf_op jit(solution)/shard_map/ppermute | solution.py:177
  58.9 1.6 constant_dynamic-update-slice_fusion.7
  60.5 1.6 constant_dynamic-update-slice_fusion.6
  62.9 3.4 %collective-permute-start.9 = (bf16[64,768]{1,0:T(8,128)(2,1)S(1)}, bf16[64,768]{1,0:T(8,128)(2,1)S(1)}, u32[]{:S(2)}, u32[]{:S(2)}) collective-permute-start(bf16[64,768]{1,0:T(8,128)(2,1)S(1)} %slice.17), channel_id=1, source_target_pairs={{0,7},{1,0},{2,1},{3,2},{4,3},{5,4},{6,5},{7,6},{8,15},{9,8},{10,9... | collective-permute-start | bytes 294920 | tf_op jit(solution)/shard_map/ppermute | solution.py:177
  66.3 0.7 constant_dynamic-update-slice_fusion.5
  66.9 0.7 constant_dynamic-update-slice_fusion.4
  67.6 0.9 collective-permute-done.8
  68.6 0.7 constant_dynamic-update-slice_fusion.3
  69.2 0.7 constant_dynamic-update-slice_fusion.2.kv_ref
  69.9 1.4 copy-done.4
  71.3 8.3 %shard_map.111 = (f32[384,1024]{1,0:T(8,128)S(1)}, f32[8,1024]{1,0:T(8,128)S(1)}) custom-call(bf16[1024,384]{1,0:T(8,128)(2,1)S(1)} %bitcast.44, bf16[1024,768]{1,0:T(8,128)(2,1)S(1)} %copy-done.4), custom_call_target="tpu_custom_call" | custom-call | tf_op jit(solution)/shard_map/pallas_call | solution.py:38
  79.6 1.2 copy-done.6
  80.7 1.4 copy-done.7
  82.1 1.6 shard_map.112
  83.8 0.9 copy-done.10
  84.7 12.4 %all_to_all.82 = f32[8,8,1024]{2,1,0:T(8,128)S(1)} all-to-all(f32[8,8,1024]{2,1,0:T(8,128)S(1)} %tile.13), channel_id=1, replica_groups=mesh['yh'=2,'co'=2,'x'=4,'yl'=2,'z'=8] {'x','yl'}, dimensions={0} | all-to-all | bytes 524288 | tf_op jit(solution)/shard_map/all_to_all | solution.py:181
  97.1 2.4 %shard_map.113 = (f32[8,1024]{1,0:T(8,128)S(1)}, bf16[1024,384]{1,0:T(8,128)(2,1)S(1)}) custom-call(f32[64,1024]{1,0:T(8,128)S(1)} %bitcast.47, f32[8,1024]{1,0:T(8,128)S(1)} %get-tuple-element.20.stat_ref, f32[384,1024]{1,0:T(8,128)S(1)} %copy-done.7, bf16[1024,512]{1,0:T(8,128)(2,1)S(1)} %bitcast.43), custom_call_target="tpu_custom_call" | custom-call | tf_op jit(solution)/shard_map/pallas_call | solution.py:38
  99.5 0.9 copy-done.9
  100.4 4.4 %all-to-all-start.4 = ((bf16[8,128,384]{2,1,0:T(8,128)(2,1)}), bf16[8,128,384]{2,1,0:T(8,128)(2,1)}, u32[]{:S(2)}, u32[]{:S(2)}) async-start(bf16[8,128,384]{2,1,0:T(8,128)(2,1)} %bitcast.48), calls=%async_computation.4 | async-start | bytes 1572864 | tf_op jit(solution)/shard_map/all_to_all | solution.py:181
  105.1 1.4 copy-done.5
  106.5 1.1 copy-done.11
  107.6 8.6 %shard_map.115 = (bf16[1024,384]{1,0:T(8,128)(2,1)}, bf16[1024,768]{1,0:T(8,128)(2,1)S(1)}) custom-call(s32[1]{0:T(128)} %bitcast.21.z_ref, bf16[1024,384]{1,0:T(8,128)(2,1)S(1)} %bitcast.45, bf16[1024,768]{1,0:T(8,128)(2,1)S(1)} %copy-done.5, bf16[1024,384]{1,0:T(8,128)(2,1)S(1)} %copy-done.11, f32[8,1024]{1,0:T(8,128)S(1)} %get-tuple-element.24.norm_ref), custom_call_target="tpu_custom_call" | custom-call | tf_op jit(solution)/shard_map/pallas_call | solution.py:38
  116.2 1.2 copy-done.8
  117.4 1.2 reduce_sum.33
  118.6 15.5 %all_to_all.83 = bf16[8,16,384]{2,1,0:T(8,128)(2,1)S(1)} all-to-all(bf16[8,16,384]{2,1,0:T(8,128)(2,1)S(1)} %bitcast.60), channel_id=1, replica_groups=mesh['yh'=2,'co'=2,'x'=4,'yl'=2,'z'=8] {'z'}, dimensions={0} | all-to-all | bytes 196608 | tf_op jit(solution)/shard_map/all_to_all | solution.py:181
  134.1 5.3 %all-to-all-start.7 = ((bf16[8,128,384]{2,1,0:T(8,128)(2,1)}), bf16[8,128,384]{2,1,0:T(8,128)(2,1)}, u32[]{:S(2)}, u32[]{:S(2)}) async-start(bf16[8,128,384]{2,1,0:T(8,128)(2,1)} %get-tuple-element.27), calls=%async_computation.8 | async-start | bytes 1572864 | tf_op jit(solution)/shard_map/all_to_all | solution.py:181
  139.5 0.9 shard_map.114
  140.3 9.6 %all-to-all-done.7 = bf16[8,128,384]{2,1,0:T(8,128)(2,1)} async-done(((bf16[8,128,384]{2,1,0:T(8,128)(2,1)}), bf16[8,128,384]{2,1,0:T(8,128)(2,1)}, u32[]{:S(2)}, u32[]{:S(2)}) %all-to-all-start.7) | async-done | bytes 786464 | tf_op jit(solution)/shard_map/all_to_all | solution.py:181
  150.0 1.0 tile.14
  150.9 5.8 %all-to-all-start.8 = ((bf16[8,128,384]{2,1,0:T(8,128)(2,1)}), bf16[8,128,384]{2,1,0:T(8,128)(2,1)S(1)}, u32[]{:S(2)}, u32[]{:S(2)}) async-start(bf16[8,128,384]{2,1,0:T(8,128)(2,1)} %tile.14), calls=%async_computation.9 | async-start | bytes 1572864 | tf_op jit(solution)/shard_map/all_to_all | solution.py:181
  156.8 9.4 %all-to-all-done.8 = bf16[8,128,384]{2,1,0:T(8,128)(2,1)S(1)} async-done(((bf16[8,128,384]{2,1,0:T(8,128)(2,1)}), bf16[8,128,384]{2,1,0:T(8,128)(2,1)S(1)}, u32[]{:S(2)}, u32[]{:S(2)}) %all-to-all-start.8) | async-done | bytes 786464 | tf_op jit(solution)/shard_map/all_to_all | solution.py:181
  166.3 3.5 %all-to-all-start.6 = ((bf16[8,128,384]{2,1,0:T(8,128)(2,1)}), bf16[8,128,384]{2,1,0:T(8,128)(2,1)S(1)}, u32[]{:S(2)}, u32[]{:S(2)}) async-start(bf16[8,128,384]{2,1,0:T(8,128)(2,1)} %bitcast.22), calls=%async_computation.6 | async-start | bytes 1572864 | tf_op jit(solution)/shard_map/all_to_all | solution.py:181
  169.8 1.1 convert_add_fusion
  171.0 2.5 %fusion = bf16[384,384]{1,0:T(8,128)(2,1)} fusion(bf16[8,128,384]{2,1,0:T(8,128)(2,1)} %all-to-all-done.7, bf16[8,128,384]{2,1,0:T(8,128)(2,1)S(1)} %all-to-all-done.8), kind=kOutput, calls=%fused_computation.1 | convolution fusion | flops 302137344 | bytes 1867776 | tf_op jit(solution)/shard_map/dot_general | solution.py:34
  173.5 5.9 %all-to-all-done.6 = bf16[8,128,384]{2,1,0:T(8,128)(2,1)S(1)} async-done(((bf16[8,128,384]{2,1,0:T(8,128)(2,1)}), bf16[8,128,384]{2,1,0:T(8,128)(2,1)S(1)}, u32[]{:S(2)}, u32[]{:S(2)}) %all-to-all-start.6) | async-done | bytes 786464 | tf_op jit(solution)/shard_map/all_to_all | solution.py:181
  179.3 5.0 %all-to-all-start.9 = ((bf16[8,48,384]{2,1,0:T(8,128)(2,1)}), bf16[8,48,384]{2,1,0:T(8,128)(2,1)S(1)}, u32[]{:S(2)}, u32[]{:S(2)}) async-start(bf16[8,48,384]{2,1,0:T(8,128)(2,1)} %bitcast.24), calls=%async_computation.10 | async-start | bytes 589824 | tf_op jit(solution)/shard_map/all_to_all | solution.py:181
  184.3 1.9 collective-permute-start.11
  186.2 0.8 reduce_sum.34
  187.0 4.6 %collective-permute-done.11 = bf16[128,768]{1,0:T(8,128)(2,1)S(1)} collective-permute-done((bf16[128,768]{1,0:T(8,128)(2,1)S(1)}, bf16[128,768]{1,0:T(8,128)(2,1)S(1)}, u32[]{:S(2)}, u32[]{:S(2)}) %collective-permute-start.11) | collective-permute-done | bytes 196640 | tf_op jit(solution)/shard_map/ppermute | solution.py:177
  191.6 0.7 fusion.2
  192.3 1.4 all-to-all-done.9
  193.7 0.7 convert_reduce_fusion
  194.4 1.6 fusion.4
  (52 shorter events, 2.1 us)
Async XLA Ops:
  7.2 10.3 %copy-start.13 = (bf16[128,768]{1,0:T(8,128)(2,1)S(1)}, bf16[128,768]{1,0:T(8,128)(2,1)}, u32[]{:S(2)}) copy-start(bf16[128,768]{1,0:T(8,128)(2,1)} %param.12) | copy-start | bytes 589828
  7.2 12.3 %copy-start.12 = (s32[128]{0:T(128)S(1)}, s32[128]{0:T(128)}, u32[]{:S(2)}) copy-start(s32[128]{0:T(128)} %param.13) | copy-start | bytes 1540
  7.2 12.4 %copy-start.16 = (bf16[128,384]{1,0:T(8,128)(2,1)S(1)}, bf16[128,384]{1,0:T(8,128)(2,1)}, u32[]{:S(2)}) copy-start(bf16[128,384]{1,0:T(8,128)(2,1)} %param.9) | copy-start | bytes 294916
  7.2 9.6 %collective-permute-start = (bf16[128,768]{1,0:T(8,128)(2,1)}, bf16[128,768]{1,0:T(8,128)(2,1)S(1)}, u32[]{:S(2)}, u32[]{:S(2)}) collective-permute-start(bf16[128,768]{1,0:T(8,128)(2,1)} %param.12), channel_id=1, source_target_pairs={{0,128},{128,0},{1,129},{129,1},{2,130},{130,2},{3,131},{131,3},{4... | collective-permute-start | bytes 589832 | tf_op jit(solution)/shard_map/ppermute | solution.py:177
  12.3 16.5 %all-to-all-start.2 = ((bf16[8,128,384]{2,1,0:T(8,128)(2,1)}), bf16[8,128,384]{2,1,0:T(8,128)(2,1)S(1)}, u32[]{:S(2)}, u32[]{:S(2)}) async-start(bf16[8,128,384]{2,1,0:T(8,128)(2,1)} %tile.12), calls=%async_computation.2 | async-start | bytes 1572864 | tf_op jit(solution)/shard_map/all_to_all | solution.py:181
  16.8 0.7 copy-start.14
  17.4 5.3 %copy-start = (bf16[384,3072]{1,0:T(8,128)(2,1)S(1)}, bf16[384,3072]{1,0:T(8,128)(2,1)}, u32[]{:S(2)}) copy-start(bf16[384,3072]{1,0:T(8,128)(2,1)} %w_ref.3) | copy-start | bytes 7077892
  19.4 2.1 %collective-permute-start.1 = (bf16[2,128,768]{2,1,0:T(8,128)(2,1)}, bf16[2,128,768]{2,1,0:T(8,128)(2,1)}, u32[]{:S(2)}, u32[]{:S(2)}) collective-permute-start(bf16[2,128,768]{2,1,0:T(8,128)(2,1)} %maximum_select_fusion.2), channel_id=1, source_target_pairs={{0,64},{64,0},{1,65},{65,1},{2,66},{66,2},{3,67},{67,3},{4,68},{68... | collective-permute-start | bytes 1179656 | tf_op jit(solution)/shard_map/ppermute | solution.py:177
  22.7 14.7 %copy-start.17 = (bf16[128,384]{1,0:T(8,128)(2,1)S(1)}, bf16[128,384]{1,0:T(8,128)(2,1)}, u32[]{:S(2)}) copy-start(bf16[128,384]{1,0:T(8,128)(2,1)} %param.10) | copy-start | bytes 294916
  28.8 19.6 %copy-start.1 = (bf16[8,128,384]{2,1,0:T(8,128)(2,1)}, bf16[8,128,384]{2,1,0:T(8,128)(2,1)S(1)}, u32[]{:S(2)}) copy-start(bf16[8,128,384]{2,1,0:T(8,128)(2,1)S(1)} %all-to-all-done.2) | copy-start | bytes 2359300
  28.9 18.5 %all-to-all-start = ((bf16[8,16,512]{2,1,0:T(8,128)(2,1)}), bf16[8,16,512]{2,1,0:T(8,128)(2,1)S(1)}, u32[]{:S(2)}, u32[]{:S(2)}) async-start(bf16[8,16,512]{2,1,0:T(8,128)(2,1)} %bitcast.8), calls=%async_computation | async-start | bytes 262144 | tf_op jit(solution)/shard_map/all_to_all | solution.py:181
  38.1 7.2 %collective-permute-start.2 = (bf16[128,768]{1,0:T(8,128)(2,1)}, bf16[128,768]{1,0:T(8,128)(2,1)}, u32[]{:S(2)}, u32[]{:S(2)}) collective-permute-start(bf16[128,768]{1,0:T(8,128)(2,1)} %get-tuple-element.31), channel_id=1, source_target_pairs={{0,1},{1,2},{2,3},{3,4},{4,5},{5,6},{6,7},{7,0},{8,9},{9,10},{10,1... | collective-permute-start | bytes 589832 | tf_op jit(solution)/shard_map/ppermute | solution.py:177
  39.6 6.8 %collective-permute-start.3 = (bf16[128,768]{1,0:T(8,128)(2,1)}, bf16[128,768]{1,0:T(8,128)(2,1)}, u32[]{:S(2)}, u32[]{:S(2)}) collective-permute-start(bf16[128,768]{1,0:T(8,128)(2,1)} %get-tuple-element.31), channel_id=1, source_target_pairs={{0,7},{1,0},{2,1},{3,2},{4,3},{5,4},{6,5},{7,6},{8,15},{9,8},{10,9... | collective-permute-start | bytes 589832 | tf_op jit(solution)/shard_map/ppermute | solution.py:177
  45.3 10.3 %collective-permute-start.4 = (bf16[128,768]{1,0:T(8,128)(2,1)}, bf16[128,768]{1,0:T(8,128)(2,1)}, u32[]{:S(2)}, u32[]{:S(2)}) collective-permute-start(bf16[128,768]{1,0:T(8,128)(2,1)} %collective-permute-done.2), channel_id=1, source_target_pairs={{0,1},{1,2},{2,3},{3,4},{4,5},{5,6},{6,7},{7,0},{8,9},{9,10},{10,1... | collective-permute-start | bytes 589832 | tf_op jit(solution)/shard_map/ppermute | solution.py:177
  46.4 10.0 %collective-permute-start.5 = (bf16[128,768]{1,0:T(8,128)(2,1)}, bf16[128,768]{1,0:T(8,128)(2,1)}, u32[]{:S(2)}, u32[]{:S(2)}) collective-permute-start(bf16[128,768]{1,0:T(8,128)(2,1)} %collective-permute-done.3), channel_id=1, source_target_pairs={{0,7},{1,0},{2,1},{3,2},{4,3},{5,4},{6,5},{7,6},{8,15},{9,8},{10,9... | collective-permute-start | bytes 589832 | tf_op jit(solution)/shard_map/ppermute | solution.py:177
  48.4 32.3 %all-to-all-start.1 = ((bf16[8,128,512]{2,1,0:T(8,128)(2,1)}), bf16[8,128,512]{2,1,0:T(8,128)(2,1)S(1)}, u32[]{:S(2)}, u32[]{:S(2)}) async-start(bf16[8,128,512]{2,1,0:T(8,128)(2,1)} %tile.11), calls=%async_computation.1 | async-start | bytes 2097152 | tf_op jit(solution)/shard_map/all_to_all | solution.py:181
  52.2 17.6 %copy-start.2 = (bf16[8,128,384]{2,1,0:T(8,128)(2,1)S(1)}, bf16[8,128,384]{2,1,0:T(8,128)(2,1)}, u32[]{:S(2)}) copy-start(bf16[8,128,384]{2,1,0:T(8,128)(2,1)} %copy-done.1) | copy-start | bytes 2359300
  55.6 7.1 %collective-permute-start.6 = (bf16[128,768]{1,0:T(8,128)(2,1)}, bf16[128,768]{1,0:T(8,128)(2,1)S(1)}, u32[]{:S(2)}, u32[]{:S(2)}) collective-permute-start(bf16[128,768]{1,0:T(8,128)(2,1)} %collective-permute-done.4), channel_id=1, source_target_pairs={{0,1},{1,2},{2,3},{3,4},{4,5},{5,6},{6,7},{7,0},{8,9},{9,10},{10,1... | collective-permute-start | bytes 589832 | tf_op jit(solution)/shard_map/ppermute | solution.py:177
  56.4 6.5 %collective-permute-start.7 = (bf16[128,768]{1,0:T(8,128)(2,1)}, bf16[128,768]{1,0:T(8,128)(2,1)S(1)}, u32[]{:S(2)}, u32[]{:S(2)}) collective-permute-start(bf16[128,768]{1,0:T(8,128)(2,1)} %collective-permute-done.5), channel_id=1, source_target_pairs={{0,7},{1,0},{2,1},{3,2},{4,3},{5,4},{6,5},{7,6},{8,15},{9,8},{10,9... | collective-permute-start | bytes 589832 | tf_op jit(solution)/shard_map/ppermute | solution.py:177
  62.7 5.9 %collective-permute-start.8 = (bf16[64,768]{1,0:T(8,128)(2,1)S(1)}, bf16[64,768]{1,0:T(8,128)(2,1)S(1)}, u32[]{:S(2)}, u32[]{:S(2)}) collective-permute-start(bf16[64,768]{1,0:T(8,128)(2,1)S(1)} %slice.16), channel_id=1, source_target_pairs={{0,1},{1,2},{2,3},{3,4},{4,5},{5,6},{6,7},{7,0},{8,9},{9,10},{10,1... | collective-permute-start | bytes 294920 | tf_op jit(solution)/shard_map/ppermute | solution.py:177
  62.9 6.3 %collective-permute-start.9 = (bf16[64,768]{1,0:T(8,128)(2,1)S(1)}, bf16[64,768]{1,0:T(8,128)(2,1)S(1)}, u32[]{:S(2)}, u32[]{:S(2)}) collective-permute-start(bf16[64,768]{1,0:T(8,128)(2,1)S(1)} %slice.17), channel_id=1, source_target_pairs={{0,7},{1,0},{2,1},{3,2},{4,3},{5,4},{6,5},{7,6},{8,15},{9,8},{10,9... | collective-permute-start | bytes 294920 | tf_op jit(solution)/shard_map/ppermute | solution.py:177
  69.9 1.4 copy-start.4
  79.6 1.2 copy-start.6
  80.7 1.4 copy-start.7
  83.8 0.9 copy-start.10
  99.5 0.9 copy-start.9
  100.4 4.6 %copy-start.3 = (bf16[8,128,384]{2,1,0:T(8,128)(2,1)S(1)}, bf16[8,128,384]{2,1,0:T(8,128)(2,1)}, u32[]{:S(2)}) copy-start(bf16[8,128,384]{2,1,0:T(8,128)(2,1)} %copy-done.1) | copy-start | bytes 2359300
  100.4 17.0 %all-to-all-start.4 = ((bf16[8,128,384]{2,1,0:T(8,128)(2,1)}), bf16[8,128,384]{2,1,0:T(8,128)(2,1)}, u32[]{:S(2)}, u32[]{:S(2)}) async-start(bf16[8,128,384]{2,1,0:T(8,128)(2,1)} %bitcast.48), calls=%async_computation.4 | async-start | bytes 1572864 | tf_op jit(solution)/shard_map/all_to_all | solution.py:181
  104.8 89.6 %reduce-scatter.2.cloned.1.call-start = ((), (), s32[]{:S(2)}) async-start(), calls=%async_computation.11 | async-start | bytes 1769472 | tf_op jit(solution)/shard_map/reduce_scatter | solution.py:244
  105.1 1.4 copy-start.5
  106.5 1.1 copy-start.11
  116.2 1.2 copy-start.8
  134.1 15.8 %all-to-all-start.7 = ((bf16[8,128,384]{2,1,0:T(8,128)(2,1)}), bf16[8,128,384]{2,1,0:T(8,128)(2,1)}, u32[]{:S(2)}, u32[]{:S(2)}) async-start(bf16[8,128,384]{2,1,0:T(8,128)(2,1)} %get-tuple-element.27), calls=%async_computation.8 | async-start | bytes 1572864 | tf_op jit(solution)/shard_map/all_to_all | solution.py:181
  150.9 15.4 %all-to-all-start.8 = ((bf16[8,128,384]{2,1,0:T(8,128)(2,1)}), bf16[8,128,384]{2,1,0:T(8,128)(2,1)S(1)}, u32[]{:S(2)}, u32[]{:S(2)}) async-start(bf16[8,128,384]{2,1,0:T(8,128)(2,1)} %tile.14), calls=%async_computation.9 | async-start | bytes 1572864 | tf_op jit(solution)/shard_map/all_to_all | solution.py:181
  156.7 13.1 %collective-permute-start.10 = (bf16[2,128,768]{2,1,0:T(8,128)(2,1)S(1)}, bf16[2,128,768]{2,1,0:T(8,128)(2,1)}, u32[]{:S(2)}, u32[]{:S(2)}) collective-permute-start(bf16[2,128,768]{2,1,0:T(8,128)(2,1)S(1)} %dynamic-slice_bitcast_fusion), channel_id=1, source_target_pairs={{0,64},{64,0},{1,65},{65,1},{2,66},{66,2},{3,67},{67,3},{4,68},{68... | collective-permute-start | bytes 1179656 | tf_op jit(solution)/shard_map/ppermute | solution.py:177
  166.3 13.0 %all-to-all-start.6 = ((bf16[8,128,384]{2,1,0:T(8,128)(2,1)}), bf16[8,128,384]{2,1,0:T(8,128)(2,1)S(1)}, u32[]{:S(2)}, u32[]{:S(2)}) async-start(bf16[8,128,384]{2,1,0:T(8,128)(2,1)} %bitcast.22), calls=%async_computation.6 | async-start | bytes 1572864 | tf_op jit(solution)/shard_map/all_to_all | solution.py:181
  170.9 20.6 %copy-start.15 = (bf16[128,768]{1,0:T(8,128)(2,1)S(1)}, bf16[128,768]{1,0:T(8,128)(2,1)}, u32[]{:S(2)}) copy-start(bf16[128,768]{1,0:T(8,128)(2,1)} %param.7) | copy-start | bytes 589828
  179.3 14.4 %all-to-all-start.9 = ((bf16[8,48,384]{2,1,0:T(8,128)(2,1)}), bf16[8,48,384]{2,1,0:T(8,128)(2,1)S(1)}, u32[]{:S(2)}, u32[]{:S(2)}) async-start(bf16[8,48,384]{2,1,0:T(8,128)(2,1)} %bitcast.24), calls=%async_computation.10 | async-start | bytes 589824 | tf_op jit(solution)/shard_map/all_to_all | solution.py:181
  184.3 7.3 %collective-permute-start.11 = (bf16[128,768]{1,0:T(8,128)(2,1)S(1)}, bf16[128,768]{1,0:T(8,128)(2,1)S(1)}, u32[]{:S(2)}, u32[]{:S(2)}) collective-permute-start(bf16[128,768]{1,0:T(8,128)(2,1)S(1)} %fusion.3), channel_id=1, source_target_pairs={{0,128},{128,0},{1,129},{129,1},{2,130},{130,2},{3,131},{131,3},{4... | collective-permute-start | bytes 589832 | tf_op jit(solution)/shard_map/ppermute | solution.py:177
Sparse Core Ops, SparseCore 0:
  117.5 40.8 reduce-scatter.1

commit v2 on v1

v2 whole, which is shorter than its diff:
```python
import math

import jax
import jax.numpy as jnp
from jax import lax
from jax.experimental import pallas as pl
from jax.experimental.pallas import tpu as pltpu
from jax.sharding import Mesh
from jax.sharding import PartitionSpec as P

HD = 128
HEADS = 3
COLS = HEADS * HD
TOK = 128
SIDE = 8
TILE = TOK * SIDE
QB = 256
SCALE = 1.0 / math.sqrt(HD)
LOG2E = math.log2(math.e)
PEER = TOK // SIDE
SPAN = 768
QUAD = ("x", "yl")
F32 = jnp.float32
BF16 = jnp.bfloat16
NT = (((1,), (1,)), ((), ()))
TN = (((0,), (0,)), ((), ()))
HBM = pl.BlockSpec(memory_space=pltpu.HBM)
VMEM = pl.BlockSpec(memory_space=pltpu.VMEM)
SMEM = pl.BlockSpec(memory_space=pltpu.SMEM)
MIB = 1024 * 1024
STAT = 16
SLAB = TOK + 3 * STAT


def dot(left, right, dims=(((1,), (0,)), ((), ()))):
    return lax.dot_general(left, right, dims, preferred_element_type=F32)


def far(array, parts=1):
    return array, parts


def block_copies(source, dest, sems, first, parts):
    width = source.shape[-1] // parts
    found = []
    for n in range(parts):
        here, there = source, dest
        if parts > 1:
            here, there = (r.at[:, n * width : (n + 1) * width] for r in (source, dest))
        found.append(pltpu.make_async_copy(here, there, sems.at[first + n]))
    return found


def call(body, out, *args, mib, stack=None):
    arg_parts = [arg[1] if isinstance(arg, tuple) else 0 for arg in args]
    args = [arg[0] if isinstance(arg, tuple) else arg for arg in args]
    out_parts = [one[1] if isinstance(one[1], int) else 0 for one in out]
    out = [one[0] if isinstance(one[1], int) else one for one in out]
    n_in, n_out = len(args), len(out)
    far_in = [i for i in range(n_in) if arg_parts[i]]
    far_out = [i for i in range(n_out) if out_parts[i]]
    n_load, n_store = sum(arg_parts), sum(out_parts)

    def kernel(*refs):
        ins, outs = list(refs[:n_in]), list(refs[n_in : n_in + n_out])
        rest = list(refs[n_in + n_out :])
        if stack:
            pieces, rest = rest[:SIDE], rest[SIDE:]
            piece_sem, whole = rest.pop(), rest.pop()
            outs.append(whole)
        loads, stores = {}, {}
        load_sem = rest.pop(0) if n_load else None
        store_sem = rest.pop(0) if n_store else None
        first = 0
        for i in far_in:
            spot = rest.pop(0)
            loads[i] = block_copies(ins[i], spot, load_sem, first, arg_parts[i])
            first += arg_parts[i]
            ins[i] = spot
        first = 0
        for i in far_out:
            spot = rest.pop(0)
            stores[i] = block_copies(spot, outs[i], store_sem, first, out_parts[i])
            first += out_parts[i]
            outs[i] = spot
        for n in range(max(arg_parts)):
            for i in far_in:
                if n < arg_parts[i]:
                    loads[i][n].start()
        for i in far_in:
            if arg_parts[i] == 1:
                loads[i][0].wait()
        started = set()

        def ready(i, n):
            loads[i][n].wait()

        def done(i, n):
            stores[i][n].start()
            started.add((i, n))

        steps = (ready, done) if max(arg_parts) > 1 or max(out_parts) > 1 else ()
        body(*steps, *ins, *outs, *rest)
        for i in far_out:
            for n in range(out_parts[i]):
                if (i, n) not in started:
                    stores[i][n].start()
        if stack:
            stores[n_out] = [
                pltpu.make_async_copy(
                    whole.at[rows_of(around(ins[0][0], step)), :], piece, piece_sem.at[step]
                )
                for step, piece in enumerate(pieces)
            ]
            for copy in stores[n_out]:
                copy.start()
        for i in stores:
            for copy in stores[i]:
                copy.wait()

    dma = pltpu.SemaphoreType.DMA
    return pl.pallas_call(
        kernel,
        out_shape=[
            pltpu.HBM(*one) if out_parts[i] else jax.ShapeDtypeStruct(*one)
            for i, one in enumerate(out)
        ]
        + ([pltpu.HBM((TOK, stack), BF16)] * SIDE if stack else []),
        in_specs=[
            HBM if arg_parts[i] else SMEM if args[i].shape == (1,) else VMEM for i in range(n_in)
        ],
        out_specs=[HBM if parts else VMEM for parts in out_parts] + ([HBM] * SIDE if stack else []),
        scratch_shapes=[
            *([dma((n_load,))] if n_load else []),
            *([dma((n_store,))] if n_store else []),
            *[pltpu.VMEM(args[i].shape, args[i].dtype) for i in far_in],
            *[pltpu.VMEM(*out[i]) for i in far_out],
            *([pltpu.VMEM((TILE, stack), BF16), dma((SIDE,))] if stack else []),
        ],
        compiler_params=pltpu.CompilerParams(vmem_limit_bytes=mib * MIB),
    )(
        *[
            pltpu.with_memory_space_constraint(arg, pltpu.HBM) if arg_parts[i] else arg
            for i, arg in enumerate(args)
        ]
    )


def around(pos, step):
    return lax.rem(pos + (step + SIDE), SIDE)


def rows_of(pos):
    return pl.ds(pl.multiple_of(pos * TOK, TOK), TOK)


def head(idx):
    return slice(idx * HD, (idx + 1) * HD)


def block_of(slot):
    return (slot >> 7) & (SIDE - 1)


def sorted_by_block(slot_row):
    first = lax.broadcasted_iota(jnp.int32, (TOK, TOK), 0)
    second = lax.broadcasted_iota(jnp.int32, (TOK, TOK), 1)
    spread = jnp.where(first == second, slot_row.astype(F32), 0.0)
    slot_col = jnp.sum(spread, axis=1, keepdims=True).astype(jnp.int32)
    same = (block_of(slot_row) == block_of(slot_col)) & (first < second)
    ahead = jnp.sum(jnp.where(same, 1.0, 0.0), axis=0, keepdims=True).astype(jnp.int32)
    rank = block_of(slot_row) * PEER + ahead
    order = jnp.where(first == rank, 1.0, 0.0).astype(BF16)
    place = jnp.where(
        second == 0,
        (slot_col >> 10).astype(F32),
        jnp.where(second == 1, (slot_col & (TOK - 1)).astype(F32), 0.0),
    )
    return order, place


def project_body(
    y_ref, core_ref, d0_ref, d1_ref, d2_ref, d3_ref, w_ref, row_ref, pay_ref, cut_ref
):
    y_pos, core = y_ref[0], core_ref[0]
    order, place = sorted_by_block(row_ref[...])
    total = jnp.zeros((TOK, COLS), F32)
    pieces = (
        (d0_ref, y_pos, core),
        (d1_ref, 1 - y_pos, core),
        (d2_ref, y_pos, 1 - core),
        (d3_ref, 1 - y_pos, 1 - core),
    )
    for d_ref, along, across in pieces:
        part = 2 * along + across
        here = pl.ds(pl.multiple_of(part * SPAN, SPAN), SPAN)
        total += dot(d_ref[...], w_ref[:, here], NT)
        rows = dot(order, d_ref[...]).astype(BF16)
        cut_ref[2 * part] = rows[:, :COLS]
        cut_ref[2 * part + 1] = rows[:, COLS:]
    pay_ref[:, :COLS] = dot(order, total.astype(BF16)).astype(BF16)
    pay_ref[:, COLS:] = dot(order, place.astype(BF16)).astype(BF16)


def forward_body(ready, done, q_ref, kv_ref, out_ref, lse_ref):
    lse_ref[...] = jnp.zeros_like(lse_ref)
    for idx in range(HEADS):
        ready(0, idx)
        ready(1, idx)
        ready(1, HEADS + idx)
        keys = kv_ref[:, head(idx)]
        values_t = kv_ref[:, head(HEADS + idx)].T
        for start in range(0, TILE, QB):
            cols = slice(start, start + QB)
            scores = dot(keys, q_ref[cols, head(idx)], NT)
            peak = jnp.max(scores, axis=0, keepdims=True)
            weights = jnp.exp2((scores - peak) * (SCALE * LOG2E))
            total = jnp.sum(weights, axis=0, keepdims=True)
            out_ref[head(idx), cols] = (dot(values_t, weights.astype(BF16)) / total).astype(BF16)
            lse_ref[idx : idx + 1, cols] = peak * SCALE + jnp.log(total)


def places(arrived):
    place = arrived.astype(F32)
    target = place[:, 0:1] * float(TOK) + place[:, 1:2]
    lanes = lax.broadcasted_iota(jnp.int32, (place.shape[0], TILE), 1)
    return jnp.where(lanes == target.astype(jnp.int32), 1.0, 0.0).astype(BF16)


def terms(value, count):
    found = []
    for _ in range(count):
        found.append(value.astype(BF16))
        value = value - found[-1].astype(F32)
    return found


def delta_body(ready, done, arrived_ref, out_ref, lse_ref, grad_ref, send_ref):
    order = places(arrived_ref[:, COLS:])
    deltas = []
    for idx in range(HEADS):
        grad_t = dot(arrived_ref[:, head(idx)].T, order)
        grad_ref[:, head(idx)] = grad_t.T.astype(BF16)
        done(0, idx)
        deltas.append(jnp.sum(grad_t * out_ref[head(idx), :].astype(F32), axis=0, keepdims=True))
        rows = dot(out_ref[head(idx), :], order, NT).T.astype(BF16)
        for peer in range(SIDE):
            send_ref[peer, :TOK, head(idx)] = rows[peer * TOK : (peer + 1) * TOK]
    zero = jnp.zeros((1, TILE), BF16)
    stats = [t for t in terms(lse_ref[:HEADS, :], 3)]
    stats += terms(jnp.concatenate(deltas, axis=0), 2)
    stats = jnp.concatenate([t.astype(F32) for t in stats] + [zero.astype(F32)], axis=0).astype(BF16)
    for peer in range(SIDE):
        for n, start in enumerate(range(0, TILE, COLS)):
            width = min(COLS, TILE - start)
            send_ref[peer, TOK + STAT * n : TOK + STAT * (n + 1), :width] = stats[:, start : start + width]


def merge_body(quad_ref, all_ref, arrived_ref, norm_ref, att_ref):
    lses, deltas = [], []
    for peer in range(SIDE):
        parts = []
        for n, start in enumerate(range(0, TILE, COLS)):
            width = min(COLS, TILE - start)
            parts.append(all_ref[peer, TOK + STAT * n : TOK + STAT * (n + 1), :width].astype(F32))
        stats = jnp.concatenate(parts, axis=1)
        lses.append(stats[0:3] + stats[3:6] + stats[6:9])
        deltas.append(stats[9:12] + stats[12:15])
    peak = lses[0]
    for one in lses[1:]:
        peak = jnp.maximum(peak, one)
    weights = [jnp.exp(one - peak) for one in lses]
    total = sum(weights)
    norm_ref[...] = jnp.zeros_like(norm_ref)
    norm_ref[:HEADS, :] = peak + jnp.log(total)
    norm_ref[HEADS : 2 * HEADS, :] = sum(w * d for w, d in zip(weights, deltas)) / total
    shares = jnp.concatenate([w / total for w in weights], axis=0)
    mine = places(arrived_ref[rows_of(quad_ref[0]), COLS:])
    shares = sum(dot(mine, term, NT) for term in terms(shares, 2))
    for idx in range(HEADS):
        out = jnp.zeros((TOK, HD), F32)
        for peer in range(SIDE):
            col = HEADS * peer + idx
            out += all_ref[peer, :TOK, head(idx)].astype(F32) * shares[:, col : col + 1]
        att_ref[:, head(idx)] = out.astype(BF16)


def backward_body(ready, done, quad_ref, q_ref, kv_ref, grad_ref, norm_ref, dkv_ref, dq_ref):
    for idx in range(HEADS):
        ready(1, idx)
        ready(2, idx)
        ready(2, HEADS + idx)
        ready(3, idx)
        keys = kv_ref[:, head(idx)]
        keys_t = keys.T
        values = kv_ref[:, head(HEADS + idx)]
        d_keys = jnp.zeros((TILE, HD), F32)
        d_values = jnp.zeros((TILE, HD), F32)
        for start in range(0, TILE, QB):
            cols = slice(start, start + QB)
            query = q_ref[cols, head(idx)]
            grad = grad_ref[cols, head(idx)]
            scores = dot(keys, query, NT) * SCALE
            weights = jnp.exp2((scores - norm_ref[idx : idx + 1, cols]) * LOG2E)
            d_probs = dot(values, grad, NT)
            d_scores = weights * (d_probs - norm_ref[HEADS + idx : HEADS + idx + 1, cols])
            d_scores = d_scores.astype(BF16)
            d_values += dot(weights.astype(BF16), grad)
            d_keys += dot(d_scores, query)
            dq_ref[cols, head(idx)] = (dot(keys_t, d_scores) * SCALE).T.astype(BF16)
        dkv_ref[:, head(idx)] = (d_keys * SCALE).astype(BF16)
        dkv_ref[:, head(HEADS + idx)] = d_values.astype(BF16)
        done(0, idx)
        done(0, HEADS + idx)


def output_body(sorted_ref, w_ref, row_ref, part_ref):
    order, _ = sorted_by_block(row_ref[...])
    attended = dot(order, sorted_ref[...], TN).astype(BF16)
    for part in range(4):
        part_ref[part] = dot(attended, w_ref[:, part * SPAN : (part + 1) * SPAN]).astype(BF16)


def weight_body(both_ref, out_ref):
    total = jnp.zeros((COLS, COLS), F32)
    for peer in range(SIDE):
        total += dot(both_ref[peer, :, COLS:], both_ref[peer, :, :COLS], TN)
    out_ref[...] = total.astype(BF16)


def shift(value, axis, step, size):
    return lax.ppermute(value, axis, [(i, (i + step) % size) for i in range(size)])


def exchange(value, axis):
    return lax.all_to_all(value, axis, split_axis=0, concat_axis=0, tiled=True)


def gather_quad(value):
    return exchange(jnp.tile(value, (SIDE, 1)), QUAD)


def scatter_quad(blocks):
    return [blocks[0]] + [shift(blocks[step], QUAD, step, SIDE) for step in range(1, SIDE)]


def pick(value, idx, axis):
    return lax.dynamic_index_in_dim(value, idx, axis, keepdims=False)


def together(*values):
    return lax.optimization_barrier(values)


def on_device(main_hidden, ctrl_query, ctrl_key, ctrl_value, w_out, d_mixed, control_slot):
    y_pos, core = lax.axis_index("yh"), lax.axis_index("co")
    quad = lax.axis_index("x") * 2 + lax.axis_index("yl")
    slot_row = control_slot.reshape(1, TOK)
    y_one, core_one, quad_one = (p.reshape(1).astype(jnp.int32) for p in (y_pos, core, quad))

    key_value = jnp.concatenate([ctrl_key, ctrl_value], axis=1)
    key_value = lax.all_gather(key_value, "z", axis=0, tiled=True)
    along = shift(d_mixed, "yh", 1, 2)
    across = shift(d_mixed, "co", 1, 2)
    query = jnp.tile(ctrl_query, (SIDE, 1))
    query, along, across = together(query, along, across)
    query = exchange(query, QUAD)
    both = shift(along, "co", 1, 2)
    payload, cuts = call(
        project_body,
        [far(((TOK, COLS + HD), BF16)), far(((SIDE, TOK, COLS), BF16))],
        y_one,
        core_one,
        far(d_mixed),
        far(along),
        far(across),
        far(both),
        far(w_out),
        slot_row,
        mib=16,
    )
    payload, query = together(payload, query)
    payload = exchange(payload, "z")
    arrived = gather_quad(payload)
    out_t, lse = call(
        forward_body,
        [((COLS, TILE), BF16), ((SIDE, TILE), F32)],
        far(query, HEADS),
        far(key_value, 2 * HEADS),
        mib=20,
    )
    grad, send = call(
        delta_body,
        [far(((TILE, COLS), BF16), HEADS), far(((SIDE, SLAB, COLS), BF16))],
        arrived,
        out_t,
        lse,
        mib=24,
    )
    norms, attended = call(
        merge_body,
        [((SIDE, TILE), F32), far(((TOK, COLS), BF16))],
        quad_one,
        exchange(send, QUAD),
        arrived,
        mib=16,
    )
    d_key_value, *d_query = call(
        backward_body,
        [far(((TILE, 2 * COLS), BF16), 2 * HEADS)],
        quad_one,
        far(query, HEADS),
        far(key_value, 2 * HEADS),
        far(grad, HEADS),
        norms,
        mib=24,
        stack=COLS,
    )
    attended = exchange(attended, "z")
    d_key_value, attended = together(d_key_value, attended)
    d_key_value = lax.psum_scatter(d_key_value, "z", scatter_dimension=0, tiled=True)
    spread = jnp.broadcast_to(attended[None], (SIDE, TOK, COLS))
    spread = jnp.concatenate([spread, cuts], axis=2)
    spread, attended = together(spread, attended)
    gathered = exchange(spread, QUAD)
    (partial_out,) = call(
        output_body,
        [((4, TOK, SPAN), BF16)],
        attended,
        w_out,
        slot_row,
        mib=16,
    )

    by_core = partial_out.reshape(2, 2, TOK, SPAN)
    summed = pick(by_core, core, 1).astype(F32) + shift(
        pick(by_core, 1 - core, 1), "co", 1, 2
    ).astype(F32)
    residual = pick(summed, y_pos, 0) + shift(
        pick(summed, 1 - y_pos, 0).astype(BF16), "yh", 1, 2
    ).astype(F32)
    main_mixed = (main_hidden.astype(F32) + residual).astype(BF16)

    (d_w_out,) = call(
        weight_body,
        [far(((COLS, COLS), BF16))],
        gathered,
        mib=16,
    )
    d_w_out, *d_query = together(d_w_out, *d_query)
    d_query = sum(block.astype(F32) for block in scatter_quad(d_query))
    d_w_out = exchange(d_w_out, "z").reshape(SIDE, COLS // SIDE, COLS)
    d_w_out = jnp.sum(d_w_out.astype(F32), axis=0).T
    return (
        main_mixed,
        d_query.astype(BF16),
        d_key_value[:, :COLS],
        d_key_value[:, COLS:],
        d_w_out,
    )


def solution(mesh):
    fine = Mesh(mesh.devices.reshape(2, 2, 4, 2, 8), ("yh", "co", "x", "yl", "z"))
    grp, blk = ("yh", "co"), ("x", "yl", "z")
    in_specs = (
        P(blk, grp),
        P(blk, grp),
        P(blk, grp),
        P(blk, grp),
        P(grp, None),
        P(blk, grp),
        P(blk),
    )
    out_specs = (
        P(blk, grp),
        P(blk, grp),
        P(blk, grp),
        P(blk, grp),
        P(grp, blk),
    )
    return jax.shard_map(
        on_device, mesh=fine, in_specs=in_specs, out_specs=out_specs, check_vma=False
    )
```

time: 205 us -> 178 us (0.87)
  local copies, waits for them, and re-layouts: 26.5 us -> 6.52 us
  Pallas kernels: 23.7 us -> 35.7 us
  starting transfers between devices: 57.1 us -> 45.4 us
  waiting for transfers between devices: 42 us -> 53.7 us
  blocking collectives: 27.9 us -> 16.6 us
  other arithmetic: 8.79 us -> 5.18 us
  matrix products: 2.5 us -> 0 us
    unnamed x44 -> x32, local copies, waits for them, and re-layouts: 19.5 us -> 1.74 us
    pallas_call x6 -> x7, Pallas kernels: 23.7 us -> 35.7 us  [call(): pl.pallas_call(kernel, out_shape=[pltpu.HBM(*one) if out_parts[i] else ja...]
    all_to_all x2 -> x1, blocking collectives: 27.9 us -> 16.6 us  [exchange(): return lax.all_to_all(value, axis, split_axis=0, concat_axis=0, tiled=True)]
    all_to_all x8 -> x6, starting transfers between devices: 40.8 us -> 30.6 us  [exchange(): return lax.all_to_all(value, axis, split_axis=0, concat_axis=0, tiled=True)]
    all_to_all x8 -> x6, waiting for transfers between devices: 30.5 us -> 39.9 us  [exchange(): return lax.all_to_all(value, axis, split_axis=0, concat_axis=0, tiled=True)]
    select_n x3 -> x0, other arithmetic: 4.29 us -> none  [the longest x2 3.06 us: on_device(): jnp.where(y_pos == 0, jnp.stack([d_mixed, other]), jnp.stack([other, d_mi...]
    concatenate x0 -> x2, other arithmetic: none -> 2.94 us  [the longest x1 1.64 us: on_device(): key_value = jnp.concatenate([ctrl_key, ctrl_value], axis=1)]
    another operation x4 -> x1, local copies, waits for them, and re-layouts: 3.91 us -> 1.06 us  [gather_quad(): return exchange(jnp.tile(value, (SIDE, 1)), QUAD)]
  transfers between devices with their start and end apart: 21 -> 20, of which waited for: 11 -> 10; matrix products, arithmetic and copies ran while one was open for 13% -> 4% of each run, Pallas kernels for 10% -> 16%
where the time goes in v2:
time: 178 us; the launch traced here: 177 us
  waiting for transfers between devices  53.7 us (30%)
  starting transfers between devices  45.4 us (26%)
  Pallas kernels  35.7 us (20%)
  blocking collectives  16.6 us (9%)
  between operations  14.3 us (8%)
  local copies, waits for them, and re-layouts  6.52 us (4%)
  other arithmetic  5.18 us (3%)
    all_to_all x6, waiting for transfers between devices, exchange(): return lax.all_to_all(value, axis, split_axis=0, concat_axis=0, tiled=True)  39.9 us
    pallas_call x7, Pallas kernels, call(): pl.pallas_call(kernel, out_shape=[pltpu.HBM(*one) if out_parts[i] else ja...  35.7 us
    all_to_all x6, starting transfers between devices, exchange(): return lax.all_to_all(value, axis, split_axis=0, concat_axis=0, tiled=True)  30.6 us
    all_to_all x1, blocking collectives, exchange(): return lax.all_to_all(value, axis, split_axis=0, concat_axis=0, tiled=True)  16.6 us
    ppermute x12, starting transfers between devices, shift(): lax.ppermute(value, axis, [(i, (i + step) % size) for i in range(size)])  14.8 us
    ppermute x12, waiting for transfers between devices, shift(): lax.ppermute(value, axis, [(i, (i + step) % size) for i in range(size)])  13.8 us
  transfers between devices with their start and end apart: 20, of which 10 were waited for; matrix products, arithmetic and copies ran while one was open for 4% of the time, Pallas kernels for 16%

profile of v2, /device:TPU:32, one launch (start us, length us, event | category | flops | bytes accessed | tf_op | source)
XLA Modules:
  0.0 177.4 jit_solution(4013914068598664413)
XLA Ops:
  7.2 0.0 all-gather.2.cloned.1.call-start
  7.2 1.6 pad_maximum_fusion.1
  8.9 0.0 all-gather.2.cloned.1.call-update
  8.9 3.3 %collective-permute-start = (bf16[128,768]{1,0:T(8,128)(2,1)}, bf16[128,768]{1,0:T(8,128)(2,1)S(1)}, u32[]{:S(2)}, u32[]{:S(2)}) collective-permute-start(bf16[128,768]{1,0:T(8,128)(2,1)} %refs_2_.1), channel_id=1, source_target_pairs={{0,128},{128,0},{1,129},{129,1},{2,130},{130,2},{3,131},{131,3},{4... | collective-permute-start | bytes 589832 | tf_op jit(solution)/shard_map/ppermute | solution.py:332
  12.2 0.0 collective-permute-start.1
  12.2 5.2 %collective-permute-done.refs_3_ = bf16[128,768]{1,0:T(8,128)(2,1)S(1)} collective-permute-done((bf16[128,768]{1,0:T(8,128)(2,1)}, bf16[128,768]{1,0:T(8,128)(2,1)S(1)}, u32[]{:S(2)}, u32[]{:S(2)}) %collective-permute-start) | collective-permute-done | bytes 196640 | tf_op jit(solution)/shard_map/ppermute | solution.py:332
  17.3 0.0 collective-permute-done.1.refs_4_
  17.3 2.0 %tile.8 = bf16[8,128,384]{2,1,0:T(8,128)(2,1)} broadcast(bf16[128,384]{1,0:T(8,128)(2,1)} %param.8), dimensions={1,2} | broadcast | bytes 884736 | tf_op jit(solution)/shard_map/tile | solution.py:365
  19.3 5.3 %all-to-all-start = ((bf16[8,128,384]{2,1,0:T(8,128)(2,1)}), bf16[8,128,384]{2,1,0:T(8,128)(2,1)S(1)}, u32[]{:S(2)}, u32[]{:S(2)}) async-start(bf16[8,128,384]{2,1,0:T(8,128)(2,1)} %bitcast.5), calls=%async_computation | async-start | bytes 1572864 | tf_op jit(solution)/shard_map/all_to_all | solution.py:336
  24.6 0.0 collective-permute-start.2
  24.6 1.4 collective-permute-done.2.refs_5_
  26.1 0.7 copy-done.7
  26.7 4.4 %shard_map.110 = (bf16[128,512]{1,0:T(8,128)(2,1)}, bf16[8,128,384]{2,1,0:T(8,128)(2,1)}) custom-call(s32[1]{0:T(128)} %bitcast.1.refs_0_, s32[1]{0:T(128)} %bitcast.2.refs_1_, bf16[128,768]{1,0:T(8,128)(2,1)} %refs_2_.1, bf16[128,768]{1,0:T(8,128)(2,1)} %copy-done.5, bf16[128,768]{1,0:T(8,128)(2,1)} %copy-done.6, bf16[128,768]{1,0:T(8,128)(2,1)} %copy-done.7, ...), custom_call_target="tpu_custom_call" | custom-call | tf_op jit(solution)/shard_map/pallas_call | solution.py:122
  31.1 5.0 %all-to-all-done = bf16[8,128,384]{2,1,0:T(8,128)(2,1)S(1)} async-done(((bf16[8,128,384]{2,1,0:T(8,128)(2,1)}), bf16[8,128,384]{2,1,0:T(8,128)(2,1)S(1)}, u32[]{:S(2)}, u32[]{:S(2)}) %all-to-all-start) | async-done | bytes 786464 | tf_op jit(solution)/shard_map/all_to_all | solution.py:336
  36.1 16.6 %all_to_all.60 = bf16[8,16,512]{2,1,0:T(8,128)(2,1)S(1)} all-to-all(bf16[8,16,512]{2,1,0:T(8,128)(2,1)} %bitcast.42), channel_id=1, replica_groups=mesh['yh'=2,'co'=2,'x'=4,'yl'=2,'z'=8] {'z'}, dimensions={0} | all-to-all | bytes 262144 | tf_op jit(solution)/shard_map/all_to_all | solution.py:336
  52.7 1.1 tile.21
  53.8 3.7 %all-to-all-start.2 = ((bf16[8,128,512]{2,1,0:T(8,128)(2,1)}), bf16[8,128,512]{2,1,0:T(8,128)(2,1)S(1)}, u32[]{:S(2)}, u32[]{:S(2)}) async-start(bf16[8,128,512]{2,1,0:T(8,128)(2,1)} %tile.21), calls=%async_computation.2 | async-start | bytes 2097152 | tf_op jit(solution)/shard_map/all_to_all | solution.py:336
  57.5 0.0 all-gather.2.cloned.1.call-done.refs_1_.refs_2_
  57.5 10.1 %shard_map.111 = (bf16[384,1024]{1,0:T(8,128)(2,1)S(1)}, f32[8,1024]{1,0:T(8,128)S(1)}) custom-call(bf16[1024,384]{1,0:T(8,128)(2,1)} %bitcast.38, bf16[1024,768]{1,0:T(8,128)(2,1)} %all-gather.2.cloned.1.call-done.refs_1_.refs_2_), custom_call_target="tpu_custom_call" | custom-call | tf_op jit(solution)/shard_map/pallas_call | solution.py:122
  67.6 4.3 %all-to-all-done.2 = bf16[8,128,512]{2,1,0:T(8,128)(2,1)S(1)} async-done(((bf16[8,128,512]{2,1,0:T(8,128)(2,1)}), bf16[8,128,512]{2,1,0:T(8,128)(2,1)S(1)}, u32[]{:S(2)}, u32[]{:S(2)}) %all-to-all-start.2) | async-done | bytes 1048608 | tf_op jit(solution)/shard_map/all_to_all | solution.py:336
  71.9 4.8 %shard_map.112 = (bf16[1024,384]{1,0:T(8,128)(2,1)}, bf16[8,176,384]{2,1,0:T(8,128)(2,1)}) custom-call(bf16[1024,512]{1,0:T(8,128)(2,1)S(1)} %bitcast.30, bf16[384,1024]{1,0:T(8,128)(2,1)S(1)} %get-tuple-element.46.refs_1_, f32[8,1024]{1,0:T(8,128)S(1)} %get-tuple-element.47.refs_2_), custom_call_target="tpu_custom_call" | custom-call | tf_op jit(solution)/shard_map/pallas_call | solution.py:122
  76.7 3.6 %all-to-all-start.3 = ((bf16[8,176,384]{2,1,0:T(8,128)(2,1)}), bf16[8,176,384]{2,1,0:T(8,128)(2,1)S(1)}, u32[]{:S(2)}, u32[]{:S(2)}) async-start(bf16[8,176,384]{2,1,0:T(8,128)(2,1)} %get-tuple-element.49), calls=%async_computation.3 | async-start | bytes 2162688 | tf_op jit(solution)/shard_map/all_to_all | solution.py:336
  80.3 14.8 %all-to-all-done.3.refs_1_ = bf16[8,176,384]{2,1,0:T(8,128)(2,1)S(1)} async-done(((bf16[8,176,384]{2,1,0:T(8,128)(2,1)}), bf16[8,176,384]{2,1,0:T(8,128)(2,1)S(1)}, u32[]{:S(2)}, u32[]{:S(2)}) %all-to-all-start.3) | async-done | bytes 1081376 | tf_op jit(solution)/shard_map/all_to_all | solution.py:336
  95.1 1.7 shard_map.113
  96.8 6.3 %all-to-all-start.4 = ((bf16[8,16,384]{2,1,0:T(8,128)(2,1)}), bf16[8,16,384]{2,1,0:T(8,128)(2,1)S(1)}, u32[]{:S(2)}, u32[]{:S(2)}) async-start(bf16[8,16,384]{2,1,0:T(8,128)(2,1)} %bitcast.43), calls=%async_computation.4 | async-start | bytes 196608 | tf_op jit(solution)/shard_map/all_to_all | solution.py:336
  103.1 0.0 reduce-scatter.2.cloned.1.call-start
  103.1 11.0 %shard_map.114 = (bf16[1024,768]{1,0:T(8,128)(2,1)}, bf16[128,384]{1,0:T(8,128)(2,1)}, bf16[128,384]{1,0:T(8,128)(2,1)}, bf16[128,384]{1,0:T(8,128)(2,1)}, bf16[...) custom-call(s32[1]{0:T(128)} %bitcast.refs_0_, ...), custom_call_target="tpu_custom_call" | custom-call | tf_op jit(solution)/shard_map/pallas_call | solution.py:122
  114.1 0.0 all-to-all-done.4
  114.1 0.0 reduce-scatter.2.cloned.1.call-update
  114.2 0.1 broadcast_in_dim.2
  114.2 1.0 copy-done.3
  115.2 1.3 pad_maximum_fusion
  116.6 4.4 %all-to-all-start.5 = ((bf16[8,128,768]{2,1,0:T(8,128)(2,1)}), bf16[8,128,768]{2,1,0:T(8,128)(2,1)}, u32[]{:S(2)}, u32[]{:S(2)}) async-start(bf16[8,128,768]{2,1,0:T(8,128)(2,1)} %pad_maximum_fusion), calls=%async_computation.5 | async-start | bytes 3145728 | tf_op jit(solution)/shard_map/all_to_all | solution.py:336
  121.0 0.8 shard_map.115
  121.9 0.1 collective-permute-start.3
  122.0 1.7 collective-permute-done.3
  123.7 0.1 convert_add_fusion
  123.8 0.0 copy-start.10
  123.8 0.0 copy-start.9
  123.8 0.0 copy-start.4
  123.9 0.0 copy-start.8
  123.9 2.6 %collective-permute-start.4 = (bf16[128,768]{1,0:T(8,128)(2,1)S(1)}, bf16[128,768]{1,0:T(8,128)(2,1)S(1)}, u32[]{:S(2)}, u32[]{:S(2)}) collective-permute-start(bf16[128,768]{1,0:T(8,128)(2,1)S(1)} %fusion.2), channel_id=1, source_target_pairs={{0,128},{128,0},{1,129},{129,1},{2,130},{130,2},{3,131},{131,3},{4... | collective-permute-start | bytes 589832 | tf_op jit(solution)/shard_map/ppermute | solution.py:332
  126.4 15.7 %all-to-all-done.5.refs_0_ = bf16[8,128,768]{2,1,0:T(8,128)(2,1)} async-done(((bf16[8,128,768]{2,1,0:T(8,128)(2,1)}), bf16[8,128,768]{2,1,0:T(8,128)(2,1)}, u32[]{:S(2)}, u32[]{:S(2)}) %all-to-all-start.5) | async-done | bytes 1572896 | tf_op jit(solution)/shard_map/all_to_all | solution.py:336
  142.2 3.0 %shard_map.116 = bf16[384,384]{1,0:T(8,128)(2,1)} custom-call(bf16[8,128,768]{2,1,0:T(8,128)(2,1)} %all-to-all-done.5.refs_0_), custom_call_target="tpu_custom_call" | custom-call | tf_op jit(solution)/shard_map/pallas_call | solution.py:122
  145.1 0.4 collective-permute-start.11
  145.5 0.3 collective-permute-start.10
  145.8 7.2 %all-to-all-start.6 = ((bf16[8,48,384]{2,1,0:T(8,128)(2,1)}), bf16[8,48,384]{2,1,0:T(8,128)(2,1)S(1)}, u32[]{:S(2)}, u32[]{:S(2)}) async-start(bf16[8,48,384]{2,1,0:T(8,128)(2,1)} %bitcast.40), calls=%async_computation.7 | async-start | bytes 589824 | tf_op jit(solution)/shard_map/all_to_all | solution.py:336
  153.0 3.2 %collective-permute-start.9 = (bf16[128,384]{1,0:T(8,128)(2,1)S(1)}, bf16[128,384]{1,0:T(8,128)(2,1)S(1)}, u32[]{:S(2)}, u32[]{:S(2)}) collective-permute-start(bf16[128,384]{1,0:T(8,128)(2,1)S(1)} %copy-done.13), channel_id=1, source_target_pairs={{0,40},{8,48},{16,56},{24,0},{32,8},{40,16},{48,24},{56,32},{1,41}... | collective-permute-start | bytes 294920 | tf_op jit(solution)/shard_map/ppermute | solution.py:332
  156.2 1.7 collective-permute-start.8
  157.9 0.0 collective-permute-done.4
  157.9 0.2 collective-permute-start.7
  158.1 0.0 collective-permute-done.11
  158.1 1.5 collective-permute-start.6
  159.6 0.0 collective-permute-done.10
  159.6 1.7 collective-permute-start.5
  161.3 0.7 fusion.1
  162.0 0.0 collective-permute-done.9
  162.0 0.9 collective-permute-done.8
  162.9 2.1 %collective-permute-done.7 = bf16[128,384]{1,0:T(8,128)(2,1)S(1)} collective-permute-done((bf16[128,384]{1,0:T(8,128)(2,1)S(1)}, bf16[128,384]{1,0:T(8,128)(2,1)S(1)}, u32[]{:S(2)}, u32[]{:S(2)}) %collective-permute-start.7) | collective-permute-done | bytes 98336 | tf_op jit(solution)/shard_map/ppermute | solution.py:332
  165.0 0.0 collective-permute-done.6
  165.0 2.5 %collective-permute-done.5 = bf16[128,384]{1,0:T(8,128)(2,1)S(1)} collective-permute-done((bf16[128,384]{1,0:T(8,128)(2,1)S(1)}, bf16[128,384]{1,0:T(8,128)(2,1)S(1)}, u32[]{:S(2)}, u32[]{:S(2)}) %collective-permute-start.5) | collective-permute-done | bytes 98336 | tf_op jit(solution)/shard_map/ppermute | solution.py:332
  167.5 0.7 add_convert_fusion
  168.2 0.7 convert_reduce_fusion
  168.9 1.6 fusion.3
  (30 shorter events, 0.1 us)
Async XLA Ops:
  7.2 19.6 %copy-start.1 = (s32[128]{0:T(128)S(1)}, s32[128]{0:T(128)}, u32[]{:S(2)}) copy-start(s32[128]{0:T(128)} %param.13) | copy-start | bytes 1540
  7.2 50.3 %all-gather.2.cloned.1.call-start = ((), (), s32[]{:S(2)}) async-start(), calls=%async_computation.8 | async-start | bytes 1769472 | tf_op jit(solution)/shard_map/all_gather | solution.py:362
  8.9 8.4 %collective-permute-start = (bf16[128,768]{1,0:T(8,128)(2,1)}, bf16[128,768]{1,0:T(8,128)(2,1)S(1)}, u32[]{:S(2)}, u32[]{:S(2)}) collective-permute-start(bf16[128,768]{1,0:T(8,128)(2,1)} %refs_2_.1), channel_id=1, source_target_pairs={{0,128},{128,0},{1,129},{129,1},{2,130},{130,2},{3,131},{131,3},{4... | collective-permute-start | bytes 589832 | tf_op jit(solution)/shard_map/ppermute | solution.py:332
  12.2 5.2 %collective-permute-start.1 = (bf16[128,768]{1,0:T(8,128)(2,1)}, bf16[128,768]{1,0:T(8,128)(2,1)S(1)}, u32[]{:S(2)}, u32[]{:S(2)}) collective-permute-start(bf16[128,768]{1,0:T(8,128)(2,1)} %refs_2_.1), channel_id=1, source_target_pairs={{0,64},{64,0},{1,65},{65,1},{2,66},{66,2},{3,67},{67,3},{4,68},{68... | collective-permute-start | bytes 589832 | tf_op jit(solution)/shard_map/ppermute | solution.py:332
  17.3 8.7 %copy-start.5 = (bf16[128,768]{1,0:T(8,128)(2,1)}, bf16[128,768]{1,0:T(8,128)(2,1)S(1)}, u32[]{:S(2)}) copy-start(bf16[128,768]{1,0:T(8,128)(2,1)S(1)} %collective-permute-done.refs_3_) | copy-start | bytes 589828
  17.3 8.7 %copy-start.6 = (bf16[128,768]{1,0:T(8,128)(2,1)}, bf16[128,768]{1,0:T(8,128)(2,1)S(1)}, u32[]{:S(2)}) copy-start(bf16[128,768]{1,0:T(8,128)(2,1)S(1)} %collective-permute-done.1.refs_4_) | copy-start | bytes 589828
  19.3 16.8 %all-to-all-start = ((bf16[8,128,384]{2,1,0:T(8,128)(2,1)}), bf16[8,128,384]{2,1,0:T(8,128)(2,1)S(1)}, u32[]{:S(2)}, u32[]{:S(2)}) async-start(bf16[8,128,384]{2,1,0:T(8,128)(2,1)} %bitcast.5), calls=%async_computation | async-start | bytes 1572864 | tf_op jit(solution)/shard_map/all_to_all | solution.py:336
  24.6 1.4 collective-permute-start.2
  26.0 0.7 copy-start.7
  36.1 17.6 %copy-start.2 = (bf16[8,128,384]{2,1,0:T(8,128)(2,1)}, bf16[8,128,384]{2,1,0:T(8,128)(2,1)S(1)}, u32[]{:S(2)}) copy-start(bf16[8,128,384]{2,1,0:T(8,128)(2,1)S(1)} %all-to-all-done) | copy-start | bytes 2359300
  53.8 18.1 %all-to-all-start.2 = ((bf16[8,128,512]{2,1,0:T(8,128)(2,1)}), bf16[8,128,512]{2,1,0:T(8,128)(2,1)S(1)}, u32[]{:S(2)}, u32[]{:S(2)}) async-start(bf16[8,128,512]{2,1,0:T(8,128)(2,1)} %tile.21), calls=%async_computation.2 | async-start | bytes 2097152 | tf_op jit(solution)/shard_map/all_to_all | solution.py:336
  76.7 18.4 %all-to-all-start.3 = ((bf16[8,176,384]{2,1,0:T(8,128)(2,1)}), bf16[8,176,384]{2,1,0:T(8,128)(2,1)S(1)}, u32[]{:S(2)}, u32[]{:S(2)}) async-start(bf16[8,176,384]{2,1,0:T(8,128)(2,1)} %get-tuple-element.49), calls=%async_computation.3 | async-start | bytes 2162688 | tf_op jit(solution)/shard_map/all_to_all | solution.py:336
  96.8 17.4 %all-to-all-start.4 = ((bf16[8,16,384]{2,1,0:T(8,128)(2,1)}), bf16[8,16,384]{2,1,0:T(8,128)(2,1)S(1)}, u32[]{:S(2)}, u32[]{:S(2)}) async-start(bf16[8,16,384]{2,1,0:T(8,128)(2,1)} %bitcast.43), calls=%async_computation.4 | async-start | bytes 196608 | tf_op jit(solution)/shard_map/all_to_all | solution.py:336
  103.1 65.8 %reduce-scatter.2.cloned.1.call-start = ((), (), s32[]{:S(2)}) async-start(), calls=%async_computation.9 | async-start | bytes 1769472 | tf_op jit(solution)/shard_map/reduce_scatter | solution.py:421
  114.1 1.1 copy-start.3
  116.6 4.4 %copy-start = (bf16[384,3072]{1,0:T(8,128)(2,1)S(1)}, bf16[384,3072]{1,0:T(8,128)(2,1)}, u32[]{:S(2)}) copy-start(bf16[384,3072]{1,0:T(8,128)(2,1)} %refs_1_.1) | copy-start | bytes 7077892
  116.6 25.6 %all-to-all-start.5 = ((bf16[8,128,768]{2,1,0:T(8,128)(2,1)}), bf16[8,128,768]{2,1,0:T(8,128)(2,1)}, u32[]{:S(2)}, u32[]{:S(2)}) async-start(bf16[8,128,768]{2,1,0:T(8,128)(2,1)} %pad_maximum_fusion), calls=%async_computation.5 | async-start | bytes 3145728 | tf_op jit(solution)/shard_map/all_to_all | solution.py:336
  121.9 1.8 %collective-permute-start.3 = (bf16[2,128,768]{2,1,0:T(8,128)(2,1)S(1)}, bf16[2,128,768]{2,1,0:T(8,128)(2,1)S(1)}, u32[]{:S(2)}, u32[]{:S(2)}) collective-permute-start(bf16[2,128,768]{2,1,0:T(8,128)(2,1)S(1)} %dynamic-slice_bitcast_fusion), channel_id=1, source_target_pairs={{0,64},{64,0},{1,65},{65,1},{2,66},{66,2},{3,67},{67,3},{4,68},{68... | collective-permute-start | bytes 1179656 | tf_op jit(solution)/shard_map/ppermute | solution.py:332
  122.0 23.2 %copy-start.15 = (bf16[128,384]{1,0:T(8,128)(2,1)S(1)}, bf16[128,384]{1,0:T(8,128)(2,1)}, u32[]{:S(2)}) copy-start(bf16[128,384]{1,0:T(8,128)(2,1)} %get-tuple-element.72) | copy-start | bytes 294916
  122.0 23.5 %copy-start.14 = (bf16[128,384]{1,0:T(8,128)(2,1)S(1)}, bf16[128,384]{1,0:T(8,128)(2,1)}, u32[]{:S(2)}) copy-start(bf16[128,384]{1,0:T(8,128)(2,1)} %get-tuple-element.71) | copy-start | bytes 294916
  123.8 29.2 %copy-start.13 = (bf16[128,384]{1,0:T(8,128)(2,1)S(1)}, bf16[128,384]{1,0:T(8,128)(2,1)}, u32[]{:S(2)}) copy-start(bf16[128,384]{1,0:T(8,128)(2,1)} %get-tuple-element.70) | copy-start | bytes 294916
  123.8 32.4 %copy-start.12 = (bf16[128,384]{1,0:T(8,128)(2,1)S(1)}, bf16[128,384]{1,0:T(8,128)(2,1)}, u32[]{:S(2)}) copy-start(bf16[128,384]{1,0:T(8,128)(2,1)} %get-tuple-element.69) | copy-start | bytes 294916
  123.8 34.1 %copy-start.11 = (bf16[128,384]{1,0:T(8,128)(2,1)S(1)}, bf16[128,384]{1,0:T(8,128)(2,1)}, u32[]{:S(2)}) copy-start(bf16[128,384]{1,0:T(8,128)(2,1)} %get-tuple-element.68) | copy-start | bytes 294916
  123.8 34.3 %copy-start.10 = (bf16[128,384]{1,0:T(8,128)(2,1)S(1)}, bf16[128,384]{1,0:T(8,128)(2,1)}, u32[]{:S(2)}) copy-start(bf16[128,384]{1,0:T(8,128)(2,1)} %get-tuple-element.67) | copy-start | bytes 294916
  123.8 35.8 %copy-start.9 = (bf16[128,384]{1,0:T(8,128)(2,1)S(1)}, bf16[128,384]{1,0:T(8,128)(2,1)}, u32[]{:S(2)}) copy-start(bf16[128,384]{1,0:T(8,128)(2,1)} %get-tuple-element.66) | copy-start | bytes 294916
  123.8 37.4 %copy-start.4 = (bf16[128,768]{1,0:T(8,128)(2,1)S(1)}, bf16[128,768]{1,0:T(8,128)(2,1)}, u32[]{:S(2)}) copy-start(bf16[128,768]{1,0:T(8,128)(2,1)} %param.7) | copy-start | bytes 589828
  123.9 43.6 %copy-start.8 = (bf16[128,384]{1,0:T(8,128)(2,1)S(1)}, bf16[128,384]{1,0:T(8,128)(2,1)}, u32[]{:S(2)}) copy-start(bf16[128,384]{1,0:T(8,128)(2,1)} %get-tuple-element.65) | copy-start | bytes 294916
  123.9 34.0 %collective-permute-start.4 = (bf16[128,768]{1,0:T(8,128)(2,1)S(1)}, bf16[128,768]{1,0:T(8,128)(2,1)S(1)}, u32[]{:S(2)}, u32[]{:S(2)}) collective-permute-start(bf16[128,768]{1,0:T(8,128)(2,1)S(1)} %fusion.2), channel_id=1, source_target_pairs={{0,128},{128,0},{1,129},{129,1},{2,130},{130,2},{3,131},{131,3},{4... | collective-permute-start | bytes 589832 | tf_op jit(solution)/shard_map/ppermute | solution.py:332
  145.1 12.9 %collective-permute-start.11 = (bf16[128,384]{1,0:T(8,128)(2,1)S(1)}, bf16[128,384]{1,0:T(8,128)(2,1)S(1)}, u32[]{:S(2)}, u32[]{:S(2)}) collective-permute-start(bf16[128,384]{1,0:T(8,128)(2,1)S(1)} %copy-done.15), channel_id=1, source_target_pairs={{0,56},{8,0},{16,8},{24,16},{32,24},{40,32},{48,40},{56,48},{1,57}... | collective-permute-start | bytes 294920 | tf_op jit(solution)/shard_map/ppermute | solution.py:332
  145.5 14.1 %collective-permute-start.10 = (bf16[128,384]{1,0:T(8,128)(2,1)S(1)}, bf16[128,384]{1,0:T(8,128)(2,1)S(1)}, u32[]{:S(2)}, u32[]{:S(2)}) collective-permute-start(bf16[128,384]{1,0:T(8,128)(2,1)S(1)} %copy-done.14), channel_id=1, source_target_pairs={{0,48},{8,56},{16,0},{24,8},{32,16},{40,24},{48,32},{56,40},{1,49}... | collective-permute-start | bytes 294920 | tf_op jit(solution)/shard_map/ppermute | solution.py:332
  145.8 22.5 %all-to-all-start.6 = ((bf16[8,48,384]{2,1,0:T(8,128)(2,1)}), bf16[8,48,384]{2,1,0:T(8,128)(2,1)S(1)}, u32[]{:S(2)}, u32[]{:S(2)}) async-start(bf16[8,48,384]{2,1,0:T(8,128)(2,1)} %bitcast.40), calls=%async_computation.7 | async-start | bytes 589824 | tf_op jit(solution)/shard_map/all_to_all | solution.py:336
  153.0 9.0 %collective-permute-start.9 = (bf16[128,384]{1,0:T(8,128)(2,1)S(1)}, bf16[128,384]{1,0:T(8,128)(2,1)S(1)}, u32[]{:S(2)}, u32[]{:S(2)}) collective-permute-start(bf16[128,384]{1,0:T(8,128)(2,1)S(1)} %copy-done.13), channel_id=1, source_target_pairs={{0,40},{8,48},{16,56},{24,0},{32,8},{40,16},{48,24},{56,32},{1,41}... | collective-permute-start | bytes 294920 | tf_op jit(solution)/shard_map/ppermute | solution.py:332
  156.2 6.7 %collective-permute-start.8 = (bf16[128,384]{1,0:T(8,128)(2,1)S(1)}, bf16[128,384]{1,0:T(8,128)(2,1)S(1)}, u32[]{:S(2)}, u32[]{:S(2)}) collective-permute-start(bf16[128,384]{1,0:T(8,128)(2,1)S(1)} %copy-done.12), channel_id=1, source_target_pairs={{0,32},{8,40},{16,48},{24,56},{32,0},{40,8},{48,16},{56,24},{1,33}... | collective-permute-start | bytes 294920 | tf_op jit(solution)/shard_map/ppermute | solution.py:332
  157.9 7.1 %collective-permute-start.7 = (bf16[128,384]{1,0:T(8,128)(2,1)S(1)}, bf16[128,384]{1,0:T(8,128)(2,1)S(1)}, u32[]{:S(2)}, u32[]{:S(2)}) collective-permute-start(bf16[128,384]{1,0:T(8,128)(2,1)S(1)} %copy-done.11), channel_id=1, source_target_pairs={{0,24},{8,32},{16,40},{24,48},{32,56},{40,0},{48,8},{56,16},{1,25}... | collective-permute-start | bytes 294920 | tf_op jit(solution)/shard_map/ppermute | solution.py:332
  158.1 6.9 %collective-permute-start.6 = (bf16[128,384]{1,0:T(8,128)(2,1)S(1)}, bf16[128,384]{1,0:T(8,128)(2,1)S(1)}, u32[]{:S(2)}, u32[]{:S(2)}) collective-permute-start(bf16[128,384]{1,0:T(8,128)(2,1)S(1)} %copy-done.10), channel_id=1, source_target_pairs={{0,16},{8,24},{16,32},{24,40},{32,48},{40,56},{48,0},{56,8},{1,17}... | collective-permute-start | bytes 294920 | tf_op jit(solution)/shard_map/ppermute | solution.py:332
  159.6 7.9 %collective-permute-start.5 = (bf16[128,384]{1,0:T(8,128)(2,1)S(1)}, bf16[128,384]{1,0:T(8,128)(2,1)S(1)}, u32[]{:S(2)}, u32[]{:S(2)}) collective-permute-start(bf16[128,384]{1,0:T(8,128)(2,1)S(1)} %copy-done.9), channel_id=1, source_target_pairs={{0,8},{8,16},{16,24},{24,32},{32,40},{40,48},{48,56},{56,0},{1,9},... | collective-permute-start | bytes 294920 | tf_op jit(solution)/shard_map/ppermute | solution.py:332
Sparse Core Ops, SparseCore 0:
  9.8 43.1 all-gather.1
  114.3 38.1 reduce-scatter.1

commit v3 on v2

--- a/solution.py
+++ b/solution.py
@@ -15,6 +15,7 @@
 SIDE = 8
 TILE = TOK * SIDE
 QB = 256
+QF = 1024
 SCALE = 1.0 / math.sqrt(HD)
 LOG2E = math.log2(math.e)
 PEER = TOK // SIDE
@@ -180,7 +181,7 @@
 
 
 def project_body(
-    y_ref, core_ref, d0_ref, d1_ref, d2_ref, d3_ref, w_ref, row_ref, pay_ref, cut_ref
+    y_ref, core_ref, d0_ref, d1_ref, d2_ref, d3_ref, w_ref, row_ref, pay_ref
 ):
     y_pos, core = y_ref[0], core_ref[0]
     order, place = sorted_by_block(row_ref[...])
@@ -195,23 +196,40 @@
         part = 2 * along + across
         here = pl.ds(pl.multiple_of(part * SPAN, SPAN), SPAN)
         total += dot(d_ref[...], w_ref[:, here], NT)
-        rows = dot(order, d_ref[...]).astype(BF16)
-        cut_ref[2 * part] = rows[:, :COLS]
-        cut_ref[2 * part + 1] = rows[:, COLS:]
     pay_ref[:, :COLS] = dot(order, total.astype(BF16)).astype(BF16)
     pay_ref[:, COLS:] = dot(order, place.astype(BF16)).astype(BF16)
 
 
-def forward_body(ready, done, q_ref, kv_ref, out_ref, lse_ref):
+def cut_body(y_ref, core_ref, d0_ref, d1_ref, d2_ref, d3_ref, row_ref, cut_ref):
+    order, _ = sorted_by_block(row_ref[...])
+    y_pos, core = y_ref[0], core_ref[0]
+    pieces = (
+        (d0_ref, y_pos, core),
+        (d1_ref, 1 - y_pos, core),
+        (d2_ref, y_pos, 1 - core),
+        (d3_ref, 1 - y_pos, 1 - core),
+    )
+    for d_ref, along, across in pieces:
+        part = 2 * along + across
+        rows = dot(order, d_ref[...]).astype(BF16)
+        cut_ref[2 * part, :, COLS:] = rows[:, :COLS]
+        cut_ref[2 * part + 1, :, COLS:] = rows[:, COLS:]
+
+
+def forward_body(ready, done, quad_ref, kv_ref, *rest):
+    blocks, (q_ref, out_ref, lse_ref) = rest[:-3], rest[-3:]
+    for step, block_ref in enumerate(blocks):
+        q_ref[rows_of(around(quad_ref[0], -step)), :] = block_ref[...]
+    for idx in range(HEADS):
+        done(0, idx)
     lse_ref[...] = jnp.zeros_like(lse_ref)
     for idx in range(HEADS):
-        ready(0, idx)
         ready(1, idx)
         ready(1, HEADS + idx)
         keys = kv_ref[:, head(idx)]
         values_t = kv_ref[:, head(HEADS + idx)].T
-        for start in range(0, TILE, QB):
-            cols = slice(start, start + QB)
+        for start in range(0, TILE, QF):
+            cols = slice(start, start + QF)
             scores = dot(keys, q_ref[cols, head(idx)], NT)
             peak = jnp.max(scores, axis=0, keepdims=True)
             weights = jnp.exp2((scores - peak) * (SCALE * LOG2E))
@@ -328,6 +346,34 @@
     out_ref[...] = total.astype(BF16)
 
 
+def fill_spread(attended, spread):
+    def kernel(att_ref, _, out_ref, held, load_sem, sems):
+        load = pltpu.make_async_copy(att_ref, held, load_sem)
+        load.start()
+        load.wait()
+        copies = [
+            pltpu.make_async_copy(held, out_ref.at[peer, :, :COLS], sems.at[peer])
+            for peer in range(SIDE)
+        ]
+        for copy in copies:
+            copy.start()
+        for copy in copies:
+            copy.wait()
+
+    return pl.pallas_call(
+        kernel,
+        out_shape=pltpu.HBM(spread.shape, spread.dtype),
+        in_specs=[HBM, HBM],
+        out_specs=HBM,
+        input_output_aliases={1: 0},
+        scratch_shapes=[
+            pltpu.VMEM(attended.shape, attended.dtype),
+            pltpu.SemaphoreType.DMA,
+            pltpu.SemaphoreType.DMA((SIDE,)),
+        ],
+    )(*[pltpu.with_memory_space_constraint(arg, pltpu.HBM) for arg in (attended, spread)])
+
+
 def shift(value, axis, step, size):
     return lax.ppermute(value, axis, [(i, (i + step) % size) for i in range(size)])
 
@@ -362,13 +408,10 @@
     key_value = lax.all_gather(key_value, "z", axis=0, tiled=True)
     along = shift(d_mixed, "yh", 1, 2)
     across = shift(d_mixed, "co", 1, 2)
-    query = jnp.tile(ctrl_query, (SIDE, 1))
-    query, along, across = together(query, along, across)
-    query = exchange(query, QUAD)
     both = shift(along, "co", 1, 2)
-    payload, cuts = call(
+    (payload,) = call(
         project_body,
-        [far(((TOK, COLS + HD), BF16)), far(((SIDE, TOK, COLS), BF16))],
+        [far(((TOK, COLS + HD), BF16))],
         y_one,
         core_one,
         far(d_mixed),
@@ -379,15 +422,18 @@
         slot_row,
         mib=16,
     )
-    payload, query = together(payload, query)
+    payload, ctrl_query = together(payload, ctrl_query)
     payload = exchange(payload, "z")
+    query = scatter_quad([ctrl_query] * SIDE)
+    payload, *query = together(payload, *query)
     arrived = gather_quad(payload)
-    out_t, lse = call(
+    query, out_t, lse = call(
         forward_body,
-        [((COLS, TILE), BF16), ((SIDE, TILE), F32)],
-        far(query, HEADS),
+        [far(((TILE, COLS), BF16), HEADS), ((COLS, TILE), BF16), ((SIDE, TILE), F32)],
+        quad_one,
         far(key_value, 2 * HEADS),
-        mib=20,
+        *[far(block) for block in query],
+        mib=40,
     )
     grad, send = call(
         delta_body,
@@ -397,11 +443,23 @@
         lse,
         mib=24,
     )
+    stats = exchange(send, QUAD)
+    send, *pieces = together(send, d_mixed, along, across, both)
+    (spread,) = call(
+        cut_body,
+        [far(((SIDE, TOK, 2 * COLS), BF16))],
+        y_one,
+        core_one,
+        *[far(piece) for piece in pieces],
+        slot_row,
+        mib=16,
+    )
+    stats, spread = together(stats, spread)
     norms, attended = call(
         merge_body,
         [((SIDE, TILE), F32), far(((TOK, COLS), BF16))],
         quad_one,
-        exchange(send, QUAD),
+        stats,
         arrived,
         mib=16,
     )
@@ -419,9 +477,8 @@
     attended = exchange(attended, "z")
     d_key_value, attended = together(d_key_value, attended)
     d_key_value = lax.psum_scatter(d_key_value, "z", scatter_dimension=0, tiled=True)
-    spread = jnp.broadcast_to(attended[None], (SIDE, TOK, COLS))
-    spread = jnp.concatenate([spread, cuts], axis=2)
-    spread, attended = together(spread, attended)
+    spread = fill_spread(attended, spread)
+    spread, attended, *d_query[1:4] = together(spread, attended, *d_query[1:4])
     gathered = exchange(spread, QUAD)
     (partial_out,) = call(
         output_body,
@@ -436,9 +493,8 @@
     summed = pick(by_core, core, 1).astype(F32) + shift(
         pick(by_core, 1 - core, 1), "co", 1, 2
     ).astype(F32)
-    residual = pick(summed, y_pos, 0) + shift(
-        pick(summed, 1 - y_pos, 0).astype(BF16), "yh", 1, 2
-    ).astype(F32)
+    half = pick(summed, 1 - y_pos, 0).astype(BF16)
+    residual = pick(summed, y_pos, 0) + shift(half, "yh", 1, 2).astype(F32)
     main_mixed = (main_hidden.astype(F32) + residual).astype(BF16)
 
     (d_w_out,) = call(
@@ -447,15 +503,17 @@
         gathered,
         mib=16,
     )
-    d_w_out, *d_query = together(d_w_out, *d_query)
+    d_w_out, *d_query[4:] = together(d_w_out, *d_query[4:])
     d_query = sum(block.astype(F32) for block in scatter_quad(d_query))
     d_w_out = exchange(d_w_out, "z").reshape(SIDE, COLS // SIDE, COLS)
+    d_key, d_value = d_key_value[:, :COLS], d_key_value[:, COLS:]
+    d_w_out, d_key, d_value = together(d_w_out, d_key, d_value)
     d_w_out = jnp.sum(d_w_out.astype(F32), axis=0).T
     return (
         main_mixed,
         d_query.astype(BF16),
-        d_key_value[:, :COLS],
-        d_key_value[:, COLS:],
+        d_key,
+        d_value,
         d_w_out,
     )
 

time: 178 us -> 173 us (0.972)
  starting transfers between devices: 45.4 us -> 66.9 us
  blocking collectives: 16.6 us -> 0 us
  waiting for transfers between devices: 53.7 us -> 45.8 us
    all_to_all x1 -> x0, blocking collectives: 16.6 us -> none  [exchange(): return lax.all_to_all(value, axis, split_axis=0, concat_axis=0, tiled=True)]
    ppermute x12 -> x19, starting transfers between devices: 14.8 us -> 30.8 us  [shift(): lax.ppermute(value, axis, [(i, (i + step) % size) for i in range(size)])]
    all_to_all x6, waiting for transfers between devices: 39.9 us -> 30 us  [exchange(): return lax.all_to_all(value, axis, split_axis=0, concat_axis=0, tiled=True)]
    all_to_all x6, starting transfers between devices: 30.6 us -> 36.1 us  [exchange(): return lax.all_to_all(value, axis, split_axis=0, concat_axis=0, tiled=True)]
    ppermute x12 -> x19, waiting for transfers between devices: 13.8 us -> 15.8 us  [shift(): lax.ppermute(value, axis, [(i, (i + step) % size) for i in range(size)])]
    another operation x1 -> x0, local copies, waits for them, and re-layouts: 1.96 us -> none  [on_device(): query = jnp.tile(ctrl_query, (SIDE, 1))]
    pallas_call x0 -> x1, Pallas kernels: none -> 1.95 us  [fill_spread(): pl.pallas_call(kernel, out_shape=pltpu.HBM(spread.shape, spread.dtype), i...]
    pallas_call x7 -> x8, Pallas kernels: 35.7 us -> 34.8 us  [call(): pl.pallas_call(kernel, out_shape=[pltpu.HBM(*one) if out_parts[i] else ja...]
  transfers between devices with their start and end apart: 20 -> 27, of which waited for: 10 -> 12; matrix products, arithmetic and copies ran while one was open for 4% -> 3% of each run, Pallas kernels for 16% -> 18%
where the time goes in v3:
time: 173 us
  starting transfers between devices  66.9 us (39%)
  waiting for transfers between devices  45.8 us (26%)
  Pallas kernels  36.7 us (21%)
  between operations  14.4 us (8%)
  local copies, waits for them, and re-layouts  4.81 us (3%)
  other arithmetic  3.88 us (2%)
    all_to_all x6, starting transfers between devices, exchange(): return lax.all_to_all(value, axis, split_axis=0, concat_axis=0, tiled=True)  36.1 us
    pallas_call x8, Pallas kernels, call(): pl.pallas_call(kernel, out_shape=[pltpu.HBM(*one) if out_parts[i] else ja...  34.8 us
    ppermute x19, starting transfers between devices, shift(): lax.ppermute(value, axis, [(i, (i + step) % size) for i in range(size)])  30.8 us
    all_to_all x6, waiting for transfers between devices, exchange(): return lax.all_to_all(value, axis, split_axis=0, concat_axis=0, tiled=True)  30 us
    ppermute x19, waiting for transfers between devices, shift(): lax.ppermute(value, axis, [(i, (i + step) % size) for i in range(size)])  15.8 us
  transfers between devices with their start and end apart: 27, of which 12 were waited for; matrix products, arithmetic and copies ran while one was open for 3% of the time, Pallas kernels for 18%

profile of v3, /device:TPU:32, one launch (start us, length us, event | category | flops | bytes accessed | tf_op | source)
XLA Modules:
  0.0 172.5 jit_solution(221476888506382326)
XLA Ops:
  7.2 0.0 all-gather.2.cloned.1.call-start
  7.2 1.6 pad_maximum_fusion
  8.8 0.0 all-gather.2.cloned.1.call-update
  8.9 3.3 %collective-permute-start = (bf16[128,768]{1,0:T(8,128)(2,1)}, bf16[128,768]{1,0:T(8,128)(2,1)S(1)}, u32[]{:S(2)}, u32[]{:S(2)}) collective-permute-start(bf16[128,768]{1,0:T(8,128)(2,1)} %refs_2_.3), channel_id=1, source_target_pairs={{0,128},{128,0},{1,129},{129,1},{2,130},{130,2},{3,131},{131,3},{4... | collective-permute-start | bytes 589832 | tf_op jit(solution)/shard_map/ppermute | solution.py:378
  12.1 0.0 collective-permute-start.1
  12.2 5.2 %collective-permute-done.refs_3_ = bf16[128,768]{1,0:T(8,128)(2,1)S(1)} collective-permute-done((bf16[128,768]{1,0:T(8,128)(2,1)}, bf16[128,768]{1,0:T(8,128)(2,1)S(1)}, u32[]{:S(2)}, u32[]{:S(2)}) %collective-permute-start) | collective-permute-done | bytes 196640 | tf_op jit(solution)/shard_map/ppermute | solution.py:378
  17.3 1.4 collective-permute-done.2.refs_5_
  18.8 0.7 copy-done.7
  19.4 0.7 copy-done.3
  20.1 3.8 %shard_map.110 = bf16[128,512]{1,0:T(8,128)(2,1)} custom-call(s32[1]{0:T(128)} %bitcast.1.refs_0_, s32[1]{0:T(128)} %bitcast.2.refs_1_, bf16[128,768]{1,0:T(8,128)(2,1)} %refs_2_.3, bf16[128,768]{1,0:T(8,128)(2,1)} %copy-done.5, bf16[128,768]{1,0:T(8,128)(2,1)} %copy-done.6, bf16[128,768]{1,0:T(8,128)(2,1)} %copy-done.7, bf16[384,3072]{1,0:T(8,128)(2,1)} %refs_1_.1, ...), custom_call_target="tpu_custom_call" | custom-call | tf_op jit(solution)/shard_map/pallas_call | solution.py:123
  23.9 8.6 %all-to-all-start = ((bf16[8,16,512]{2,1,0:T(8,128)(2,1)}), bf16[8,16,512]{2,1,0:T(8,128)(2,1)S(1)}, u32[]{:S(2)}, u32[]{:S(2)}) async-start(bf16[8,16,512]{2,1,0:T(8,128)(2,1)} %bitcast.38), calls=%async_computation | async-start | bytes 262144 | tf_op jit(solution)/shard_map/all_to_all | solution.py:382
  32.5 1.6 collective-permute-start.3
  34.1 1.5 collective-permute-start.4
  35.6 2.0 %collective-permute-start.5 = (bf16[128,384]{1,0:T(8,128)(2,1)S(1)}, bf16[128,384]{1,0:T(8,128)(2,1)S(1)}, u32[]{:S(2)}, u32[]{:S(2)}) collective-permute-start(bf16[128,384]{1,0:T(8,128)(2,1)S(1)} %copy-done.9), channel_id=1, source_target_pairs={{0,24},{8,32},{16,40},{24,48},{32,56},{40,0},{48,8},{56,16},{1,25}... | collective-permute-start | bytes 294920 | tf_op jit(solution)/shard_map/ppermute | solution.py:378
  37.6 2.0 %collective-permute-start.6 = (bf16[128,384]{1,0:T(8,128)(2,1)S(1)}, bf16[128,384]{1,0:T(8,128)(2,1)S(1)}, u32[]{:S(2)}, u32[]{:S(2)}) collective-permute-start(bf16[128,384]{1,0:T(8,128)(2,1)S(1)} %copy-done.9), channel_id=1, source_target_pairs={{0,32},{8,40},{16,48},{24,56},{32,0},{40,8},{48,16},{56,24},{1,33}... | collective-permute-start | bytes 294920 | tf_op jit(solution)/shard_map/ppermute | solution.py:378
  39.6 3.1 %collective-permute-start.7 = (bf16[128,384]{1,0:T(8,128)(2,1)S(1)}, bf16[128,384]{1,0:T(8,128)(2,1)S(1)}, u32[]{:S(2)}, u32[]{:S(2)}) collective-permute-start(bf16[128,384]{1,0:T(8,128)(2,1)S(1)} %copy-done.9), channel_id=1, source_target_pairs={{0,40},{8,48},{16,56},{24,0},{32,8},{40,16},{48,24},{56,32},{1,41}... | collective-permute-start | bytes 294920 | tf_op jit(solution)/shard_map/ppermute | solution.py:378
  42.7 1.4 collective-permute-start.8
  44.2 1.1 collective-permute-done.5.refs_5_
  45.2 0.3 collective-permute-done.6.refs_6_
  45.5 1.4 collective-permute-done.7.refs_7_
  47.0 1.0 collective-permute-done.8.refs_8_
  47.9 0.8 collective-permute-done.9.refs_9_
  48.8 1.1 tile.2
  49.9 5.1 %all-to-all-start.1 = ((bf16[8,128,512]{2,1,0:T(8,128)(2,1)}), bf16[8,128,512]{2,1,0:T(8,128)(2,1)S(1)}, u32[]{:S(2)}, u32[]{:S(2)}) async-start(bf16[8,128,512]{2,1,0:T(8,128)(2,1)} %tile.2), calls=%async_computation.1 | async-start | bytes 2097152 | tf_op jit(solution)/shard_map/all_to_all | solution.py:382
  55.0 0.0 all-gather.2.cloned.1.call-done.refs_1_.refs_2_
  55.0 6.9 %shard_map.111 = (bf16[1024,384]{1,0:T(8,128)(2,1)}, bf16[384,1024]{1,0:T(8,128)(2,1)S(1)}, f32[8,1024]{1,0:T(8,128)S(1)}) custom-call(s32[1]{0:T(128)} %bitcast.refs_0_, bf16[1024,768]{1,0:T(8,128)(2,1)} %all-gather.2.cloned.1.call-done.refs_1_.refs_2_, bf16[128,384]{1,0:T(8,128)(2,1)} %refs_2_.2, bf16[128,384]{1,0:T(8,128)(2,1)} %copy-done.10, ...), custom_call_target="tpu_custom_call" | custom-call | tf_op jit(solution)/shard_map/pallas_call | solution.py:123
  61.9 7.1 %all-to-all-done.1 = bf16[8,128,512]{2,1,0:T(8,128)(2,1)S(1)} async-done(((bf16[8,128,512]{2,1,0:T(8,128)(2,1)}), bf16[8,128,512]{2,1,0:T(8,128)(2,1)S(1)}, u32[]{:S(2)}, u32[]{:S(2)}) %all-to-all-start.1) | async-done | bytes 1048608 | tf_op jit(solution)/shard_map/all_to_all | solution.py:382
  69.0 4.8 %shard_map.112 = (bf16[1024,384]{1,0:T(8,128)(2,1)}, bf16[8,176,384]{2,1,0:T(8,128)(2,1)}) custom-call(bf16[1024,512]{1,0:T(8,128)(2,1)S(1)} %bitcast.27, bf16[384,1024]{1,0:T(8,128)(2,1)S(1)} %get-tuple-element.65.refs_1_, f32[8,1024]{1,0:T(8,128)S(1)} %get-tuple-element.66.refs_2_), custom_call_target="tpu_custom_call" | custom-call | tf_op jit(solution)/shard_map/pallas_call | solution.py:123
  73.8 3.6 %all-to-all-start.2 = ((bf16[8,176,384]{2,1,0:T(8,128)(2,1)}), bf16[8,176,384]{2,1,0:T(8,128)(2,1)S(1)}, u32[]{:S(2)}, u32[]{:S(2)}) async-start(bf16[8,176,384]{2,1,0:T(8,128)(2,1)} %get-tuple-element.68), calls=%async_computation.2 | async-start | bytes 2162688 | tf_op jit(solution)/shard_map/all_to_all | solution.py:382
  77.4 2.9 %shard_map.113._ = bf16[8,128,768]{2,1,0:T(8,128)(2,1)} custom-call(s32[1]{0:T(128)} %bitcast.1.refs_0_, s32[1]{0:T(128)} %bitcast.2.refs_1_, bf16[128,768]{1,0:T(8,128)(2,1)} %refs_2_.3, bf16[128,768]{1,0:T(8,128)(2,1)} %copy-done.5, bf16[128,768]{1,0:T(8,128)(2,1)} %copy-done.6, bf16[128,768]{1,0:T(8,128)(2,1)} %copy-done.7, s32[1,128]{1,0:T(1,128)S(1)} %bitcast.34), custom_call_target="tpu_custom_call" | custom-call | tf_op jit(solution)/shard_map/pallas_call | solution.py:123
  80.3 11.9 %all-to-all-done.2.refs_1_ = bf16[8,176,384]{2,1,0:T(8,128)(2,1)S(1)} async-done(((bf16[8,176,384]{2,1,0:T(8,128)(2,1)}), bf16[8,176,384]{2,1,0:T(8,128)(2,1)S(1)}, u32[]{:S(2)}, u32[]{:S(2)}) %all-to-all-start.2) | async-done | bytes 1081376 | tf_op jit(solution)/shard_map/all_to_all | solution.py:382
  92.2 1.7 shard_map.114
  93.9 7.2 %all-to-all-start.3 = ((bf16[8,16,384]{2,1,0:T(8,128)(2,1)}), bf16[8,16,384]{2,1,0:T(8,128)(2,1)S(1)}, u32[]{:S(2)}, u32[]{:S(2)}) async-start(bf16[8,16,384]{2,1,0:T(8,128)(2,1)} %bitcast.39), calls=%async_computation.3 | async-start | bytes 196608 | tf_op jit(solution)/shard_map/all_to_all | solution.py:382
  101.1 11.0 %shard_map.115 = (bf16[1024,768]{1,0:T(8,128)(2,1)}, bf16[128,384]{1,0:T(8,128)(2,1)}, bf16[128,384]{1,0:T(8,128)(2,1)}, bf16[128,384]{1,0:T(8,128)(2,1)}, bf16[...) custom-call(s32[1]{0:T(128)} %bitcast.refs_0_, ...), custom_call_target="tpu_custom_call" | custom-call | tf_op jit(solution)/shard_map/pallas_call | solution.py:123
  112.1 0.0 copy-start.1
  112.2 0.0 reduce-scatter.2.cloned.1.call-update
  112.2 0.6 copy-done.1
  112.8 2.0 %shard_map.116 = bf16[8,128,768]{2,1,0:T(8,128)(2,1)} custom-call(bf16[128,384]{1,0:T(8,128)(2,1)} %bitcast.31, bf16[8,128,768]{2,1,0:T(8,128)(2,1)} %shard_map.113._), custom_call_target="tpu_custom_call", output_to_operand_aliasing={{}: (1, {})} | custom-call | tf_op jit(solution)/shard_map/pallas_call | solution.py:363
  114.8 0.0 copy-start
  114.8 0.0 copy-start.2
  114.8 4.4 %all-to-all-start.4 = ((bf16[8,128,768]{2,1,0:T(8,128)(2,1)}), bf16[8,128,768]{2,1,0:T(8,128)(2,1)}, u32[]{:S(2)}, u32[]{:S(2)}) async-start(bf16[8,128,768]{2,1,0:T(8,128)(2,1)} %shard_map.116), calls=%async_computation.4 | async-start | bytes 3145728 | tf_op jit(solution)/shard_map/all_to_all | solution.py:382
  119.2 0.8 shard_map.117
  120.1 0.0 copy-start.23
  120.1 0.0 copy-start.22
  120.1 0.1 collective-permute-start.10
  120.3 1.7 collective-permute-done.10
  122.0 0.1 convert_add_fusion
  122.1 0.0 copy-start.8
  122.1 3.3 %collective-permute-start.11 = (bf16[128,768]{1,0:T(8,128)(2,1)S(1)}, bf16[128,768]{1,0:T(8,128)(2,1)S(1)}, u32[]{:S(2)}, u32[]{:S(2)}) collective-permute-start(bf16[128,768]{1,0:T(8,128)(2,1)S(1)} %fusion.2), channel_id=1, source_target_pairs={{0,128},{128,0},{1,129},{129,1},{2,130},{130,2},{3,131},{131,3},{4... | collective-permute-start | bytes 589832 | tf_op jit(solution)/shard_map/ppermute | solution.py:378
  125.4 2.2 %collective-permute-start.14 = (bf16[128,384]{1,0:T(8,128)(2,1)S(1)}, bf16[128,384]{1,0:T(8,128)(2,1)S(1)}, u32[]{:S(2)}, u32[]{:S(2)}) collective-permute-start(bf16[128,384]{1,0:T(8,128)(2,1)S(1)} %copy-done.24), channel_id=1, source_target_pairs={{0,24},{8,32},{16,40},{24,48},{32,56},{40,0},{48,8},{56,16},{1,25}... | collective-permute-start | bytes 294920 | tf_op jit(solution)/shard_map/ppermute | solution.py:378
  127.6 1.5 collective-permute-start.13
  129.1 1.8 %collective-permute-start.12 = (bf16[128,384]{1,0:T(8,128)(2,1)S(1)}, bf16[128,384]{1,0:T(8,128)(2,1)S(1)}, u32[]{:S(2)}, u32[]{:S(2)}) collective-permute-start(bf16[128,384]{1,0:T(8,128)(2,1)S(1)} %copy-done.22), channel_id=1, source_target_pairs={{0,8},{8,16},{16,24},{24,32},{32,40},{40,48},{48,56},{56,0},{1,9},... | collective-permute-start | bytes 294920 | tf_op jit(solution)/shard_map/ppermute | solution.py:378
  130.9 11.0 %all-to-all-done.4.refs_0_ = bf16[8,128,768]{2,1,0:T(8,128)(2,1)} async-done(((bf16[8,128,768]{2,1,0:T(8,128)(2,1)}), bf16[8,128,768]{2,1,0:T(8,128)(2,1)}, u32[]{:S(2)}, u32[]{:S(2)}) %all-to-all-start.4) | async-done | bytes 1572896 | tf_op jit(solution)/shard_map/all_to_all | solution.py:382
  141.8 2.9 %shard_map.118 = bf16[384,384]{1,0:T(8,128)(2,1)} custom-call(bf16[8,128,768]{2,1,0:T(8,128)(2,1)} %all-to-all-done.4.refs_0_), custom_call_target="tpu_custom_call" | custom-call | tf_op jit(solution)/shard_map/pallas_call | solution.py:123
  144.8 0.8 collective-permute-start.18
  145.5 7.2 %all-to-all-start.5 = ((bf16[8,48,384]{2,1,0:T(8,128)(2,1)}), bf16[8,48,384]{2,1,0:T(8,128)(2,1)S(1)}, u32[]{:S(2)}, u32[]{:S(2)}) async-start(bf16[8,48,384]{2,1,0:T(8,128)(2,1)} %bitcast.36), calls=%async_computation.5 | async-start | bytes 589824 | tf_op jit(solution)/shard_map/all_to_all | solution.py:382
  152.7 1.3 collective-permute-start.17
  154.0 2.0 %collective-permute-start.16 = (bf16[128,384]{1,0:T(8,128)(2,1)S(1)}, bf16[128,384]{1,0:T(8,128)(2,1)S(1)}, u32[]{:S(2)}, u32[]{:S(2)}) collective-permute-start(bf16[128,384]{1,0:T(8,128)(2,1)S(1)} %copy-done.19), channel_id=1, source_target_pairs={{0,40},{8,48},{16,56},{24,0},{32,8},{40,16},{48,24},{56,32},{1,41}... | collective-permute-start | bytes 294920 | tf_op jit(solution)/shard_map/ppermute | solution.py:378
  156.0 2.9 %collective-permute-start.15 = (bf16[128,384]{1,0:T(8,128)(2,1)S(1)}, bf16[128,384]{1,0:T(8,128)(2,1)S(1)}, u32[]{:S(2)}, u32[]{:S(2)}) collective-permute-start(bf16[128,384]{1,0:T(8,128)(2,1)S(1)} %copy-done.18), channel_id=1, source_target_pairs={{0,32},{8,40},{16,48},{24,56},{32,0},{40,8},{48,16},{56,24},{1,33}... | collective-permute-start | bytes 294920 | tf_op jit(solution)/shard_map/ppermute | solution.py:378
  159.0 0.7 fusion.1
  159.7 2.9 %collective-permute-done.15 = bf16[128,384]{1,0:T(8,128)(2,1)S(1)} collective-permute-done((bf16[128,384]{1,0:T(8,128)(2,1)S(1)}, bf16[128,384]{1,0:T(8,128)(2,1)S(1)}, u32[]{:S(2)}, u32[]{:S(2)}) %collective-permute-start.15) | collective-permute-done | bytes 98336 | tf_op jit(solution)/shard_map/ppermute | solution.py:378
  162.6 0.7 add_convert_fusion
  163.4 1.6 fusion.3
  165.0 0.7 convert_reduce_fusion
  (60 shorter events, 0.2 us)
Async XLA Ops:
  7.2 47.8 %all-gather.2.cloned.1.call-start = ((), (), s32[]{:S(2)}) async-start(), calls=%async_computation.7 | async-start | bytes 1769472 | tf_op jit(solution)/shard_map/all_gather | solution.py:408
  8.9 8.4 %collective-permute-start = (bf16[128,768]{1,0:T(8,128)(2,1)}, bf16[128,768]{1,0:T(8,128)(2,1)S(1)}, u32[]{:S(2)}, u32[]{:S(2)}) collective-permute-start(bf16[128,768]{1,0:T(8,128)(2,1)} %refs_2_.3), channel_id=1, source_target_pairs={{0,128},{128,0},{1,129},{129,1},{2,130},{130,2},{3,131},{131,3},{4... | collective-permute-start | bytes 589832 | tf_op jit(solution)/shard_map/ppermute | solution.py:378
  12.1 5.2 %collective-permute-start.1 = (bf16[128,768]{1,0:T(8,128)(2,1)}, bf16[128,768]{1,0:T(8,128)(2,1)S(1)}, u32[]{:S(2)}, u32[]{:S(2)}) collective-permute-start(bf16[128,768]{1,0:T(8,128)(2,1)} %refs_2_.3), channel_id=1, source_target_pairs={{0,64},{64,0},{1,65},{65,1},{2,66},{66,2},{3,67},{67,3},{4,68},{68... | collective-permute-start | bytes 589832 | tf_op jit(solution)/shard_map/ppermute | solution.py:378
  17.3 1.4 copy-start.5
  17.3 1.4 collective-permute-start.2
  17.3 1.4 copy-start.6
  18.8 0.7 copy-start.7
  19.4 0.7 copy-start.3
  20.1 12.4 %copy-start.9 = (bf16[128,384]{1,0:T(8,128)(2,1)S(1)}, bf16[128,384]{1,0:T(8,128)(2,1)}, u32[]{:S(2)}) copy-start(bf16[128,384]{1,0:T(8,128)(2,1)} %refs_2_.2) | copy-start | bytes 294916
  23.9 24.9 %all-to-all-start = ((bf16[8,16,512]{2,1,0:T(8,128)(2,1)}), bf16[8,16,512]{2,1,0:T(8,128)(2,1)S(1)}, u32[]{:S(2)}, u32[]{:S(2)}) async-start(bf16[8,16,512]{2,1,0:T(8,128)(2,1)} %bitcast.38), calls=%async_computation | async-start | bytes 262144 | tf_op jit(solution)/shard_map/all_to_all | solution.py:382
  32.5 10.2 %collective-permute-start.3 = (bf16[128,384]{1,0:T(8,128)(2,1)S(1)}, bf16[128,384]{1,0:T(8,128)(2,1)S(1)}, u32[]{:S(2)}, u32[]{:S(2)}) collective-permute-start(bf16[128,384]{1,0:T(8,128)(2,1)S(1)} %copy-done.9), channel_id=1, source_target_pairs={{0,8},{8,16},{16,24},{24,32},{32,40},{40,48},{48,56},{56,0},{1,9},... | collective-permute-start | bytes 294920 | tf_op jit(solution)/shard_map/ppermute | solution.py:378
  34.1 10.1 %collective-permute-start.4 = (bf16[128,384]{1,0:T(8,128)(2,1)S(1)}, bf16[128,384]{1,0:T(8,128)(2,1)S(1)}, u32[]{:S(2)}, u32[]{:S(2)}) collective-permute-start(bf16[128,384]{1,0:T(8,128)(2,1)S(1)} %copy-done.9), channel_id=1, source_target_pairs={{0,16},{8,24},{16,32},{24,40},{32,48},{40,56},{48,0},{56,8},{1,17}... | collective-permute-start | bytes 294920 | tf_op jit(solution)/shard_map/ppermute | solution.py:378
  35.6 9.7 %collective-permute-start.5 = (bf16[128,384]{1,0:T(8,128)(2,1)S(1)}, bf16[128,384]{1,0:T(8,128)(2,1)S(1)}, u32[]{:S(2)}, u32[]{:S(2)}) collective-permute-start(bf16[128,384]{1,0:T(8,128)(2,1)S(1)} %copy-done.9), channel_id=1, source_target_pairs={{0,24},{8,32},{16,40},{24,48},{32,56},{40,0},{48,8},{56,16},{1,25}... | collective-permute-start | bytes 294920 | tf_op jit(solution)/shard_map/ppermute | solution.py:378
  37.6 8.0 %collective-permute-start.6 = (bf16[128,384]{1,0:T(8,128)(2,1)S(1)}, bf16[128,384]{1,0:T(8,128)(2,1)S(1)}, u32[]{:S(2)}, u32[]{:S(2)}) collective-permute-start(bf16[128,384]{1,0:T(8,128)(2,1)S(1)} %copy-done.9), channel_id=1, source_target_pairs={{0,32},{8,40},{16,48},{24,56},{32,0},{40,8},{48,16},{56,24},{1,33}... | collective-permute-start | bytes 294920 | tf_op jit(solution)/shard_map/ppermute | solution.py:378
  39.6 7.4 %collective-permute-start.7 = (bf16[128,384]{1,0:T(8,128)(2,1)S(1)}, bf16[128,384]{1,0:T(8,128)(2,1)S(1)}, u32[]{:S(2)}, u32[]{:S(2)}) collective-permute-start(bf16[128,384]{1,0:T(8,128)(2,1)S(1)} %copy-done.9), channel_id=1, source_target_pairs={{0,40},{8,48},{16,56},{24,0},{32,8},{40,16},{48,24},{56,32},{1,41}... | collective-permute-start | bytes 294920 | tf_op jit(solution)/shard_map/ppermute | solution.py:378
  42.7 7.1 %copy-start.10 = (bf16[128,384]{1,0:T(8,128)(2,1)}, bf16[128,384]{1,0:T(8,128)(2,1)S(1)}, u32[]{:S(2)}) copy-start(bf16[128,384]{1,0:T(8,128)(2,1)S(1)} %collective-permute-done.3.refs_3_) | copy-start | bytes 294916
  42.7 5.2 %collective-permute-start.8 = (bf16[128,384]{1,0:T(8,128)(2,1)S(1)}, bf16[128,384]{1,0:T(8,128)(2,1)S(1)}, u32[]{:S(2)}, u32[]{:S(2)}) collective-permute-start(bf16[128,384]{1,0:T(8,128)(2,1)S(1)} %copy-done.9), channel_id=1, source_target_pairs={{0,48},{8,56},{16,0},{24,8},{32,16},{40,24},{48,32},{56,40},{1,49}... | collective-permute-start | bytes 294920 | tf_op jit(solution)/shard_map/ppermute | solution.py:378
  44.2 5.7 %copy-start.11 = (bf16[128,384]{1,0:T(8,128)(2,1)}, bf16[128,384]{1,0:T(8,128)(2,1)S(1)}, u32[]{:S(2)}) copy-start(bf16[128,384]{1,0:T(8,128)(2,1)S(1)} %collective-permute-done.4.refs_4_) | copy-start | bytes 294916
  44.2 4.6 %collective-permute-start.9 = (bf16[128,384]{1,0:T(8,128)(2,1)S(1)}, bf16[128,384]{1,0:T(8,128)(2,1)S(1)}, u32[]{:S(2)}, u32[]{:S(2)}) collective-permute-start(bf16[128,384]{1,0:T(8,128)(2,1)S(1)} %copy-done.9), channel_id=1, source_target_pairs={{0,56},{8,0},{16,8},{24,16},{32,24},{40,32},{48,40},{56,48},{1,57}... | collective-permute-start | bytes 294920 | tf_op jit(solution)/shard_map/ppermute | solution.py:378
  45.2 4.6 %copy-start.12 = (bf16[128,384]{1,0:T(8,128)(2,1)}, bf16[128,384]{1,0:T(8,128)(2,1)S(1)}, u32[]{:S(2)}) copy-start(bf16[128,384]{1,0:T(8,128)(2,1)S(1)} %collective-permute-done.5.refs_5_) | copy-start | bytes 294916
  45.5 4.3 %copy-start.13 = (bf16[128,384]{1,0:T(8,128)(2,1)}, bf16[128,384]{1,0:T(8,128)(2,1)S(1)}, u32[]{:S(2)}) copy-start(bf16[128,384]{1,0:T(8,128)(2,1)S(1)} %collective-permute-done.6.refs_6_) | copy-start | bytes 294916
  47.0 2.9 %copy-start.14 = (bf16[128,384]{1,0:T(8,128)(2,1)}, bf16[128,384]{1,0:T(8,128)(2,1)S(1)}, u32[]{:S(2)}) copy-start(bf16[128,384]{1,0:T(8,128)(2,1)S(1)} %collective-permute-done.7.refs_7_) | copy-start | bytes 294916
  47.9 2.0 %copy-start.15 = (bf16[128,384]{1,0:T(8,128)(2,1)}, bf16[128,384]{1,0:T(8,128)(2,1)S(1)}, u32[]{:S(2)}) copy-start(bf16[128,384]{1,0:T(8,128)(2,1)S(1)} %collective-permute-done.8.refs_8_) | copy-start | bytes 294916
  48.8 1.1 copy-start.16
  49.9 19.1 %all-to-all-start.1 = ((bf16[8,128,512]{2,1,0:T(8,128)(2,1)}), bf16[8,128,512]{2,1,0:T(8,128)(2,1)S(1)}, u32[]{:S(2)}, u32[]{:S(2)}) async-start(bf16[8,128,512]{2,1,0:T(8,128)(2,1)} %tile.2), calls=%async_computation.1 | async-start | bytes 2097152 | tf_op jit(solution)/shard_map/all_to_all | solution.py:382
  69.0 8.4 %copy-start.4 = (s32[128]{0:T(128)S(1)}, s32[128]{0:T(128)}, u32[]{:S(2)}) copy-start(s32[128]{0:T(128)} %param.13) | copy-start | bytes 1540
  73.8 18.4 %all-to-all-start.2 = ((bf16[8,176,384]{2,1,0:T(8,128)(2,1)}), bf16[8,176,384]{2,1,0:T(8,128)(2,1)S(1)}, u32[]{:S(2)}, u32[]{:S(2)}) async-start(bf16[8,176,384]{2,1,0:T(8,128)(2,1)} %get-tuple-element.68), calls=%async_computation.2 | async-start | bytes 2162688 | tf_op jit(solution)/shard_map/all_to_all | solution.py:382
  93.9 18.2 %all-to-all-start.3 = ((bf16[8,16,384]{2,1,0:T(8,128)(2,1)}), bf16[8,16,384]{2,1,0:T(8,128)(2,1)S(1)}, u32[]{:S(2)}, u32[]{:S(2)}) async-start(bf16[8,16,384]{2,1,0:T(8,128)(2,1)} %bitcast.39), calls=%async_computation.3 | async-start | bytes 196608 | tf_op jit(solution)/shard_map/all_to_all | solution.py:382
  101.1 62.2 %reduce-scatter.2.cloned.1.call-start = ((), (), s32[]{:S(2)}) async-start(), calls=%async_computation.8 | async-start | bytes 1769472 | tf_op jit(solution)/shard_map/reduce_scatter | solution.py:479
  112.1 0.6 copy-start.1
  114.8 4.5 %copy-start = (bf16[384,3072]{1,0:T(8,128)(2,1)S(1)}, bf16[384,3072]{1,0:T(8,128)(2,1)}, u32[]{:S(2)}) copy-start(bf16[384,3072]{1,0:T(8,128)(2,1)} %refs_1_.1) | copy-start | bytes 7077892
  114.8 4.5 %copy-start.2 = (bf16[8,16,384]{2,1,0:T(8,128)(2,1)S(1)}, bf16[8,16,384]{2,1,0:T(8,128)(2,1)}, u32[]{:S(2)}) copy-start(bf16[8,16,384]{2,1,0:T(8,128)(2,1)} %copy-done.1) | copy-start | bytes 294916
  114.8 27.0 %all-to-all-start.4 = ((bf16[8,128,768]{2,1,0:T(8,128)(2,1)}), bf16[8,128,768]{2,1,0:T(8,128)(2,1)}, u32[]{:S(2)}, u32[]{:S(2)}) async-start(bf16[8,128,768]{2,1,0:T(8,128)(2,1)} %shard_map.116), calls=%async_computation.4 | async-start | bytes 3145728 | tf_op jit(solution)/shard_map/all_to_all | solution.py:382
  120.1 5.3 %copy-start.24 = (bf16[128,384]{1,0:T(8,128)(2,1)S(1)}, bf16[128,384]{1,0:T(8,128)(2,1)}, u32[]{:S(2)}) copy-start(bf16[128,384]{1,0:T(8,128)(2,1)} %get-tuple-element.86) | copy-start | bytes 294916
  120.1 7.5 %copy-start.23 = (bf16[128,384]{1,0:T(8,128)(2,1)S(1)}, bf16[128,384]{1,0:T(8,128)(2,1)}, u32[]{:S(2)}) copy-start(bf16[128,384]{1,0:T(8,128)(2,1)} %get-tuple-element.85) | copy-start | bytes 294916
  120.1 9.0 %copy-start.22 = (bf16[128,384]{1,0:T(8,128)(2,1)S(1)}, bf16[128,384]{1,0:T(8,128)(2,1)}, u32[]{:S(2)}) copy-start(bf16[128,384]{1,0:T(8,128)(2,1)} %get-tuple-element.84) | copy-start | bytes 294916
  120.1 1.8 %collective-permute-start.10 = (bf16[2,128,768]{2,1,0:T(8,128)(2,1)S(1)}, bf16[2,128,768]{2,1,0:T(8,128)(2,1)S(1)}, u32[]{:S(2)}, u32[]{:S(2)}) collective-permute-start(bf16[2,128,768]{2,1,0:T(8,128)(2,1)S(1)} %dynamic-slice_bitcast_fusion), channel_id=1, source_target_pairs={{0,64},{64,0},{1,65},{65,1},{2,66},{66,2},{3,67},{67,3},{4,68},{68... | collective-permute-start | bytes 1179656 | tf_op jit(solution)/shard_map/ppermute | solution.py:378
  120.2 24.5 %copy-start.21 = (bf16[128,384]{1,0:T(8,128)(2,1)S(1)}, bf16[128,384]{1,0:T(8,128)(2,1)}, u32[]{:S(2)}) copy-start(bf16[128,384]{1,0:T(8,128)(2,1)} %get-tuple-element.95) | copy-start | bytes 294916
  122.0 30.7 %copy-start.20 = (bf16[128,384]{1,0:T(8,128)(2,1)S(1)}, bf16[128,384]{1,0:T(8,128)(2,1)}, u32[]{:S(2)}) copy-start(bf16[128,384]{1,0:T(8,128)(2,1)} %get-tuple-element.94) | copy-start | bytes 294916
  122.1 31.9 %copy-start.19 = (bf16[128,384]{1,0:T(8,128)(2,1)S(1)}, bf16[128,384]{1,0:T(8,128)(2,1)}, u32[]{:S(2)}) copy-start(bf16[128,384]{1,0:T(8,128)(2,1)} %get-tuple-element.93) | copy-start | bytes 294916
  122.1 34.0 %copy-start.18 = (bf16[128,384]{1,0:T(8,128)(2,1)S(1)}, bf16[128,384]{1,0:T(8,128)(2,1)}, u32[]{:S(2)}) copy-start(bf16[128,384]{1,0:T(8,128)(2,1)} %get-tuple-element.92) | copy-start | bytes 294916
  122.1 36.9 %copy-start.8 = (bf16[128,768]{1,0:T(8,128)(2,1)S(1)}, bf16[128,768]{1,0:T(8,128)(2,1)}, u32[]{:S(2)}) copy-start(bf16[128,768]{1,0:T(8,128)(2,1)} %param.7) | copy-start | bytes 589828
  122.1 33.9 %collective-permute-start.11 = (bf16[128,768]{1,0:T(8,128)(2,1)S(1)}, bf16[128,768]{1,0:T(8,128)(2,1)S(1)}, u32[]{:S(2)}, u32[]{:S(2)}) collective-permute-start(bf16[128,768]{1,0:T(8,128)(2,1)S(1)} %fusion.2), channel_id=1, source_target_pairs={{0,128},{128,0},{1,129},{129,1},{2,130},{130,2},{3,131},{131,3},{4... | collective-permute-start | bytes 589832 | tf_op jit(solution)/shard_map/ppermute | solution.py:378
  125.4 27.3 %collective-permute-start.14 = (bf16[128,384]{1,0:T(8,128)(2,1)S(1)}, bf16[128,384]{1,0:T(8,128)(2,1)S(1)}, u32[]{:S(2)}, u32[]{:S(2)}) collective-permute-start(bf16[128,384]{1,0:T(8,128)(2,1)S(1)} %copy-done.24), channel_id=1, source_target_pairs={{0,24},{8,32},{16,40},{24,48},{32,56},{40,0},{48,8},{56,16},{1,25}... | collective-permute-start | bytes 294920 | tf_op jit(solution)/shard_map/ppermute | solution.py:378
  127.6 26.4 %collective-permute-start.13 = (bf16[128,384]{1,0:T(8,128)(2,1)S(1)}, bf16[128,384]{1,0:T(8,128)(2,1)S(1)}, u32[]{:S(2)}, u32[]{:S(2)}) collective-permute-start(bf16[128,384]{1,0:T(8,128)(2,1)S(1)} %copy-done.23), channel_id=1, source_target_pairs={{0,16},{8,24},{16,32},{24,40},{32,48},{40,56},{48,0},{56,8},{1,17}... | collective-permute-start | bytes 294920 | tf_op jit(solution)/shard_map/ppermute | solution.py:378
  129.1 33.5 %copy-start.17 = (bf16[128,384]{1,0:T(8,128)(2,1)S(1)}, bf16[128,384]{1,0:T(8,128)(2,1)}, u32[]{:S(2)}) copy-start(bf16[128,384]{1,0:T(8,128)(2,1)} %get-tuple-element.83) | copy-start | bytes 294916
  129.1 30.6 %collective-permute-start.12 = (bf16[128,384]{1,0:T(8,128)(2,1)S(1)}, bf16[128,384]{1,0:T(8,128)(2,1)S(1)}, u32[]{:S(2)}, u32[]{:S(2)}) collective-permute-start(bf16[128,384]{1,0:T(8,128)(2,1)S(1)} %copy-done.22), channel_id=1, source_target_pairs={{0,8},{8,16},{16,24},{24,32},{32,40},{40,48},{48,56},{56,0},{1,9},... | collective-permute-start | bytes 294920 | tf_op jit(solution)/shard_map/ppermute | solution.py:378
  144.8 15.0 %collective-permute-start.18 = (bf16[128,384]{1,0:T(8,128)(2,1)S(1)}, bf16[128,384]{1,0:T(8,128)(2,1)S(1)}, u32[]{:S(2)}, u32[]{:S(2)}) collective-permute-start(bf16[128,384]{1,0:T(8,128)(2,1)S(1)} %copy-done.21), channel_id=1, source_target_pairs={{0,56},{8,0},{16,8},{24,16},{32,24},{40,32},{48,40},{56,48},{1,57}... | collective-permute-start | bytes 294920 | tf_op jit(solution)/shard_map/ppermute | solution.py:378
  145.5 19.5 %all-to-all-start.5 = ((bf16[8,48,384]{2,1,0:T(8,128)(2,1)}), bf16[8,48,384]{2,1,0:T(8,128)(2,1)S(1)}, u32[]{:S(2)}, u32[]{:S(2)}) async-start(bf16[8,48,384]{2,1,0:T(8,128)(2,1)} %bitcast.36), calls=%async_computation.5 | async-start | bytes 589824 | tf_op jit(solution)/shard_map/all_to_all | solution.py:382
  152.7 7.0 %collective-permute-start.17 = (bf16[128,384]{1,0:T(8,128)(2,1)S(1)}, bf16[128,384]{1,0:T(8,128)(2,1)S(1)}, u32[]{:S(2)}, u32[]{:S(2)}) collective-permute-start(bf16[128,384]{1,0:T(8,128)(2,1)S(1)} %copy-done.20), channel_id=1, source_target_pairs={{0,48},{8,56},{16,0},{24,8},{32,16},{40,24},{48,32},{56,40},{1,49}... | collective-permute-start | bytes 294920 | tf_op jit(solution)/shard_map/ppermute | solution.py:378
  154.0 5.7 %collective-permute-start.16 = (bf16[128,384]{1,0:T(8,128)(2,1)S(1)}, bf16[128,384]{1,0:T(8,128)(2,1)S(1)}, u32[]{:S(2)}, u32[]{:S(2)}) collective-permute-start(bf16[128,384]{1,0:T(8,128)(2,1)S(1)} %copy-done.19), channel_id=1, source_target_pairs={{0,40},{8,48},{16,56},{24,0},{32,8},{40,16},{48,24},{56,32},{1,41}... | collective-permute-start | bytes 294920 | tf_op jit(solution)/shard_map/ppermute | solution.py:378
  156.0 6.6 %collective-permute-start.15 = (bf16[128,384]{1,0:T(8,128)(2,1)S(1)}, bf16[128,384]{1,0:T(8,128)(2,1)S(1)}, u32[]{:S(2)}, u32[]{:S(2)}) collective-permute-start(bf16[128,384]{1,0:T(8,128)(2,1)S(1)} %copy-done.18), channel_id=1, source_target_pairs={{0,32},{8,40},{16,48},{24,56},{32,0},{40,8},{48,16},{56,24},{1,33}... | collective-permute-start | bytes 294920 | tf_op jit(solution)/shard_map/ppermute | solution.py:378
Sparse Core Ops, SparseCore 0:
  9.8 43.6 all-gather.1
  112.3 38.8 reduce-scatter.1

commit v4 on v3

--- a/solution.py
+++ b/solution.py
@@ -326,10 +326,14 @@
             d_values += dot(weights.astype(BF16), grad)
             d_keys += dot(d_scores, query)
             dq_ref[cols, head(idx)] = (dot(keys_t, d_scores) * SCALE).T.astype(BF16)
-        dkv_ref[:, head(idx)] = (d_keys * SCALE).astype(BF16)
-        dkv_ref[:, head(HEADS + idx)] = d_values.astype(BF16)
+        d_keys = (d_keys * SCALE).astype(BF16)
+        d_values = d_values.astype(BF16)
+        for peer in range(SIDE):
+            rows = slice(peer * TOK, (peer + 1) * TOK)
+            first = 2 * peer * TOK
+            dkv_ref[first : first + TOK, head(idx)] = d_keys[rows]
+            dkv_ref[first + TOK : first + 2 * TOK, head(idx)] = d_values[rows]
         done(0, idx)
-        done(0, HEADS + idx)
 
 
 def output_body(sorted_ref, w_ref, row_ref, part_ref):
@@ -340,17 +344,13 @@
 
 
 def weight_body(both_ref, out_ref):
-    total = jnp.zeros((COLS, COLS), F32)
-    for peer in range(SIDE):
-        total += dot(both_ref[peer, :, COLS:], both_ref[peer, :, :COLS], TN)
+    both = both_ref[...].reshape(TILE, 2 * COLS)
+    total = dot(both[:, COLS:], both[:, :COLS], TN)
     out_ref[...] = total.astype(BF16)
 
 
 def fill_spread(attended, spread):
-    def kernel(att_ref, _, out_ref, held, load_sem, sems):
-        load = pltpu.make_async_copy(att_ref, held, load_sem)
-        load.start()
-        load.wait()
+    def kernel(held, _, out_ref, sems):
         copies = [
             pltpu.make_async_copy(held, out_ref.at[peer, :, :COLS], sems.at[peer])
             for peer in range(SIDE)
@@ -363,15 +363,11 @@
     return pl.pallas_call(
         kernel,
         out_shape=pltpu.HBM(spread.shape, spread.dtype),
-        in_specs=[HBM, HBM],
+        in_specs=[VMEM, HBM],
         out_specs=HBM,
         input_output_aliases={1: 0},
-        scratch_shapes=[
-            pltpu.VMEM(attended.shape, attended.dtype),
-            pltpu.SemaphoreType.DMA,
-            pltpu.SemaphoreType.DMA((SIDE,)),
-        ],
-    )(*[pltpu.with_memory_space_constraint(arg, pltpu.HBM) for arg in (attended, spread)])
+        scratch_shapes=[pltpu.SemaphoreType.DMA((SIDE,))],
+    )(attended, pltpu.with_memory_space_constraint(spread, pltpu.HBM))
 
 
 def shift(value, axis, step, size):
@@ -380,10 +376,6 @@
 
 def exchange(value, axis):
     return lax.all_to_all(value, axis, split_axis=0, concat_axis=0, tiled=True)
-
-
-def gather_quad(value):
-    return exchange(jnp.tile(value, (SIDE, 1)), QUAD)
 
 
 def scatter_quad(blocks):
@@ -415,9 +407,9 @@
         y_one,
         core_one,
         far(d_mixed),
-        far(along),
-        far(across),
-        far(both),
+        along,
+        across,
+        both,
         far(w_out),
         slot_row,
         mib=16,
@@ -425,8 +417,8 @@
     payload, ctrl_query = together(payload, ctrl_query)
     payload = exchange(payload, "z")
     query = scatter_quad([ctrl_query] * SIDE)
-    payload, *query = together(payload, *query)
-    arrived = gather_quad(payload)
+    payload, *query = together(jnp.tile(payload, (SIDE, 1)), *query)
+    arrived = exchange(payload, QUAD)
     query, out_t, lse = call(
         forward_body,
         [far(((TILE, COLS), BF16), HEADS), ((COLS, TILE), BF16), ((SIDE, TILE), F32)],
@@ -465,7 +457,7 @@
     )
     d_key_value, *d_query = call(
         backward_body,
-        [far(((TILE, 2 * COLS), BF16), 2 * HEADS)],
+        [far(((2 * TILE, COLS), BF16), HEADS)],
         quad_one,
         far(query, HEADS),
         far(key_value, 2 * HEADS),
@@ -506,7 +498,7 @@
     d_w_out, *d_query[4:] = together(d_w_out, *d_query[4:])
     d_query = sum(block.astype(F32) for block in scatter_quad(d_query))
     d_w_out = exchange(d_w_out, "z").reshape(SIDE, COLS // SIDE, COLS)
-    d_key, d_value = d_key_value[:, :COLS], d_key_value[:, COLS:]
+    d_key, d_value = d_key_value[:TOK], d_key_value[TOK:]
     d_w_out, d_key, d_value = together(d_w_out, d_key, d_value)
     d_w_out = jnp.sum(d_w_out.astype(F32), axis=0).T
     return (

time: 173 us -> 172 us (level)
  transfers between devices with their start and end apart: 27 -> 27, of which waited for: 12 -> 13; matrix products, arithmetic and copies ran while one was open for 3% -> 3% of each run, Pallas kernels for 18% -> 17%
where the time goes in v4:
time: 172 us; the launch traced here: 171 us
  starting transfers between devices  66.9 us (39%)
  waiting for transfers between devices  45.8 us (27%)
  Pallas kernels  36.2 us (21%)
  between operations  14.4 us (8%)
  local copies, waits for them, and re-layouts  4.14 us (2%)
  other arithmetic  3.88 us (2%)
    all_to_all x6, starting transfers between devices, exchange(): return lax.all_to_all(value, axis, split_axis=0, concat_axis=0, tiled=True)  36.1 us
    pallas_call x8, Pallas kernels, call(): pl.pallas_call(kernel, out_shape=[pltpu.HBM(*one) if out_parts[i] else ja...  34.3 us
    ppermute x19, starting transfers between devices, shift(): lax.ppermute(value, axis, [(i, (i + step) % size) for i in range(size)])  30.7 us
    all_to_all x6, waiting for transfers between devices, exchange(): return lax.all_to_all(value, axis, split_axis=0, concat_axis=0, tiled=True)  29.2 us
    ppermute x19, waiting for transfers between devices, shift(): lax.ppermute(value, axis, [(i, (i + step) % size) for i in range(size)])  15.8 us
  transfers between devices with their start and end apart: 27, of which 13 were waited for; matrix products, arithmetic and copies ran while one was open for 3% of the time, Pallas kernels for 17%

profile of v4, /device:TPU:32, one launch (start us, length us, event | category | flops | bytes accessed | tf_op | source)
XLA Modules:
  0.0 171.4 jit_solution(2515006659943485962)
XLA Ops:
  7.2 0.0 all-gather.2.cloned.1.call-start
  7.2 1.6 pad_maximum_fusion
  8.8 0.0 all-gather.2.cloned.1.call-update
  8.9 3.3 %collective-permute-start = (bf16[128,768]{1,0:T(8,128)(2,1)}, bf16[128,768]{1,0:T(8,128)(2,1)S(1)}, u32[]{:S(2)}, u32[]{:S(2)}) collective-permute-start(bf16[128,768]{1,0:T(8,128)(2,1)} %refs_2_.3), channel_id=1, source_target_pairs={{0,128},{128,0},{1,129},{129,1},{2,130},{130,2},{3,131},{131,3},{4... | collective-permute-start | bytes 589832 | tf_op jit(solution)/shard_map/ppermute | solution.py:374
  12.2 0.0 collective-permute-start.1
  12.2 5.2 %collective-permute-done.refs_3_ = bf16[128,768]{1,0:T(8,128)(2,1)S(1)} collective-permute-done((bf16[128,768]{1,0:T(8,128)(2,1)}, bf16[128,768]{1,0:T(8,128)(2,1)S(1)}, u32[]{:S(2)}, u32[]{:S(2)}) %collective-permute-start) | collective-permute-done | bytes 196640 | tf_op jit(solution)/shard_map/ppermute | solution.py:374
  17.3 0.0 collective-permute-start.2
  17.3 1.4 collective-permute-done.2.refs_5_
  18.8 0.7 copy-done.6
  19.4 3.5 %shard_map.110 = bf16[128,512]{1,0:T(8,128)(2,1)} custom-call(s32[1]{0:T(128)} %bitcast.1.refs_0_, s32[1]{0:T(128)} %bitcast.2.refs_1_, bf16[128,768]{1,0:T(8,128)(2,1)} %refs_2_.3, bf16[128,768]{1,0:T(8,128)(2,1)S(1)} %collective-permute-done.refs_3_, bf16[128,768]{1,0:T(8,128)(2,1)S(1)} %collective-permute-done.1.refs_4_, ...), custom_call_target="tpu_custom_call" | custom-call | tf_op jit(solution)/shard_map/pallas_call | solution.py:123
  23.0 8.6 %all-to-all-start = ((bf16[8,16,512]{2,1,0:T(8,128)(2,1)}), bf16[8,16,512]{2,1,0:T(8,128)(2,1)S(1)}, u32[]{:S(2)}, u32[]{:S(2)}) async-start(bf16[8,16,512]{2,1,0:T(8,128)(2,1)} %bitcast.40), calls=%async_computation | async-start | bytes 262144 | tf_op jit(solution)/shard_map/all_to_all | solution.py:378
  31.6 1.6 collective-permute-start.3
  33.2 1.5 collective-permute-start.4
  34.7 2.0 %collective-permute-start.5 = (bf16[128,384]{1,0:T(8,128)(2,1)S(1)}, bf16[128,384]{1,0:T(8,128)(2,1)S(1)}, u32[]{:S(2)}, u32[]{:S(2)}) collective-permute-start(bf16[128,384]{1,0:T(8,128)(2,1)S(1)} %copy-done.9), channel_id=1, source_target_pairs={{0,24},{8,32},{16,40},{24,48},{32,56},{40,0},{48,8},{56,16},{1,25}... | collective-permute-start | bytes 294920 | tf_op jit(solution)/shard_map/ppermute | solution.py:374
  36.7 2.0 %collective-permute-start.6 = (bf16[128,384]{1,0:T(8,128)(2,1)S(1)}, bf16[128,384]{1,0:T(8,128)(2,1)S(1)}, u32[]{:S(2)}, u32[]{:S(2)}) collective-permute-start(bf16[128,384]{1,0:T(8,128)(2,1)S(1)} %copy-done.9), channel_id=1, source_target_pairs={{0,32},{8,40},{16,48},{24,56},{32,0},{40,8},{48,16},{56,24},{1,33}... | collective-permute-start | bytes 294920 | tf_op jit(solution)/shard_map/ppermute | solution.py:374
  38.7 3.1 %collective-permute-start.7 = (bf16[128,384]{1,0:T(8,128)(2,1)S(1)}, bf16[128,384]{1,0:T(8,128)(2,1)S(1)}, u32[]{:S(2)}, u32[]{:S(2)}) collective-permute-start(bf16[128,384]{1,0:T(8,128)(2,1)S(1)} %copy-done.9), channel_id=1, source_target_pairs={{0,40},{8,48},{16,56},{24,0},{32,8},{40,16},{48,24},{56,32},{1,41}... | collective-permute-start | bytes 294920 | tf_op jit(solution)/shard_map/ppermute | solution.py:374
  41.8 1.4 collective-permute-start.8
  43.3 1.1 collective-permute-done.5.refs_5_
  44.3 0.3 collective-permute-done.6.refs_6_
  44.6 1.4 collective-permute-done.7.refs_7_
  46.1 1.0 collective-permute-done.8.refs_8_
  47.0 0.8 collective-permute-done.9.refs_9_
  47.9 1.1 tile.12
  49.0 5.1 %all-to-all-start.1 = ((bf16[8,128,512]{2,1,0:T(8,128)(2,1)}), bf16[8,128,512]{2,1,0:T(8,128)(2,1)S(1)}, u32[]{:S(2)}, u32[]{:S(2)}) async-start(bf16[8,128,512]{2,1,0:T(8,128)(2,1)} %bitcast.7), calls=%async_computation.1 | async-start | bytes 2097152 | tf_op jit(solution)/shard_map/all_to_all | solution.py:378
  54.1 0.8 all-gather.2.cloned.1.call-done.refs_1_.refs_2_
  54.9 6.9 %shard_map.111 = (bf16[1024,384]{1,0:T(8,128)(2,1)}, bf16[384,1024]{1,0:T(8,128)(2,1)S(1)}, f32[8,1024]{1,0:T(8,128)S(1)}) custom-call(s32[1]{0:T(128)} %bitcast.refs_0_, bf16[1024,768]{1,0:T(8,128)(2,1)} %all-gather.2.cloned.1.call-done.refs_1_.refs_2_, bf16[128,384]{1,0:T(8,128)(2,1)} %refs_2_.2, bf16[128,384]{1,0:T(8,128)(2,1)} %copy-done.10, ...), custom_call_target="tpu_custom_call" | custom-call | tf_op jit(solution)/shard_map/pallas_call | solution.py:123
  61.8 6.3 %all-to-all-done.1 = bf16[8,128,512]{2,1,0:T(8,128)(2,1)S(1)} async-done(((bf16[8,128,512]{2,1,0:T(8,128)(2,1)}), bf16[8,128,512]{2,1,0:T(8,128)(2,1)S(1)}, u32[]{:S(2)}, u32[]{:S(2)}) %all-to-all-start.1) | async-done | bytes 1048608 | tf_op jit(solution)/shard_map/all_to_all | solution.py:378
  68.1 4.8 %shard_map.112 = (bf16[1024,384]{1,0:T(8,128)(2,1)}, bf16[8,176,384]{2,1,0:T(8,128)(2,1)}) custom-call(bf16[1024,512]{1,0:T(8,128)(2,1)S(1)} %bitcast.29, bf16[384,1024]{1,0:T(8,128)(2,1)S(1)} %get-tuple-element.65.refs_1_, f32[8,1024]{1,0:T(8,128)S(1)} %get-tuple-element.66.refs_2_), custom_call_target="tpu_custom_call" | custom-call | tf_op jit(solution)/shard_map/pallas_call | solution.py:123
  72.9 3.6 %all-to-all-start.2 = ((bf16[8,176,384]{2,1,0:T(8,128)(2,1)}), bf16[8,176,384]{2,1,0:T(8,128)(2,1)S(1)}, u32[]{:S(2)}, u32[]{:S(2)}) async-start(bf16[8,176,384]{2,1,0:T(8,128)(2,1)} %get-tuple-element.68), calls=%async_computation.2 | async-start | bytes 2162688 | tf_op jit(solution)/shard_map/all_to_all | solution.py:378
  76.5 2.9 %shard_map.113._ = bf16[8,128,768]{2,1,0:T(8,128)(2,1)} custom-call(s32[1]{0:T(128)} %bitcast.1.refs_0_, s32[1]{0:T(128)} %bitcast.2.refs_1_, bf16[128,768]{1,0:T(8,128)(2,1)} %refs_2_.3, bf16[128,768]{1,0:T(8,128)(2,1)} %copy-done.3, bf16[128,768]{1,0:T(8,128)(2,1)} %copy-done.4, bf16[128,768]{1,0:T(8,128)(2,1)} %copy-done.5, s32[1,128]{1,0:T(1,128)S(1)} %bitcast.36), custom_call_target="tpu_custom_call" | custom-call | tf_op jit(solution)/shard_map/pallas_call | solution.py:123
  79.4 11.9 %all-to-all-done.2.refs_1_ = bf16[8,176,384]{2,1,0:T(8,128)(2,1)S(1)} async-done(((bf16[8,176,384]{2,1,0:T(8,128)(2,1)}), bf16[8,176,384]{2,1,0:T(8,128)(2,1)S(1)}, u32[]{:S(2)}, u32[]{:S(2)}) %all-to-all-start.2) | async-done | bytes 1081376 | tf_op jit(solution)/shard_map/all_to_all | solution.py:378
  91.3 1.7 shard_map.114
  93.0 7.2 %all-to-all-start.3 = ((bf16[8,16,384]{2,1,0:T(8,128)(2,1)}), bf16[8,16,384]{2,1,0:T(8,128)(2,1)S(1)}, u32[]{:S(2)}, u32[]{:S(2)}) async-start(bf16[8,16,384]{2,1,0:T(8,128)(2,1)} %bitcast.41), calls=%async_computation.3 | async-start | bytes 196608 | tf_op jit(solution)/shard_map/all_to_all | solution.py:378
  100.2 11.0 %shard_map.115 = (bf16[2048,384]{1,0:T(8,128)(2,1)}, bf16[128,384]{1,0:T(8,128)(2,1)}, bf16[128,384]{1,0:T(8,128)(2,1)}, bf16[128,384]{1,0:T(8,128)(2,1)}, bf16[...) custom-call(s32[1]{0:T(128)} %bitcast.refs_0_, ...), custom_call_target="tpu_custom_call" | custom-call | tf_op jit(solution)/shard_map/pallas_call | solution.py:123
  111.2 0.0 copy-start.1
  111.2 0.0 reduce-scatter.2.cloned.1.call-update
  111.2 0.6 copy-done.1
  111.9 1.9 %shard_map.116 = bf16[8,128,768]{2,1,0:T(8,128)(2,1)} custom-call(bf16[128,384]{1,0:T(8,128)(2,1)} %bitcast.33, bf16[8,128,768]{2,1,0:T(8,128)(2,1)} %shard_map.113._), custom_call_target="tpu_custom_call", output_to_operand_aliasing={{}: (1, {})} | custom-call | tf_op jit(solution)/shard_map/pallas_call | solution.py:363
  113.8 0.0 copy-start
  113.8 0.0 copy-start.2
  113.8 4.4 %all-to-all-start.4 = ((bf16[8,128,768]{2,1,0:T(8,128)(2,1)}), bf16[8,128,768]{2,1,0:T(8,128)(2,1)}, u32[]{:S(2)}, u32[]{:S(2)}) async-start(bf16[8,128,768]{2,1,0:T(8,128)(2,1)} %shard_map.116), calls=%async_computation.4 | async-start | bytes 3145728 | tf_op jit(solution)/shard_map/all_to_all | solution.py:378
  118.3 0.8 shard_map.117
  119.1 0.0 copy-start.23
  119.1 0.0 copy-start.22
  119.2 0.1 collective-permute-start.10
  119.3 1.7 collective-permute-done.10
  121.0 0.1 convert_add_fusion
  121.1 0.0 copy-start.8
  121.2 3.3 %collective-permute-start.11 = (bf16[128,768]{1,0:T(8,128)(2,1)S(1)}, bf16[128,768]{1,0:T(8,128)(2,1)S(1)}, u32[]{:S(2)}, u32[]{:S(2)}) collective-permute-start(bf16[128,768]{1,0:T(8,128)(2,1)S(1)} %fusion.2), channel_id=1, source_target_pairs={{0,128},{128,0},{1,129},{129,1},{2,130},{130,2},{3,131},{131,3},{4... | collective-permute-start | bytes 589832 | tf_op jit(solution)/shard_map/ppermute | solution.py:374
  124.5 2.2 %collective-permute-start.14 = (bf16[128,384]{1,0:T(8,128)(2,1)S(1)}, bf16[128,384]{1,0:T(8,128)(2,1)S(1)}, u32[]{:S(2)}, u32[]{:S(2)}) collective-permute-start(bf16[128,384]{1,0:T(8,128)(2,1)S(1)} %copy-done.24), channel_id=1, source_target_pairs={{0,24},{8,32},{16,40},{24,48},{32,56},{40,0},{48,8},{56,16},{1,25}... | collective-permute-start | bytes 294920 | tf_op jit(solution)/shard_map/ppermute | solution.py:374
  126.6 1.5 collective-permute-start.13
  128.1 1.8 %collective-permute-start.12 = (bf16[128,384]{1,0:T(8,128)(2,1)S(1)}, bf16[128,384]{1,0:T(8,128)(2,1)S(1)}, u32[]{:S(2)}, u32[]{:S(2)}) collective-permute-start(bf16[128,384]{1,0:T(8,128)(2,1)S(1)} %copy-done.22), channel_id=1, source_target_pairs={{0,8},{8,16},{16,24},{24,32},{32,40},{40,48},{48,56},{56,0},{1,9},... | collective-permute-start | bytes 294920 | tf_op jit(solution)/shard_map/ppermute | solution.py:374
  129.9 10.9 %all-to-all-done.4.refs_0_ = bf16[8,128,768]{2,1,0:T(8,128)(2,1)} async-done(((bf16[8,128,768]{2,1,0:T(8,128)(2,1)}), bf16[8,128,768]{2,1,0:T(8,128)(2,1)}, u32[]{:S(2)}, u32[]{:S(2)}) %all-to-all-start.4) | async-done | bytes 1572896 | tf_op jit(solution)/shard_map/all_to_all | solution.py:378
  140.8 2.7 %shard_map.118 = bf16[384,384]{1,0:T(8,128)(2,1)} custom-call(bf16[8,128,768]{2,1,0:T(8,128)(2,1)} %all-to-all-done.4.refs_0_), custom_call_target="tpu_custom_call" | custom-call | tf_op jit(solution)/shard_map/pallas_call | solution.py:123
  143.6 0.7 collective-permute-start.18
  144.3 7.3 %all-to-all-start.5 = ((bf16[8,48,384]{2,1,0:T(8,128)(2,1)}), bf16[8,48,384]{2,1,0:T(8,128)(2,1)S(1)}, u32[]{:S(2)}, u32[]{:S(2)}) async-start(bf16[8,48,384]{2,1,0:T(8,128)(2,1)} %bitcast.38), calls=%async_computation.5 | async-start | bytes 589824 | tf_op jit(solution)/shard_map/all_to_all | solution.py:378
  151.6 1.3 collective-permute-start.17
  152.9 2.0 %collective-permute-start.16 = (bf16[128,384]{1,0:T(8,128)(2,1)S(1)}, bf16[128,384]{1,0:T(8,128)(2,1)S(1)}, u32[]{:S(2)}, u32[]{:S(2)}) collective-permute-start(bf16[128,384]{1,0:T(8,128)(2,1)S(1)} %copy-done.19), channel_id=1, source_target_pairs={{0,40},{8,48},{16,56},{24,0},{32,8},{40,16},{48,24},{56,32},{1,41}... | collective-permute-start | bytes 294920 | tf_op jit(solution)/shard_map/ppermute | solution.py:374
  154.9 2.9 %collective-permute-start.15 = (bf16[128,384]{1,0:T(8,128)(2,1)S(1)}, bf16[128,384]{1,0:T(8,128)(2,1)S(1)}, u32[]{:S(2)}, u32[]{:S(2)}) collective-permute-start(bf16[128,384]{1,0:T(8,128)(2,1)S(1)} %copy-done.18), channel_id=1, source_target_pairs={{0,32},{8,40},{16,48},{24,56},{32,0},{40,8},{48,16},{56,24},{1,33}... | collective-permute-start | bytes 294920 | tf_op jit(solution)/shard_map/ppermute | solution.py:374
  157.8 0.7 fusion.1
  158.6 2.9 %collective-permute-done.15 = bf16[128,384]{1,0:T(8,128)(2,1)S(1)} collective-permute-done((bf16[128,384]{1,0:T(8,128)(2,1)S(1)}, bf16[128,384]{1,0:T(8,128)(2,1)S(1)}, u32[]{:S(2)}, u32[]{:S(2)}) %collective-permute-start.15) | collective-permute-done | bytes 98336 | tf_op jit(solution)/shard_map/ppermute | solution.py:374
  161.5 0.7 add_convert_fusion
  162.2 1.6 fusion.3
  163.9 0.7 convert_reduce_fusion
  (60 shorter events, 0.2 us)
Async XLA Ops:
  7.2 47.7 %all-gather.2.cloned.1.call-start = ((), (), s32[]{:S(2)}) async-start(), calls=%async_computation.7 | async-start | bytes 1769472 | tf_op jit(solution)/shard_map/all_gather | solution.py:400
  8.9 8.4 %collective-permute-start = (bf16[128,768]{1,0:T(8,128)(2,1)}, bf16[128,768]{1,0:T(8,128)(2,1)S(1)}, u32[]{:S(2)}, u32[]{:S(2)}) collective-permute-start(bf16[128,768]{1,0:T(8,128)(2,1)} %refs_2_.3), channel_id=1, source_target_pairs={{0,128},{128,0},{1,129},{129,1},{2,130},{130,2},{3,131},{131,3},{4... | collective-permute-start | bytes 589832 | tf_op jit(solution)/shard_map/ppermute | solution.py:374
  12.2 5.2 %collective-permute-start.1 = (bf16[128,768]{1,0:T(8,128)(2,1)}, bf16[128,768]{1,0:T(8,128)(2,1)S(1)}, u32[]{:S(2)}, u32[]{:S(2)}) collective-permute-start(bf16[128,768]{1,0:T(8,128)(2,1)} %refs_2_.3), channel_id=1, source_target_pairs={{0,64},{64,0},{1,65},{65,1},{2,66},{66,2},{3,67},{67,3},{4,68},{68... | collective-permute-start | bytes 589832 | tf_op jit(solution)/shard_map/ppermute | solution.py:374
  17.3 5.7 %copy-start.3 = (bf16[128,768]{1,0:T(8,128)(2,1)}, bf16[128,768]{1,0:T(8,128)(2,1)S(1)}, u32[]{:S(2)}) copy-start(bf16[128,768]{1,0:T(8,128)(2,1)S(1)} %collective-permute-done.refs_3_) | copy-start | bytes 589828
  17.3 1.4 collective-permute-start.2
  17.3 5.7 %copy-start.4 = (bf16[128,768]{1,0:T(8,128)(2,1)}, bf16[128,768]{1,0:T(8,128)(2,1)S(1)}, u32[]{:S(2)}) copy-start(bf16[128,768]{1,0:T(8,128)(2,1)S(1)} %collective-permute-done.1.refs_4_) | copy-start | bytes 589828
  18.8 4.2 %copy-start.5 = (bf16[128,768]{1,0:T(8,128)(2,1)}, bf16[128,768]{1,0:T(8,128)(2,1)S(1)}, u32[]{:S(2)}) copy-start(bf16[128,768]{1,0:T(8,128)(2,1)S(1)} %collective-permute-done.2.refs_5_) | copy-start | bytes 589828
  18.8 0.7 copy-start.6
  19.4 12.2 %copy-start.9 = (bf16[128,384]{1,0:T(8,128)(2,1)S(1)}, bf16[128,384]{1,0:T(8,128)(2,1)}, u32[]{:S(2)}) copy-start(bf16[128,384]{1,0:T(8,128)(2,1)} %refs_2_.2) | copy-start | bytes 294916
  23.0 24.9 %all-to-all-start = ((bf16[8,16,512]{2,1,0:T(8,128)(2,1)}), bf16[8,16,512]{2,1,0:T(8,128)(2,1)S(1)}, u32[]{:S(2)}, u32[]{:S(2)}) async-start(bf16[8,16,512]{2,1,0:T(8,128)(2,1)} %bitcast.40), calls=%async_computation | async-start | bytes 262144 | tf_op jit(solution)/shard_map/all_to_all | solution.py:378
  31.6 10.2 %collective-permute-start.3 = (bf16[128,384]{1,0:T(8,128)(2,1)S(1)}, bf16[128,384]{1,0:T(8,128)(2,1)S(1)}, u32[]{:S(2)}, u32[]{:S(2)}) collective-permute-start(bf16[128,384]{1,0:T(8,128)(2,1)S(1)} %copy-done.9), channel_id=1, source_target_pairs={{0,8},{8,16},{16,24},{24,32},{32,40},{40,48},{48,56},{56,0},{1,9},... | collective-permute-start | bytes 294920 | tf_op jit(solution)/shard_map/ppermute | solution.py:374
  33.2 10.1 %collective-permute-start.4 = (bf16[128,384]{1,0:T(8,128)(2,1)S(1)}, bf16[128,384]{1,0:T(8,128)(2,1)S(1)}, u32[]{:S(2)}, u32[]{:S(2)}) collective-permute-start(bf16[128,384]{1,0:T(8,128)(2,1)S(1)} %copy-done.9), channel_id=1, source_target_pairs={{0,16},{8,24},{16,32},{24,40},{32,48},{40,56},{48,0},{56,8},{1,17}... | collective-permute-start | bytes 294920 | tf_op jit(solution)/shard_map/ppermute | solution.py:374
  34.7 9.7 %collective-permute-start.5 = (bf16[128,384]{1,0:T(8,128)(2,1)S(1)}, bf16[128,384]{1,0:T(8,128)(2,1)S(1)}, u32[]{:S(2)}, u32[]{:S(2)}) collective-permute-start(bf16[128,384]{1,0:T(8,128)(2,1)S(1)} %copy-done.9), channel_id=1, source_target_pairs={{0,24},{8,32},{16,40},{24,48},{32,56},{40,0},{48,8},{56,16},{1,25}... | collective-permute-start | bytes 294920 | tf_op jit(solution)/shard_map/ppermute | solution.py:374
  36.7 8.0 %collective-permute-start.6 = (bf16[128,384]{1,0:T(8,128)(2,1)S(1)}, bf16[128,384]{1,0:T(8,128)(2,1)S(1)}, u32[]{:S(2)}, u32[]{:S(2)}) collective-permute-start(bf16[128,384]{1,0:T(8,128)(2,1)S(1)} %copy-done.9), channel_id=1, source_target_pairs={{0,32},{8,40},{16,48},{24,56},{32,0},{40,8},{48,16},{56,24},{1,33}... | collective-permute-start | bytes 294920 | tf_op jit(solution)/shard_map/ppermute | solution.py:374
  38.7 7.4 %collective-permute-start.7 = (bf16[128,384]{1,0:T(8,128)(2,1)S(1)}, bf16[128,384]{1,0:T(8,128)(2,1)S(1)}, u32[]{:S(2)}, u32[]{:S(2)}) collective-permute-start(bf16[128,384]{1,0:T(8,128)(2,1)S(1)} %copy-done.9), channel_id=1, source_target_pairs={{0,40},{8,48},{16,56},{24,0},{32,8},{40,16},{48,24},{56,32},{1,41}... | collective-permute-start | bytes 294920 | tf_op jit(solution)/shard_map/ppermute | solution.py:374
  41.8 7.1 %copy-start.10 = (bf16[128,384]{1,0:T(8,128)(2,1)}, bf16[128,384]{1,0:T(8,128)(2,1)S(1)}, u32[]{:S(2)}) copy-start(bf16[128,384]{1,0:T(8,128)(2,1)S(1)} %collective-permute-done.3.refs_3_) | copy-start | bytes 294916
  41.8 5.2 %collective-permute-start.8 = (bf16[128,384]{1,0:T(8,128)(2,1)S(1)}, bf16[128,384]{1,0:T(8,128)(2,1)S(1)}, u32[]{:S(2)}, u32[]{:S(2)}) collective-permute-start(bf16[128,384]{1,0:T(8,128)(2,1)S(1)} %copy-done.9), channel_id=1, source_target_pairs={{0,48},{8,56},{16,0},{24,8},{32,16},{40,24},{48,32},{56,40},{1,49}... | collective-permute-start | bytes 294920 | tf_op jit(solution)/shard_map/ppermute | solution.py:374
  43.3 5.7 %copy-start.11 = (bf16[128,384]{1,0:T(8,128)(2,1)}, bf16[128,384]{1,0:T(8,128)(2,1)S(1)}, u32[]{:S(2)}) copy-start(bf16[128,384]{1,0:T(8,128)(2,1)S(1)} %collective-permute-done.4.refs_4_) | copy-start | bytes 294916
  43.3 4.6 %collective-permute-start.9 = (bf16[128,384]{1,0:T(8,128)(2,1)S(1)}, bf16[128,384]{1,0:T(8,128)(2,1)S(1)}, u32[]{:S(2)}, u32[]{:S(2)}) collective-permute-start(bf16[128,384]{1,0:T(8,128)(2,1)S(1)} %copy-done.9), channel_id=1, source_target_pairs={{0,56},{8,0},{16,8},{24,16},{32,24},{40,32},{48,40},{56,48},{1,57}... | collective-permute-start | bytes 294920 | tf_op jit(solution)/shard_map/ppermute | solution.py:374
  44.3 4.6 %copy-start.12 = (bf16[128,384]{1,0:T(8,128)(2,1)}, bf16[128,384]{1,0:T(8,128)(2,1)S(1)}, u32[]{:S(2)}) copy-start(bf16[128,384]{1,0:T(8,128)(2,1)S(1)} %collective-permute-done.5.refs_5_) | copy-start | bytes 294916
  44.6 4.3 %copy-start.13 = (bf16[128,384]{1,0:T(8,128)(2,1)}, bf16[128,384]{1,0:T(8,128)(2,1)S(1)}, u32[]{:S(2)}) copy-start(bf16[128,384]{1,0:T(8,128)(2,1)S(1)} %collective-permute-done.6.refs_6_) | copy-start | bytes 294916
  46.1 2.9 %copy-start.14 = (bf16[128,384]{1,0:T(8,128)(2,1)}, bf16[128,384]{1,0:T(8,128)(2,1)S(1)}, u32[]{:S(2)}) copy-start(bf16[128,384]{1,0:T(8,128)(2,1)S(1)} %collective-permute-done.7.refs_7_) | copy-start | bytes 294916
  47.0 1.9 %copy-start.15 = (bf16[128,384]{1,0:T(8,128)(2,1)}, bf16[128,384]{1,0:T(8,128)(2,1)S(1)}, u32[]{:S(2)}) copy-start(bf16[128,384]{1,0:T(8,128)(2,1)S(1)} %collective-permute-done.8.refs_8_) | copy-start | bytes 294916
  47.9 1.1 copy-start.16
  49.0 19.1 %all-to-all-start.1 = ((bf16[8,128,512]{2,1,0:T(8,128)(2,1)}), bf16[8,128,512]{2,1,0:T(8,128)(2,1)S(1)}, u32[]{:S(2)}, u32[]{:S(2)}) async-start(bf16[8,128,512]{2,1,0:T(8,128)(2,1)} %bitcast.7), calls=%async_computation.1 | async-start | bytes 2097152 | tf_op jit(solution)/shard_map/all_to_all | solution.py:378
  68.1 8.4 %copy-start.7 = (s32[128]{0:T(128)S(1)}, s32[128]{0:T(128)}, u32[]{:S(2)}) copy-start(s32[128]{0:T(128)} %param.13) | copy-start | bytes 1540
  72.9 18.4 %all-to-all-start.2 = ((bf16[8,176,384]{2,1,0:T(8,128)(2,1)}), bf16[8,176,384]{2,1,0:T(8,128)(2,1)S(1)}, u32[]{:S(2)}, u32[]{:S(2)}) async-start(bf16[8,176,384]{2,1,0:T(8,128)(2,1)} %get-tuple-element.68), calls=%async_computation.2 | async-start | bytes 2162688 | tf_op jit(solution)/shard_map/all_to_all | solution.py:378
  93.0 18.2 %all-to-all-start.3 = ((bf16[8,16,384]{2,1,0:T(8,128)(2,1)}), bf16[8,16,384]{2,1,0:T(8,128)(2,1)S(1)}, u32[]{:S(2)}, u32[]{:S(2)}) async-start(bf16[8,16,384]{2,1,0:T(8,128)(2,1)} %bitcast.41), calls=%async_computation.3 | async-start | bytes 196608 | tf_op jit(solution)/shard_map/all_to_all | solution.py:378
  100.2 62.0 %reduce-scatter.2.cloned.1.call-start = ((), (), s32[]{:S(2)}) async-start(), calls=%async_computation.8 | async-start | bytes 1769472 | tf_op jit(solution)/shard_map/reduce_scatter | solution.py:471
  111.2 0.6 copy-start.1
  113.8 4.5 %copy-start = (bf16[384,3072]{1,0:T(8,128)(2,1)S(1)}, bf16[384,3072]{1,0:T(8,128)(2,1)}, u32[]{:S(2)}) copy-start(bf16[384,3072]{1,0:T(8,128)(2,1)} %refs_1_.1) | copy-start | bytes 7077892
  113.8 4.5 %copy-start.2 = (bf16[8,16,384]{2,1,0:T(8,128)(2,1)S(1)}, bf16[8,16,384]{2,1,0:T(8,128)(2,1)}, u32[]{:S(2)}) copy-start(bf16[8,16,384]{2,1,0:T(8,128)(2,1)} %copy-done.1) | copy-start | bytes 294916
  113.8 27.0 %all-to-all-start.4 = ((bf16[8,128,768]{2,1,0:T(8,128)(2,1)}), bf16[8,128,768]{2,1,0:T(8,128)(2,1)}, u32[]{:S(2)}, u32[]{:S(2)}) async-start(bf16[8,128,768]{2,1,0:T(8,128)(2,1)} %shard_map.116), calls=%async_computation.4 | async-start | bytes 3145728 | tf_op jit(solution)/shard_map/all_to_all | solution.py:378
  119.1 5.3 %copy-start.24 = (bf16[128,384]{1,0:T(8,128)(2,1)S(1)}, bf16[128,384]{1,0:T(8,128)(2,1)}, u32[]{:S(2)}) copy-start(bf16[128,384]{1,0:T(8,128)(2,1)} %get-tuple-element.86) | copy-start | bytes 294916
  119.1 7.5 %copy-start.23 = (bf16[128,384]{1,0:T(8,128)(2,1)S(1)}, bf16[128,384]{1,0:T(8,128)(2,1)}, u32[]{:S(2)}) copy-start(bf16[128,384]{1,0:T(8,128)(2,1)} %get-tuple-element.85) | copy-start | bytes 294916
  119.1 9.0 %copy-start.22 = (bf16[128,384]{1,0:T(8,128)(2,1)S(1)}, bf16[128,384]{1,0:T(8,128)(2,1)}, u32[]{:S(2)}) copy-start(bf16[128,384]{1,0:T(8,128)(2,1)} %get-tuple-element.84) | copy-start | bytes 294916
  119.2 1.8 %collective-permute-start.10 = (bf16[2,128,768]{2,1,0:T(8,128)(2,1)S(1)}, bf16[2,128,768]{2,1,0:T(8,128)(2,1)S(1)}, u32[]{:S(2)}, u32[]{:S(2)}) collective-permute-start(bf16[2,128,768]{2,1,0:T(8,128)(2,1)S(1)} %dynamic-slice_bitcast_fusion), channel_id=1, source_target_pairs={{0,64},{64,0},{1,65},{65,1},{2,66},{66,2},{3,67},{67,3},{4,68},{68... | collective-permute-start | bytes 1179656 | tf_op jit(solution)/shard_map/ppermute | solution.py:374
  119.3 24.3 %copy-start.21 = (bf16[128,384]{1,0:T(8,128)(2,1)S(1)}, bf16[128,384]{1,0:T(8,128)(2,1)}, u32[]{:S(2)}) copy-start(bf16[128,384]{1,0:T(8,128)(2,1)} %get-tuple-element.95) | copy-start | bytes 294916
  121.1 30.5 %copy-start.20 = (bf16[128,384]{1,0:T(8,128)(2,1)S(1)}, bf16[128,384]{1,0:T(8,128)(2,1)}, u32[]{:S(2)}) copy-start(bf16[128,384]{1,0:T(8,128)(2,1)} %get-tuple-element.94) | copy-start | bytes 294916
  121.1 31.7 %copy-start.19 = (bf16[128,384]{1,0:T(8,128)(2,1)S(1)}, bf16[128,384]{1,0:T(8,128)(2,1)}, u32[]{:S(2)}) copy-start(bf16[128,384]{1,0:T(8,128)(2,1)} %get-tuple-element.93) | copy-start | bytes 294916
  121.1 33.8 %copy-start.18 = (bf16[128,384]{1,0:T(8,128)(2,1)S(1)}, bf16[128,384]{1,0:T(8,128)(2,1)}, u32[]{:S(2)}) copy-start(bf16[128,384]{1,0:T(8,128)(2,1)} %get-tuple-element.92) | copy-start | bytes 294916
  121.1 36.7 %copy-start.8 = (bf16[128,768]{1,0:T(8,128)(2,1)S(1)}, bf16[128,768]{1,0:T(8,128)(2,1)}, u32[]{:S(2)}) copy-start(bf16[128,768]{1,0:T(8,128)(2,1)} %param.7) | copy-start | bytes 589828
  121.2 33.7 %collective-permute-start.11 = (bf16[128,768]{1,0:T(8,128)(2,1)S(1)}, bf16[128,768]{1,0:T(8,128)(2,1)S(1)}, u32[]{:S(2)}, u32[]{:S(2)}) collective-permute-start(bf16[128,768]{1,0:T(8,128)(2,1)S(1)} %fusion.2), channel_id=1, source_target_pairs={{0,128},{128,0},{1,129},{129,1},{2,130},{130,2},{3,131},{131,3},{4... | collective-permute-start | bytes 589832 | tf_op jit(solution)/shard_map/ppermute | solution.py:374
  124.5 27.1 %collective-permute-start.14 = (bf16[128,384]{1,0:T(8,128)(2,1)S(1)}, bf16[128,384]{1,0:T(8,128)(2,1)S(1)}, u32[]{:S(2)}, u32[]{:S(2)}) collective-permute-start(bf16[128,384]{1,0:T(8,128)(2,1)S(1)} %copy-done.24), channel_id=1, source_target_pairs={{0,24},{8,32},{16,40},{24,48},{32,56},{40,0},{48,8},{56,16},{1,25}... | collective-permute-start | bytes 294920 | tf_op jit(solution)/shard_map/ppermute | solution.py:374
  126.6 26.2 %collective-permute-start.13 = (bf16[128,384]{1,0:T(8,128)(2,1)S(1)}, bf16[128,384]{1,0:T(8,128)(2,1)S(1)}, u32[]{:S(2)}, u32[]{:S(2)}) collective-permute-start(bf16[128,384]{1,0:T(8,128)(2,1)S(1)} %copy-done.23), channel_id=1, source_target_pairs={{0,16},{8,24},{16,32},{24,40},{32,48},{40,56},{48,0},{56,8},{1,17}... | collective-permute-start | bytes 294920 | tf_op jit(solution)/shard_map/ppermute | solution.py:374
  128.1 33.3 %copy-start.17 = (bf16[128,384]{1,0:T(8,128)(2,1)S(1)}, bf16[128,384]{1,0:T(8,128)(2,1)}, u32[]{:S(2)}) copy-start(bf16[128,384]{1,0:T(8,128)(2,1)} %get-tuple-element.83) | copy-start | bytes 294916
  128.1 30.5 %collective-permute-start.12 = (bf16[128,384]{1,0:T(8,128)(2,1)S(1)}, bf16[128,384]{1,0:T(8,128)(2,1)S(1)}, u32[]{:S(2)}, u32[]{:S(2)}) collective-permute-start(bf16[128,384]{1,0:T(8,128)(2,1)S(1)} %copy-done.22), channel_id=1, source_target_pairs={{0,8},{8,16},{16,24},{24,32},{32,40},{40,48},{48,56},{56,0},{1,9},... | collective-permute-start | bytes 294920 | tf_op jit(solution)/shard_map/ppermute | solution.py:374
  143.6 15.0 %collective-permute-start.18 = (bf16[128,384]{1,0:T(8,128)(2,1)S(1)}, bf16[128,384]{1,0:T(8,128)(2,1)S(1)}, u32[]{:S(2)}, u32[]{:S(2)}) collective-permute-start(bf16[128,384]{1,0:T(8,128)(2,1)S(1)} %copy-done.21), channel_id=1, source_target_pairs={{0,56},{8,0},{16,8},{24,16},{32,24},{40,32},{48,40},{56,48},{1,57}... | collective-permute-start | bytes 294920 | tf_op jit(solution)/shard_map/ppermute | solution.py:374
  144.3 19.5 %all-to-all-start.5 = ((bf16[8,48,384]{2,1,0:T(8,128)(2,1)}), bf16[8,48,384]{2,1,0:T(8,128)(2,1)S(1)}, u32[]{:S(2)}, u32[]{:S(2)}) async-start(bf16[8,48,384]{2,1,0:T(8,128)(2,1)} %bitcast.38), calls=%async_computation.5 | async-start | bytes 589824 | tf_op jit(solution)/shard_map/all_to_all | solution.py:378
  151.6 7.0 %collective-permute-start.17 = (bf16[128,384]{1,0:T(8,128)(2,1)S(1)}, bf16[128,384]{1,0:T(8,128)(2,1)S(1)}, u32[]{:S(2)}, u32[]{:S(2)}) collective-permute-start(bf16[128,384]{1,0:T(8,128)(2,1)S(1)} %copy-done.20), channel_id=1, source_target_pairs={{0,48},{8,56},{16,0},{24,8},{32,16},{40,24},{48,32},{56,40},{1,49}... | collective-permute-start | bytes 294920 | tf_op jit(solution)/shard_map/ppermute | solution.py:374
  152.9 5.7 %collective-permute-start.16 = (bf16[128,384]{1,0:T(8,128)(2,1)S(1)}, bf16[128,384]{1,0:T(8,128)(2,1)S(1)}, u32[]{:S(2)}, u32[]{:S(2)}) collective-permute-start(bf16[128,384]{1,0:T(8,128)(2,1)S(1)} %copy-done.19), channel_id=1, source_target_pairs={{0,40},{8,48},{16,56},{24,0},{32,8},{40,16},{48,24},{56,32},{1,41}... | collective-permute-start | bytes 294920 | tf_op jit(solution)/shard_map/ppermute | solution.py:374
  154.9 6.6 %collective-permute-start.15 = (bf16[128,384]{1,0:T(8,128)(2,1)S(1)}, bf16[128,384]{1,0:T(8,128)(2,1)S(1)}, u32[]{:S(2)}, u32[]{:S(2)}) collective-permute-start(bf16[128,384]{1,0:T(8,128)(2,1)S(1)} %copy-done.18), channel_id=1, source_target_pairs={{0,32},{8,40},{16,48},{24,56},{32,0},{40,8},{48,16},{56,24},{1,33}... | collective-permute-start | bytes 294920 | tf_op jit(solution)/shard_map/ppermute | solution.py:374
Sparse Core Ops, SparseCore 0:
  10.4 44.5 all-gather.1
  111.4 38.8 reduce-scatter.1

commit v5 on v4

--- a/solution.py
+++ b/solution.py
@@ -151,8 +151,8 @@
     return lax.rem(pos + (step + SIDE), SIDE)
 
 
-def rows_of(pos):
-    return pl.ds(pl.multiple_of(pos * TOK, TOK), TOK)
+def rows_of(pos, rows=TOK):
+    return pl.ds(pl.multiple_of(pos * rows, rows), rows)
 
 
 def head(idx):
@@ -216,10 +216,10 @@
         cut_ref[2 * part + 1, :, COLS:] = rows[:, COLS:]
 
 
-def forward_body(ready, done, quad_ref, kv_ref, *rest):
+def forward_body(ready, done, x_ref, kv_ref, *rest):
     blocks, (q_ref, out_ref, lse_ref) = rest[:-3], rest[-3:]
     for step, block_ref in enumerate(blocks):
-        q_ref[rows_of(around(quad_ref[0], -step)), :] = block_ref[...]
+        q_ref[rows_of(lax.rem(x_ref[0] + (4 - step), 4), 2 * TOK), :] = block_ref[...]
     for idx in range(HEADS):
         done(0, idx)
     lse_ref[...] = jnp.zeros_like(lse_ref)
@@ -392,6 +392,7 @@
 
 def on_device(main_hidden, ctrl_query, ctrl_key, ctrl_value, w_out, d_mixed, control_slot):
     y_pos, core = lax.axis_index("yh"), lax.axis_index("co")
+    x_one = lax.axis_index("x").reshape(1).astype(jnp.int32)
     quad = lax.axis_index("x") * 2 + lax.axis_index("yl")
     slot_row = control_slot.reshape(1, TOK)
     y_one, core_one, quad_one = (p.reshape(1).astype(jnp.int32) for p in (y_pos, core, quad))
@@ -399,7 +400,13 @@
     key_value = jnp.concatenate([ctrl_key, ctrl_value], axis=1)
     key_value = lax.all_gather(key_value, "z", axis=0, tiled=True)
     along = shift(d_mixed, "yh", 1, 2)
-    across = shift(d_mixed, "co", 1, 2)
+    near = shift(ctrl_query, "yl", 1, 2)
+    d_later, near = together(d_mixed, near)
+    across = shift(d_later, "co", 1, 2)
+    y_low = lax.axis_index("yl")
+    near = jnp.where(
+        y_low == 0, jnp.stack([ctrl_query, near]), jnp.stack([near, ctrl_query])
+    ).reshape(2 * TOK, COLS)
     both = shift(along, "co", 1, 2)
     (payload,) = call(
         project_body,
@@ -414,15 +421,15 @@
         slot_row,
         mib=16,
     )
-    payload, ctrl_query = together(payload, ctrl_query)
+    payload, near = together(payload, near)
     payload = exchange(payload, "z")
-    query = scatter_quad([ctrl_query] * SIDE)
+    query = [near] + [shift(near, "x", step, 4) for step in range(1, 4)]
     payload, *query = together(jnp.tile(payload, (SIDE, 1)), *query)
     arrived = exchange(payload, QUAD)
     query, out_t, lse = call(
         forward_body,
         [far(((TILE, COLS), BF16), HEADS), ((COLS, TILE), BF16), ((SIDE, TILE), F32)],
-        quad_one,
+        x_one,
         far(key_value, 2 * HEADS),
         *[far(block) for block in query],
         mib=40,

time: 172 us -> 172 us (level)
  starting transfers between devices: 66.9 us -> 59.9 us
  waiting for transfers between devices: 45.8 us -> 51.4 us
    ppermute x19 -> x16, starting transfers between devices: 30.7 us -> 24.1 us  [shift(): lax.ppermute(value, axis, [(i, (i + step) % size) for i in range(size)])]
    ppermute x19 -> x16, waiting for transfers between devices: 15.8 us -> 18.9 us  [shift(): lax.ppermute(value, axis, [(i, (i + step) % size) for i in range(size)])]
    all_to_all x6, waiting for transfers between devices: 29.2 us -> 31.8 us  [exchange(): return lax.all_to_all(value, axis, split_axis=0, concat_axis=0, tiled=True)]
  transfers between devices with their start and end apart: 27 -> 24, of which waited for: 13 -> 11; matrix products, arithmetic and copies ran while one was open for 3% -> 3% of each run, Pallas kernels for 17% -> 17%
where the time goes in v5:
time: 172 us; the launch traced here: 171 us
  starting transfers between devices  59.9 us (35%)
  waiting for transfers between devices  51.4 us (30%)
  Pallas kernels  36.2 us (21%)
  between operations  14.4 us (8%)
  other arithmetic  4.89 us (3%)
  local copies, waits for them, and re-layouts  4.2 us (2%)
    all_to_all x6, starting transfers between devices, exchange(): return lax.all_to_all(value, axis, split_axis=0, concat_axis=0, tiled=True)  35.8 us
    pallas_call x8, Pallas kernels, call(): pl.pallas_call(kernel, out_shape=[pltpu.HBM(*one) if out_parts[i] else ja...  34.2 us
    all_to_all x6, waiting for transfers between devices, exchange(): return lax.all_to_all(value, axis, split_axis=0, concat_axis=0, tiled=True)  31.8 us
    ppermute x16, starting transfers between devices, shift(): lax.ppermute(value, axis, [(i, (i + step) % size) for i in range(size)])  24.1 us
    ppermute x16, waiting for transfers between devices, shift(): lax.ppermute(value, axis, [(i, (i + step) % size) for i in range(size)])  18.9 us
  transfers between devices with their start and end apart: 24, of which 11 were waited for; matrix products, arithmetic and copies ran while one was open for 3% of the time, Pallas kernels for 17%

profile of v5, /device:TPU:32, one launch (start us, length us, event | category | flops | bytes accessed | tf_op | source)
XLA Modules:
  0.0 171.0 jit_solution(5353655302071101686)
XLA Ops:
  7.2 0.0 all-gather.2.cloned.1.call-start
  7.2 1.6 pad_maximum_fusion
  8.8 0.0 all-gather.2.cloned.1.call-update
  8.9 3.3 %collective-permute-start = (bf16[128,768]{1,0:T(8,128)(2,1)}, bf16[128,768]{1,0:T(8,128)(2,1)S(1)}, u32[]{:S(2)}, u32[]{:S(2)}) collective-permute-start(bf16[128,768]{1,0:T(8,128)(2,1)} %refs_2_.2), channel_id=1, source_target_pairs={{0,128},{128,0},{1,129},{129,1},{2,130},{130,2},{3,131},{131,3},{4... | collective-permute-start | bytes 589832 | tf_op jit(solution)/shard_map/ppermute | solution.py:374
  12.2 0.7 collective-permute-start.1
  12.8 6.9 %collective-permute-done.1 = bf16[128,384]{1,0:T(8,128)(2,1)S(1)} collective-permute-done((bf16[128,384]{1,0:T(8,128)(2,1)}, bf16[128,384]{1,0:T(8,128)(2,1)S(1)}, u32[]{:S(2)}, u32[]{:S(2)}) %collective-permute-start.1) | collective-permute-done | bytes 98336 | tf_op jit(solution)/shard_map/ppermute | solution.py:374
  19.8 0.0 collective-permute-start.2
  19.8 0.0 collective-permute-done.refs_3_
  19.8 0.5 collective-permute-start.3
  20.3 1.0 maximum_select_fusion
  21.3 0.1 collective-permute-done.2.refs_4_
  21.4 0.1 collective-permute-done.3.refs_5_
  21.5 0.7 copy-done.6
  22.2 3.5 %shard_map.110 = bf16[128,512]{1,0:T(8,128)(2,1)} custom-call(s32[1]{0:T(128)} %bitcast.2.refs_0_, s32[1]{0:T(128)} %bitcast.3.refs_1_, bf16[128,768]{1,0:T(8,128)(2,1)} %refs_2_.2, bf16[128,768]{1,0:T(8,128)(2,1)S(1)} %collective-permute-done.refs_3_, bf16[128,768]{1,0:T(8,128)(2,1)S(1)} %collective-permute-done.2.refs_4_, ...), custom_call_target="tpu_custom_call" | custom-call | tf_op jit(solution)/shard_map/pallas_call | solution.py:123
  25.8 8.6 %all-to-all-start = ((bf16[8,16,512]{2,1,0:T(8,128)(2,1)}), bf16[8,16,512]{2,1,0:T(8,128)(2,1)S(1)}, u32[]{:S(2)}, u32[]{:S(2)}) async-start(bf16[8,16,512]{2,1,0:T(8,128)(2,1)} %bitcast.48), calls=%async_computation | async-start | bytes 262144 | tf_op jit(solution)/shard_map/all_to_all | solution.py:378
  34.4 1.5 collective-permute-start.4
  35.9 2.7 %collective-permute-start.5 = (bf16[256,384]{1,0:T(8,128)(2,1)S(1)}, bf16[256,384]{1,0:T(8,128)(2,1)S(1)}, u32[]{:S(2)}, u32[]{:S(2)}) collective-permute-start(bf16[256,384]{1,0:T(8,128)(2,1)S(1)} %bitcast.44), channel_id=1, source_target_pairs={{0,32},{16,48},{32,0},{48,16},{1,33},{17,49},{33,1},{49,17},{2,34}... | collective-permute-start | bytes 589832 | tf_op jit(solution)/shard_map/ppermute | solution.py:374
  38.6 1.4 collective-permute-start.6
  40.1 2.4 %collective-permute-done.4.refs_3_ = bf16[256,384]{1,0:T(8,128)(2,1)S(1)} collective-permute-done((bf16[256,384]{1,0:T(8,128)(2,1)S(1)}, bf16[256,384]{1,0:T(8,128)(2,1)S(1)}, u32[]{:S(2)}, u32[]{:S(2)}) %collective-permute-start.4) | collective-permute-done | bytes 196640 | tf_op jit(solution)/shard_map/ppermute | solution.py:374
  42.5 4.8 %collective-permute-done.5.refs_4_ = bf16[256,384]{1,0:T(8,128)(2,1)S(1)} collective-permute-done((bf16[256,384]{1,0:T(8,128)(2,1)S(1)}, bf16[256,384]{1,0:T(8,128)(2,1)S(1)}, u32[]{:S(2)}, u32[]{:S(2)}) %collective-permute-start.5) | collective-permute-done | bytes 196640 | tf_op jit(solution)/shard_map/ppermute | solution.py:374
  47.2 0.0 collective-permute-done.6.refs_5_
  47.3 0.0 all-to-all-done
  47.3 1.1 tile.12
  48.4 4.7 %all-to-all-start.1 = ((bf16[8,128,512]{2,1,0:T(8,128)(2,1)}), bf16[8,128,512]{2,1,0:T(8,128)(2,1)S(1)}, u32[]{:S(2)}, u32[]{:S(2)}) async-start(bf16[8,128,512]{2,1,0:T(8,128)(2,1)} %bitcast.11), calls=%async_computation.1 | async-start | bytes 2097152 | tf_op jit(solution)/shard_map/all_to_all | solution.py:378
  53.1 0.7 all-gather.2.cloned.1.call-done.refs_1_.refs_2_
  53.8 6.9 %shard_map.111 = (bf16[1024,384]{1,0:T(8,128)(2,1)}, bf16[384,1024]{1,0:T(8,128)(2,1)S(1)}, f32[8,1024]{1,0:T(8,128)S(1)}) custom-call(s32[1]{0:T(128)} %bitcast.1.refs_0_, bf16[1024,768]{1,0:T(8,128)(2,1)} %all-gather.2.cloned.1.call-done.refs_1_.refs_2_, bf16[256,384]{1,0:T(8,128)(2,1)} %bitcast.46, bf16[256,384]{1,0:T(8,128)(2,1)} %copy-done.10, ...), custom_call_target="tpu_custom_call" | custom-call | tf_op jit(solution)/shard_map/pallas_call | solution.py:123
  60.6 7.2 %all-to-all-done.1 = bf16[8,128,512]{2,1,0:T(8,128)(2,1)S(1)} async-done(((bf16[8,128,512]{2,1,0:T(8,128)(2,1)}), bf16[8,128,512]{2,1,0:T(8,128)(2,1)S(1)}, u32[]{:S(2)}, u32[]{:S(2)}) %all-to-all-start.1) | async-done | bytes 1048608 | tf_op jit(solution)/shard_map/all_to_all | solution.py:378
  67.8 4.8 %shard_map.112 = (bf16[1024,384]{1,0:T(8,128)(2,1)}, bf16[8,176,384]{2,1,0:T(8,128)(2,1)}) custom-call(bf16[1024,512]{1,0:T(8,128)(2,1)S(1)} %bitcast.33, bf16[384,1024]{1,0:T(8,128)(2,1)S(1)} %get-tuple-element.61.refs_1_, f32[8,1024]{1,0:T(8,128)S(1)} %get-tuple-element.62.refs_2_), custom_call_target="tpu_custom_call" | custom-call | tf_op jit(solution)/shard_map/pallas_call | solution.py:123
  72.6 3.6 %all-to-all-start.2 = ((bf16[8,176,384]{2,1,0:T(8,128)(2,1)}), bf16[8,176,384]{2,1,0:T(8,128)(2,1)S(1)}, u32[]{:S(2)}, u32[]{:S(2)}) async-start(bf16[8,176,384]{2,1,0:T(8,128)(2,1)} %get-tuple-element.64), calls=%async_computation.2 | async-start | bytes 2162688 | tf_op jit(solution)/shard_map/all_to_all | solution.py:378
  76.2 2.9 %shard_map.113._ = bf16[8,128,768]{2,1,0:T(8,128)(2,1)} custom-call(s32[1]{0:T(128)} %bitcast.2.refs_0_, s32[1]{0:T(128)} %bitcast.3.refs_1_, bf16[128,768]{1,0:T(8,128)(2,1)} %refs_2_.2, bf16[128,768]{1,0:T(8,128)(2,1)} %copy-done.3, bf16[128,768]{1,0:T(8,128)(2,1)} %copy-done.4, bf16[128,768]{1,0:T(8,128)(2,1)} %copy-done.5, s32[1,128]{1,0:T(1,128)S(1)} %bitcast.40), custom_call_target="tpu_custom_call" | custom-call | tf_op jit(solution)/shard_map/pallas_call | solution.py:123
  79.1 12.0 %all-to-all-done.2.refs_1_ = bf16[8,176,384]{2,1,0:T(8,128)(2,1)S(1)} async-done(((bf16[8,176,384]{2,1,0:T(8,128)(2,1)}), bf16[8,176,384]{2,1,0:T(8,128)(2,1)S(1)}, u32[]{:S(2)}, u32[]{:S(2)}) %all-to-all-start.2) | async-done | bytes 1081376 | tf_op jit(solution)/shard_map/all_to_all | solution.py:378
  91.1 1.7 shard_map.114
  92.7 7.2 %all-to-all-start.3 = ((bf16[8,16,384]{2,1,0:T(8,128)(2,1)}), bf16[8,16,384]{2,1,0:T(8,128)(2,1)S(1)}, u32[]{:S(2)}, u32[]{:S(2)}) async-start(bf16[8,16,384]{2,1,0:T(8,128)(2,1)} %bitcast.49), calls=%async_computation.3 | async-start | bytes 196608 | tf_op jit(solution)/shard_map/all_to_all | solution.py:378
  100.0 11.0 %shard_map.115 = (bf16[2048,384]{1,0:T(8,128)(2,1)}, bf16[128,384]{1,0:T(8,128)(2,1)}, bf16[128,384]{1,0:T(8,128)(2,1)}, bf16[128,384]{1,0:T(8,128)(2,1)}, bf16[...) custom-call(s32[1]{0:T(128)} %bitcast.refs_0_, ...), custom_call_target="tpu_custom_call" | custom-call | tf_op jit(solution)/shard_map/pallas_call | solution.py:123
  110.9 0.0 copy-start.1
  111.0 0.0 reduce-scatter.2.cloned.1.call-update
  111.0 0.6 copy-done.1
  111.6 1.9 %shard_map.116 = bf16[8,128,768]{2,1,0:T(8,128)(2,1)} custom-call(bf16[128,384]{1,0:T(8,128)(2,1)} %bitcast.37, bf16[8,128,768]{2,1,0:T(8,128)(2,1)} %shard_map.113._), custom_call_target="tpu_custom_call", output_to_operand_aliasing={{}: (1, {})} | custom-call | tf_op jit(solution)/shard_map/pallas_call | solution.py:363
  113.5 0.0 copy-start
  113.5 0.0 copy-start.2
  113.5 4.4 %all-to-all-start.4 = ((bf16[8,128,768]{2,1,0:T(8,128)(2,1)}), bf16[8,128,768]{2,1,0:T(8,128)(2,1)}, u32[]{:S(2)}, u32[]{:S(2)}) async-start(bf16[8,128,768]{2,1,0:T(8,128)(2,1)} %shard_map.116), calls=%async_computation.4 | async-start | bytes 3145728 | tf_op jit(solution)/shard_map/all_to_all | solution.py:378
  118.0 0.8 shard_map.117
  118.8 0.0 copy-start.19
  118.9 0.0 copy-start.18
  118.9 0.1 collective-permute-start.7
  119.0 1.7 collective-permute-done.7
  120.7 0.1 convert_add_fusion
  120.8 0.0 copy-start.9
  120.9 1.5 collective-permute-start.8
  122.4 2.2 %collective-permute-start.11 = (bf16[128,384]{1,0:T(8,128)(2,1)S(1)}, bf16[128,384]{1,0:T(8,128)(2,1)S(1)}, u32[]{:S(2)}, u32[]{:S(2)}) collective-permute-start(bf16[128,384]{1,0:T(8,128)(2,1)S(1)} %copy-done.20), channel_id=1, source_target_pairs={{0,24},{8,32},{16,40},{24,48},{32,56},{40,0},{48,8},{56,16},{1,25}... | collective-permute-start | bytes 294920 | tf_op jit(solution)/shard_map/ppermute | solution.py:374
  124.6 1.5 collective-permute-start.10
  126.1 1.8 %collective-permute-start.9 = (bf16[128,384]{1,0:T(8,128)(2,1)S(1)}, bf16[128,384]{1,0:T(8,128)(2,1)S(1)}, u32[]{:S(2)}, u32[]{:S(2)}) collective-permute-start(bf16[128,384]{1,0:T(8,128)(2,1)S(1)} %copy-done.18), channel_id=1, source_target_pairs={{0,8},{8,16},{16,24},{24,32},{32,40},{40,48},{48,56},{56,0},{1,9},... | collective-permute-start | bytes 294920 | tf_op jit(solution)/shard_map/ppermute | solution.py:374
  127.9 12.7 %all-to-all-done.4.refs_0_ = bf16[8,128,768]{2,1,0:T(8,128)(2,1)} async-done(((bf16[8,128,768]{2,1,0:T(8,128)(2,1)}), bf16[8,128,768]{2,1,0:T(8,128)(2,1)}, u32[]{:S(2)}, u32[]{:S(2)}) %all-to-all-start.4) | async-done | bytes 1572896 | tf_op jit(solution)/shard_map/all_to_all | solution.py:378
  140.6 2.7 %shard_map.118 = bf16[384,384]{1,0:T(8,128)(2,1)} custom-call(bf16[8,128,768]{2,1,0:T(8,128)(2,1)} %all-to-all-done.4.refs_0_), custom_call_target="tpu_custom_call" | custom-call | tf_op jit(solution)/shard_map/pallas_call | solution.py:123
  143.3 0.7 collective-permute-start.15
  144.0 7.2 %all-to-all-start.5 = ((bf16[8,48,384]{2,1,0:T(8,128)(2,1)}), bf16[8,48,384]{2,1,0:T(8,128)(2,1)S(1)}, u32[]{:S(2)}, u32[]{:S(2)}) async-start(bf16[8,48,384]{2,1,0:T(8,128)(2,1)} %bitcast.42), calls=%async_computation.5 | async-start | bytes 589824 | tf_op jit(solution)/shard_map/all_to_all | solution.py:378
  151.2 1.2 collective-permute-start.14
  152.5 2.1 %collective-permute-start.13 = (bf16[128,384]{1,0:T(8,128)(2,1)S(1)}, bf16[128,384]{1,0:T(8,128)(2,1)S(1)}, u32[]{:S(2)}, u32[]{:S(2)}) collective-permute-start(bf16[128,384]{1,0:T(8,128)(2,1)S(1)} %copy-done.15), channel_id=1, source_target_pairs={{0,40},{8,48},{16,56},{24,0},{32,8},{40,16},{48,24},{56,32},{1,41}... | collective-permute-start | bytes 294920 | tf_op jit(solution)/shard_map/ppermute | solution.py:374
  154.6 2.9 %collective-permute-start.12 = (bf16[128,384]{1,0:T(8,128)(2,1)S(1)}, bf16[128,384]{1,0:T(8,128)(2,1)S(1)}, u32[]{:S(2)}, u32[]{:S(2)}) collective-permute-start(bf16[128,384]{1,0:T(8,128)(2,1)S(1)} %copy-done.14), channel_id=1, source_target_pairs={{0,32},{8,40},{16,48},{24,56},{32,0},{40,8},{48,16},{56,24},{1,33}... | collective-permute-start | bytes 294920 | tf_op jit(solution)/shard_map/ppermute | solution.py:374
  157.5 0.7 fusion.1
  158.2 2.9 %collective-permute-done.12 = bf16[128,384]{1,0:T(8,128)(2,1)S(1)} collective-permute-done((bf16[128,384]{1,0:T(8,128)(2,1)S(1)}, bf16[128,384]{1,0:T(8,128)(2,1)S(1)}, u32[]{:S(2)}, u32[]{:S(2)}) %collective-permute-start.12) | collective-permute-done | bytes 98336 | tf_op jit(solution)/shard_map/ppermute | solution.py:374
  161.1 0.7 add_convert_fusion
  161.9 1.6 fusion.3
  163.5 0.7 convert_reduce_fusion
  (47 shorter events, 0.2 us)
Async XLA Ops:
  7.2 46.6 %all-gather.2.cloned.1.call-start = ((), (), s32[]{:S(2)}) async-start(), calls=%async_computation.7 | async-start | bytes 1769472 | tf_op jit(solution)/shard_map/all_gather | solution.py:401
  8.9 10.9 %collective-permute-start = (bf16[128,768]{1,0:T(8,128)(2,1)}, bf16[128,768]{1,0:T(8,128)(2,1)S(1)}, u32[]{:S(2)}, u32[]{:S(2)}) collective-permute-start(bf16[128,768]{1,0:T(8,128)(2,1)} %refs_2_.2), channel_id=1, source_target_pairs={{0,128},{128,0},{1,129},{129,1},{2,130},{130,2},{3,131},{131,3},{4... | collective-permute-start | bytes 589832 | tf_op jit(solution)/shard_map/ppermute | solution.py:374
  12.2 7.6 %collective-permute-start.1 = (bf16[128,384]{1,0:T(8,128)(2,1)}, bf16[128,384]{1,0:T(8,128)(2,1)S(1)}, u32[]{:S(2)}, u32[]{:S(2)}) collective-permute-start(bf16[128,384]{1,0:T(8,128)(2,1)} %param.8), channel_id=1, source_target_pairs={{0,8},{8,0},{1,9},{9,1},{2,10},{10,2},{3,11},{11,3},{4,12},{12,4},... | collective-permute-start | bytes 294920 | tf_op jit(solution)/shard_map/ppermute | solution.py:374
  19.8 1.7 collective-permute-start.2
  19.8 6.0 %copy-start.3 = (bf16[128,768]{1,0:T(8,128)(2,1)}, bf16[128,768]{1,0:T(8,128)(2,1)S(1)}, u32[]{:S(2)}) copy-start(bf16[128,768]{1,0:T(8,128)(2,1)S(1)} %collective-permute-done.refs_3_) | copy-start | bytes 589828
  19.8 1.7 %collective-permute-start.3 = (bf16[128,768]{1,0:T(8,128)(2,1)S(1)}, bf16[128,768]{1,0:T(8,128)(2,1)S(1)}, u32[]{:S(2)}, u32[]{:S(2)}) collective-permute-start(bf16[128,768]{1,0:T(8,128)(2,1)S(1)} %collective-permute-done.refs_3_), channel_id=1, source_target_pairs={{0,64},{64,0},{1,65},{65,1},{2,66},{66,2},{3,67},{67,3},{4,68},{68... | collective-permute-start | bytes 589832 | tf_op jit(solution)/shard_map/ppermute | solution.py:374
  21.3 17.4 %copy-start.8 = (bf16[2,128,384]{2,1,0:T(8,128)(2,1)}, bf16[2,128,384]{2,1,0:T(8,128)(2,1)S(1)}, u32[]{:S(2)}) copy-start(bf16[2,128,384]{2,1,0:T(8,128)(2,1)S(1)} %maximum_select_fusion) | copy-start | bytes 589828
  21.4 4.3 %copy-start.4 = (bf16[128,768]{1,0:T(8,128)(2,1)}, bf16[128,768]{1,0:T(8,128)(2,1)S(1)}, u32[]{:S(2)}) copy-start(bf16[128,768]{1,0:T(8,128)(2,1)S(1)} %collective-permute-done.2.refs_4_) | copy-start | bytes 589828
  21.5 4.3 %copy-start.5 = (bf16[128,768]{1,0:T(8,128)(2,1)}, bf16[128,768]{1,0:T(8,128)(2,1)S(1)}, u32[]{:S(2)}) copy-start(bf16[128,768]{1,0:T(8,128)(2,1)S(1)} %collective-permute-done.3.refs_5_) | copy-start | bytes 589828
  21.5 0.7 copy-start.6
  25.8 21.5 %all-to-all-start = ((bf16[8,16,512]{2,1,0:T(8,128)(2,1)}), bf16[8,16,512]{2,1,0:T(8,128)(2,1)S(1)}, u32[]{:S(2)}, u32[]{:S(2)}) async-start(bf16[8,16,512]{2,1,0:T(8,128)(2,1)} %bitcast.48), calls=%async_computation | async-start | bytes 262144 | tf_op jit(solution)/shard_map/all_to_all | solution.py:378
  34.4 8.0 %collective-permute-start.4 = (bf16[256,384]{1,0:T(8,128)(2,1)S(1)}, bf16[256,384]{1,0:T(8,128)(2,1)S(1)}, u32[]{:S(2)}, u32[]{:S(2)}) collective-permute-start(bf16[256,384]{1,0:T(8,128)(2,1)S(1)} %bitcast.43), channel_id=1, source_target_pairs={{0,16},{16,32},{32,48},{48,0},{1,17},{17,33},{33,49},{49,1},{2,18}... | collective-permute-start | bytes 589832 | tf_op jit(solution)/shard_map/ppermute | solution.py:374
  35.9 11.3 %collective-permute-start.5 = (bf16[256,384]{1,0:T(8,128)(2,1)S(1)}, bf16[256,384]{1,0:T(8,128)(2,1)S(1)}, u32[]{:S(2)}, u32[]{:S(2)}) collective-permute-start(bf16[256,384]{1,0:T(8,128)(2,1)S(1)} %bitcast.44), channel_id=1, source_target_pairs={{0,32},{16,48},{32,0},{48,16},{1,33},{17,49},{33,1},{49,17},{2,34}... | collective-permute-start | bytes 589832 | tf_op jit(solution)/shard_map/ppermute | solution.py:374
  38.6 8.6 %collective-permute-start.6 = (bf16[256,384]{1,0:T(8,128)(2,1)S(1)}, bf16[256,384]{1,0:T(8,128)(2,1)S(1)}, u32[]{:S(2)}, u32[]{:S(2)}) collective-permute-start(bf16[256,384]{1,0:T(8,128)(2,1)S(1)} %bitcast.45), channel_id=1, source_target_pairs={{0,48},{16,0},{32,16},{48,32},{1,49},{17,1},{33,17},{49,33},{2,50}... | collective-permute-start | bytes 589832 | tf_op jit(solution)/shard_map/ppermute | solution.py:374
  42.5 5.9 %copy-start.10 = (bf16[256,384]{1,0:T(8,128)(2,1)}, bf16[256,384]{1,0:T(8,128)(2,1)S(1)}, u32[]{:S(2)}) copy-start(bf16[256,384]{1,0:T(8,128)(2,1)S(1)} %collective-permute-done.4.refs_3_) | copy-start | bytes 589828
  47.2 1.1 copy-start.11
  47.2 1.1 copy-start.12
  48.4 19.5 %all-to-all-start.1 = ((bf16[8,128,512]{2,1,0:T(8,128)(2,1)}), bf16[8,128,512]{2,1,0:T(8,128)(2,1)S(1)}, u32[]{:S(2)}, u32[]{:S(2)}) async-start(bf16[8,128,512]{2,1,0:T(8,128)(2,1)} %bitcast.11), calls=%async_computation.1 | async-start | bytes 2097152 | tf_op jit(solution)/shard_map/all_to_all | solution.py:378
  67.8 8.4 %copy-start.7 = (s32[128]{0:T(128)S(1)}, s32[128]{0:T(128)}, u32[]{:S(2)}) copy-start(s32[128]{0:T(128)} %param.13) | copy-start | bytes 1540
  72.6 18.4 %all-to-all-start.2 = ((bf16[8,176,384]{2,1,0:T(8,128)(2,1)}), bf16[8,176,384]{2,1,0:T(8,128)(2,1)S(1)}, u32[]{:S(2)}, u32[]{:S(2)}) async-start(bf16[8,176,384]{2,1,0:T(8,128)(2,1)} %get-tuple-element.64), calls=%async_computation.2 | async-start | bytes 2162688 | tf_op jit(solution)/shard_map/all_to_all | solution.py:378
  92.7 18.2 %all-to-all-start.3 = ((bf16[8,16,384]{2,1,0:T(8,128)(2,1)}), bf16[8,16,384]{2,1,0:T(8,128)(2,1)S(1)}, u32[]{:S(2)}, u32[]{:S(2)}) async-start(bf16[8,16,384]{2,1,0:T(8,128)(2,1)} %bitcast.49), calls=%async_computation.3 | async-start | bytes 196608 | tf_op jit(solution)/shard_map/all_to_all | solution.py:378
  99.9 61.9 %reduce-scatter.2.cloned.1.call-start = ((), (), s32[]{:S(2)}) async-start(), calls=%async_computation.8 | async-start | bytes 1769472 | tf_op jit(solution)/shard_map/reduce_scatter | solution.py:478
  110.9 0.6 copy-start.1
  113.5 4.5 %copy-start = (bf16[384,3072]{1,0:T(8,128)(2,1)S(1)}, bf16[384,3072]{1,0:T(8,128)(2,1)}, u32[]{:S(2)}) copy-start(bf16[384,3072]{1,0:T(8,128)(2,1)} %refs_1_.1) | copy-start | bytes 7077892
  113.5 4.5 %copy-start.2 = (bf16[8,16,384]{2,1,0:T(8,128)(2,1)S(1)}, bf16[8,16,384]{2,1,0:T(8,128)(2,1)}, u32[]{:S(2)}) copy-start(bf16[8,16,384]{2,1,0:T(8,128)(2,1)} %copy-done.1) | copy-start | bytes 294916
  113.5 27.0 %all-to-all-start.4 = ((bf16[8,128,768]{2,1,0:T(8,128)(2,1)}), bf16[8,128,768]{2,1,0:T(8,128)(2,1)}, u32[]{:S(2)}, u32[]{:S(2)}) async-start(bf16[8,128,768]{2,1,0:T(8,128)(2,1)} %shard_map.116), calls=%async_computation.4 | async-start | bytes 3145728 | tf_op jit(solution)/shard_map/all_to_all | solution.py:378
  118.8 3.6 %copy-start.20 = (bf16[128,384]{1,0:T(8,128)(2,1)S(1)}, bf16[128,384]{1,0:T(8,128)(2,1)}, u32[]{:S(2)}) copy-start(bf16[128,384]{1,0:T(8,128)(2,1)} %get-tuple-element.82) | copy-start | bytes 294916
  118.8 5.8 %copy-start.19 = (bf16[128,384]{1,0:T(8,128)(2,1)S(1)}, bf16[128,384]{1,0:T(8,128)(2,1)}, u32[]{:S(2)}) copy-start(bf16[128,384]{1,0:T(8,128)(2,1)} %get-tuple-element.81) | copy-start | bytes 294916
  118.9 7.3 %copy-start.18 = (bf16[128,384]{1,0:T(8,128)(2,1)S(1)}, bf16[128,384]{1,0:T(8,128)(2,1)}, u32[]{:S(2)}) copy-start(bf16[128,384]{1,0:T(8,128)(2,1)} %get-tuple-element.80) | copy-start | bytes 294916
  118.9 1.8 %collective-permute-start.7 = (bf16[2,128,768]{2,1,0:T(8,128)(2,1)S(1)}, bf16[2,128,768]{2,1,0:T(8,128)(2,1)S(1)}, u32[]{:S(2)}, u32[]{:S(2)}) collective-permute-start(bf16[2,128,768]{2,1,0:T(8,128)(2,1)S(1)} %dynamic-slice_bitcast_fusion), channel_id=1, source_target_pairs={{0,64},{64,0},{1,65},{65,1},{2,66},{66,2},{3,67},{67,3},{4,68},{68... | collective-permute-start | bytes 1179656 | tf_op jit(solution)/shard_map/ppermute | solution.py:374
  119.0 24.3 %copy-start.17 = (bf16[128,384]{1,0:T(8,128)(2,1)S(1)}, bf16[128,384]{1,0:T(8,128)(2,1)}, u32[]{:S(2)}) copy-start(bf16[128,384]{1,0:T(8,128)(2,1)} %get-tuple-element.91) | copy-start | bytes 294916
  120.8 30.4 %copy-start.16 = (bf16[128,384]{1,0:T(8,128)(2,1)S(1)}, bf16[128,384]{1,0:T(8,128)(2,1)}, u32[]{:S(2)}) copy-start(bf16[128,384]{1,0:T(8,128)(2,1)} %get-tuple-element.90) | copy-start | bytes 294916
  120.8 31.7 %copy-start.15 = (bf16[128,384]{1,0:T(8,128)(2,1)S(1)}, bf16[128,384]{1,0:T(8,128)(2,1)}, u32[]{:S(2)}) copy-start(bf16[128,384]{1,0:T(8,128)(2,1)} %get-tuple-element.89) | copy-start | bytes 294916
  120.8 33.7 %copy-start.14 = (bf16[128,384]{1,0:T(8,128)(2,1)S(1)}, bf16[128,384]{1,0:T(8,128)(2,1)}, u32[]{:S(2)}) copy-start(bf16[128,384]{1,0:T(8,128)(2,1)} %get-tuple-element.88) | copy-start | bytes 294916
  120.8 36.6 %copy-start.9 = (bf16[128,768]{1,0:T(8,128)(2,1)S(1)}, bf16[128,768]{1,0:T(8,128)(2,1)}, u32[]{:S(2)}) copy-start(bf16[128,768]{1,0:T(8,128)(2,1)} %param.7) | copy-start | bytes 589828
  120.9 33.7 %collective-permute-start.8 = (bf16[128,768]{1,0:T(8,128)(2,1)S(1)}, bf16[128,768]{1,0:T(8,128)(2,1)S(1)}, u32[]{:S(2)}, u32[]{:S(2)}) collective-permute-start(bf16[128,768]{1,0:T(8,128)(2,1)S(1)} %fusion.2), channel_id=1, source_target_pairs={{0,128},{128,0},{1,129},{129,1},{2,130},{130,2},{3,131},{131,3},{4... | collective-permute-start | bytes 589832 | tf_op jit(solution)/shard_map/ppermute | solution.py:374
  122.4 28.8 %collective-permute-start.11 = (bf16[128,384]{1,0:T(8,128)(2,1)S(1)}, bf16[128,384]{1,0:T(8,128)(2,1)S(1)}, u32[]{:S(2)}, u32[]{:S(2)}) collective-permute-start(bf16[128,384]{1,0:T(8,128)(2,1)S(1)} %copy-done.20), channel_id=1, source_target_pairs={{0,24},{8,32},{16,40},{24,48},{32,56},{40,0},{48,8},{56,16},{1,25}... | collective-permute-start | bytes 294920 | tf_op jit(solution)/shard_map/ppermute | solution.py:374
  124.6 27.8 %collective-permute-start.10 = (bf16[128,384]{1,0:T(8,128)(2,1)S(1)}, bf16[128,384]{1,0:T(8,128)(2,1)S(1)}, u32[]{:S(2)}, u32[]{:S(2)}) collective-permute-start(bf16[128,384]{1,0:T(8,128)(2,1)S(1)} %copy-done.19), channel_id=1, source_target_pairs={{0,16},{8,24},{16,32},{24,40},{32,48},{40,56},{48,0},{56,8},{1,17}... | collective-permute-start | bytes 294920 | tf_op jit(solution)/shard_map/ppermute | solution.py:374
  126.1 35.0 %copy-start.13 = (bf16[128,384]{1,0:T(8,128)(2,1)S(1)}, bf16[128,384]{1,0:T(8,128)(2,1)}, u32[]{:S(2)}) copy-start(bf16[128,384]{1,0:T(8,128)(2,1)} %get-tuple-element.79) | copy-start | bytes 294916
  126.1 32.1 %collective-permute-start.9 = (bf16[128,384]{1,0:T(8,128)(2,1)S(1)}, bf16[128,384]{1,0:T(8,128)(2,1)S(1)}, u32[]{:S(2)}, u32[]{:S(2)}) collective-permute-start(bf16[128,384]{1,0:T(8,128)(2,1)S(1)} %copy-done.18), channel_id=1, source_target_pairs={{0,8},{8,16},{16,24},{24,32},{32,40},{40,48},{48,56},{56,0},{1,9},... | collective-permute-start | bytes 294920 | tf_op jit(solution)/shard_map/ppermute | solution.py:374
  143.3 14.9 %collective-permute-start.15 = (bf16[128,384]{1,0:T(8,128)(2,1)S(1)}, bf16[128,384]{1,0:T(8,128)(2,1)S(1)}, u32[]{:S(2)}, u32[]{:S(2)}) collective-permute-start(bf16[128,384]{1,0:T(8,128)(2,1)S(1)} %copy-done.17), channel_id=1, source_target_pairs={{0,56},{8,0},{16,8},{24,16},{32,24},{40,32},{48,40},{56,48},{1,57}... | collective-permute-start | bytes 294920 | tf_op jit(solution)/shard_map/ppermute | solution.py:374
  144.0 19.5 %all-to-all-start.5 = ((bf16[8,48,384]{2,1,0:T(8,128)(2,1)}), bf16[8,48,384]{2,1,0:T(8,128)(2,1)S(1)}, u32[]{:S(2)}, u32[]{:S(2)}) async-start(bf16[8,48,384]{2,1,0:T(8,128)(2,1)} %bitcast.42), calls=%async_computation.5 | async-start | bytes 589824 | tf_op jit(solution)/shard_map/all_to_all | solution.py:378
  151.2 7.0 %collective-permute-start.14 = (bf16[128,384]{1,0:T(8,128)(2,1)S(1)}, bf16[128,384]{1,0:T(8,128)(2,1)S(1)}, u32[]{:S(2)}, u32[]{:S(2)}) collective-permute-start(bf16[128,384]{1,0:T(8,128)(2,1)S(1)} %copy-done.16), channel_id=1, source_target_pairs={{0,48},{8,56},{16,0},{24,8},{32,16},{40,24},{48,32},{56,40},{1,49}... | collective-permute-start | bytes 294920 | tf_op jit(solution)/shard_map/ppermute | solution.py:374
  152.5 5.7 %collective-permute-start.13 = (bf16[128,384]{1,0:T(8,128)(2,1)S(1)}, bf16[128,384]{1,0:T(8,128)(2,1)S(1)}, u32[]{:S(2)}, u32[]{:S(2)}) collective-permute-start(bf16[128,384]{1,0:T(8,128)(2,1)S(1)} %copy-done.15), channel_id=1, source_target_pairs={{0,40},{8,48},{16,56},{24,0},{32,8},{40,16},{48,24},{56,32},{1,41}... | collective-permute-start | bytes 294920 | tf_op jit(solution)/shard_map/ppermute | solution.py:374
  154.6 6.5 %collective-permute-start.12 = (bf16[128,384]{1,0:T(8,128)(2,1)S(1)}, bf16[128,384]{1,0:T(8,128)(2,1)S(1)}, u32[]{:S(2)}, u32[]{:S(2)}) collective-permute-start(bf16[128,384]{1,0:T(8,128)(2,1)S(1)} %copy-done.14), channel_id=1, source_target_pairs={{0,32},{8,40},{16,48},{24,56},{32,0},{40,8},{48,16},{56,24},{1,33}... | collective-permute-start | bytes 294920 | tf_op jit(solution)/shard_map/ppermute | solution.py:374
Sparse Core Ops, SparseCore 0:
  10.4 43.3 all-gather.1
  111.1 37.1 reduce-scatter.1
